TPU v7x, 32 devices: a whole 2x2x4 slice. The times are simulated.
32 devices in a mesh: grp: 8 (over y, x, core), ep: 4 (over z).
Axes of the slice: x: 2, y: 2, z: 4, core: 2. Of those that a mesh axis runs over, the one named last changes fastest.
Arguments:
- layer_input: bfloat16 [8192, 2048], P(('grp', 'ep')), may hold values from -6 to 6
- kv_weight: float32 [4096, 2048], P(None, 'grp'), may hold values from -0.125 to 0.125
- norm_gains: float32 [2, 2048], P(None, 'grp'), may hold values from 0.5 to 1.5
- query_maps: float32 [4, 2048, 2048], P('ep', 'grp'), may hold values from -0.125 to 0.125
- output_maps: float32 [4, 2048, 2048], P('ep', 'grp'), may hold values from -1 to 1
- gate_up_maps: float32 [4, 2048, 11264], P('ep', 'grp'), may hold values from -0.125 to 0.125
- down_maps: float32 [4, 5632, 2048], P('ep', 'grp'), may hold values from -0.15625 to 0.15625
- att_routes: int32 [8, 1024, 2], P('grp'), may hold values from 0 to 3, all different within a row; in each aligned block of 256 rows (0 to 255, 256 to 511, ..., all dimensions but the last counted through in order) at most 192 rows name the same one
- att_gates: float32 [8192, 2], P(('grp', 'ep')), may hold values from 0.25 to 0.75
- mlp_routes: int32 [8, 1024, 2], P('grp'), may hold values from 0 to 3, all different within a row; in each aligned block of 256 rows (0 to 255, 256 to 511, ..., all dimensions but the last counted through in order) at most 192 rows name the same one
- mlp_gates: float32 [8192, 2], P(('grp', 'ep')), may hold values from 0.25 to 0.75
- segments: int32 [8, 1024], P('grp'), may hold values from 0 to 1023, as said below
- cotangent: bfloat16 [8192, 2048], P(('grp', 'ep')), may hold values from -6 to 6
Outputs:
- output: bfloat16 [8192, 2048], P(('grp', 'ep'))
- d_input: float32 [8192, 2048], P(('grp', 'ep'))
- d_kv_weight: float32 [4096, 2048], P(None, 'grp')
- d_norm_gains: float32 [2, 2048], P(None, 'grp')
- d_query_maps: float32 [4, 2048, 2048], P('ep', 'grp')
- d_output_maps: float32 [4, 2048, 2048], P('ep', 'grp')
- d_gate_up_maps: float32 [4, 2048, 11264], P('ep', 'grp')
- d_down_maps: float32 [4, 5632, 2048], P('ep', 'grp')
Inputs may be any that keep to these rules, and one draw needn't show every extreme that they name: `att_routes`: each token names 2 different experts; among the tokens of one device no expert is named more than 192 times. `mlp_routes`: each token names 2 different experts; among the tokens of one device no expert is named more than 192 times. `segments`: a token's document number is the position of its document's first token in the sequence, so numbers never fall along a sequence; in every sequence one document runs from the first device's tokens into the last device's tokens.
All inputs are finite; a program needn't handle non-finite values.
Results may differ from a plain program's by a relative error of at most 0.019.
Values may be sent and summed in bfloat16 or wider, within the bound.
A program may use at most 384 MiB of HBM per device.

v0:
```python
import jax
import jax.numpy as jnp
from jax import lax
from jax.sharding import PartitionSpec as P

HEADS = 16
HEAD_DIM = 128
TOP = 2


EPSILON = 1e-06
NEGATIVE = -1e30
CONTRACT_ROWS = (((0,), (0,)), ((), ()))
CONTRACT_COLUMNS = (((1,), (1,)), ((), ()))


def route_slots(routes, sources, capacity, experts):
    routes_flat = routes.reshape(sources, -1)
    matches = (
        routes_flat[:, :, None] == jnp.arange(experts, dtype=jnp.int32)[None, None, :]
    ).astype(jnp.int32)
    running = jnp.cumsum(matches, axis=1) - 1
    placed = jnp.sum(matches * running, axis=2)
    return routes_flat * capacity + placed


def slot_tokens(slots, sources, capacity, experts, choices_each):
    per_source = slots.shape[1]
    token_ids = (jnp.arange(sources * per_source, dtype=jnp.int32) // choices_each).reshape(
        sources, per_source
    )
    source_ids = jnp.arange(sources, dtype=jnp.int32)[:, None]
    table = jnp.zeros((sources, experts * capacity), jnp.int32).at[source_ids, slots].set(token_ids)
    return table.reshape(sources, experts, capacity)


def place_rows(spread, slots, total_rows):
    return jnp.zeros((total_rows, spread.shape[1]), spread.dtype).at[slots].set(spread)


def pick_rows(buffer, slots):
    return jnp.take(buffer, slots, axis=0).reshape(-1, TOP, buffer.shape[1]).astype(jnp.float32)


def normalize(values):
    inverse = lax.rsqrt(jnp.mean(values * values, axis=-1, keepdims=True) + EPSILON)
    return (inverse, values * inverse)


def norm_backward(grad_normed, unit, inverse, gain):
    grad_unit = grad_normed * gain
    inner = jnp.mean(grad_unit * unit, axis=-1, keepdims=True)
    return (inverse * (grad_unit - unit * inner), jnp.sum(grad_normed * unit, axis=0))


def masked_scores(query_head, key_head, allowed, scaling):
    scores = (
        lax.dot_general(query_head, key_head, CONTRACT_COLUMNS, preferred_element_type=jnp.float32)
        * scaling
    )
    return jnp.where(allowed, scores, NEGATIVE)


def local(
    layer_input,
    kv_weight,
    norm_gains,
    query_maps,
    output_maps,
    gate_up_maps,
    down_maps,
    att_routes,
    att_gates,
    mlp_routes,
    mlp_gates,
    segments,
    cotangent,
):
    experts = lax.axis_size("ep")
    me_index = lax.axis_index("ep")
    tok_dev = layer_input.shape[0]
    model_width = layer_input.shape[1]
    capacity = 3 * tok_dev // experts
    seq_len = tok_dev * experts
    rows_total = experts * capacity
    features = HEADS * HEAD_DIM
    scaling = HEAD_DIM ** (-0.5)
    kv_full, gains_full, query_full, output_full, gate_up_full, down_full = (
        lax.all_gather(kv_weight.astype(jnp.bfloat16), "grp", axis=1, tiled=True),
        lax.all_gather(norm_gains.astype(jnp.bfloat16), "grp", axis=1, tiled=True),
        lax.all_gather(query_maps.astype(jnp.bfloat16), "grp", axis=1, tiled=True),
        lax.all_gather(output_maps.astype(jnp.bfloat16), "grp", axis=1, tiled=True),
        lax.all_gather(gate_up_maps.astype(jnp.bfloat16), "grp", axis=1, tiled=True),
        lax.all_gather(down_maps.astype(jnp.bfloat16), "grp", axis=1, tiled=True),
    )
    query_full = query_full[0]
    output_full = output_full[0]
    gate_up_full = gate_up_full[0]
    down_full = down_full[0]
    hidden = down_full.shape[0]
    gain_one = gains_full[0].astype(jnp.float32)
    gain_two = gains_full[1].astype(jnp.float32)
    att_all = route_slots(att_routes[0], experts, capacity, experts)
    mlp_all = route_slots(mlp_routes[0], experts, capacity, experts)
    att_mine = lax.dynamic_index_in_dim(att_all, me_index, 0, keepdims=False)
    mlp_mine = lax.dynamic_index_in_dim(mlp_all, me_index, 0, keepdims=False)
    query_places = lax.dynamic_index_in_dim(
        slot_tokens(att_all, experts, capacity, experts, TOP), me_index, 1, keepdims=False
    ).reshape(-1)
    segment_row = segments[0]
    key_places = jnp.arange(seq_len, dtype=jnp.int32)
    allowed = (segment_row[None, :] == jnp.take(segment_row, query_places)[:, None]) & (
        key_places[None, :] <= query_places[:, None]
    )
    xfloat = layer_input.astype(jnp.float32)
    inverse_one, unit_one = normalize(xfloat)
    normed_one = (unit_one * gain_one).astype(jnp.bfloat16)
    keys_values = lax.dot_general(
        normed_one, kv_full, CONTRACT_COLUMNS, preferred_element_type=jnp.float32
    ).astype(jnp.bfloat16)
    group_kv = lax.all_gather(keys_values, "ep", axis=0, tiled=True)
    key_heads = group_kv[:, :features].reshape(seq_len, HEADS, HEAD_DIM).transpose(1, 0, 2)
    value_heads = group_kv[:, features:].reshape(seq_len, HEADS, HEAD_DIM).transpose(1, 0, 2)
    send_att = place_rows(jnp.repeat(normed_one, TOP, axis=0), att_mine, rows_total).reshape(
        experts, capacity, model_width
    )
    att_in = lax.all_to_all(send_att, "ep", split_axis=0, concat_axis=0, tiled=True).reshape(
        rows_total, model_width
    )
    queries = jnp.dot(att_in, query_full, preferred_element_type=jnp.float32).astype(jnp.bfloat16)
    query_heads = queries.reshape(rows_total, HEADS, HEAD_DIM).transpose(1, 0, 2)

    def head_forward(operands):
        query_head, key_head, value_head = operands
        scores = masked_scores(query_head, key_head, allowed, scaling)
        row_peak = jnp.max(scores, axis=1, keepdims=True)
        exponent = jnp.exp(scores - row_peak)
        row_total = jnp.sum(exponent, axis=1, keepdims=True)
        probs_low = (exponent / row_total).astype(jnp.bfloat16)
        head_out = jnp.dot(probs_low, value_head, preferred_element_type=jnp.float32).astype(
            jnp.bfloat16
        )
        return (head_out, (row_peak + jnp.log(row_total))[:, 0])

    head_outs, logsums = lax.map(head_forward, (query_heads, key_heads, value_heads))
    att_heads = head_outs.transpose(1, 0, 2).reshape(rows_total, features)
    att_rows = jnp.dot(att_heads, output_full, preferred_element_type=jnp.float32).astype(
        jnp.bfloat16
    )
    att_back = lax.all_to_all(
        att_rows.reshape(experts, capacity, model_width),
        "ep",
        split_axis=0,
        concat_axis=0,
        tiled=True,
    ).reshape(rows_total, model_width)
    residual_one = xfloat + jnp.sum(att_gates[:, :, None] * pick_rows(att_back, att_mine), axis=1)
    inverse_two, unit_two = normalize(residual_one)
    normed_two = (unit_two * gain_two).astype(jnp.bfloat16)
    send_mlp = place_rows(jnp.repeat(normed_two, TOP, axis=0), mlp_mine, rows_total).reshape(
        experts, capacity, model_width
    )
    mlp_in = lax.all_to_all(send_mlp, "ep", split_axis=0, concat_axis=0, tiled=True).reshape(
        rows_total, model_width
    )
    gate_up = jnp.dot(mlp_in, gate_up_full, preferred_element_type=jnp.float32)
    gate_part = gate_up[:, :hidden]
    up_part = gate_up[:, hidden:]
    sigmoid_gate = jax.nn.sigmoid(gate_part)
    silu_gate = gate_part * sigmoid_gate
    activated = (silu_gate * up_part).astype(jnp.bfloat16)
    mlp_rows = jnp.dot(activated, down_full, preferred_element_type=jnp.float32).astype(
        jnp.bfloat16
    )
    mlp_back = lax.all_to_all(
        mlp_rows.reshape(experts, capacity, model_width),
        "ep",
        split_axis=0,
        concat_axis=0,
        tiled=True,
    ).reshape(rows_total, model_width)
    final = residual_one + jnp.sum(mlp_gates[:, :, None] * pick_rows(mlp_back, mlp_mine), axis=1)
    output = final.astype(jnp.bfloat16)
    grad_final = cotangent.astype(jnp.float32)
    grad_mlp_ret = (
        (mlp_gates[:, :, None] * grad_final[:, None, :])
        .astype(jnp.bfloat16)
        .reshape(-1, model_width)
    )
    send_grad_mlp = place_rows(grad_mlp_ret, mlp_mine, rows_total).reshape(
        experts, capacity, model_width
    )
    grad_mlp_rows = lax.all_to_all(
        send_grad_mlp, "ep", split_axis=0, concat_axis=0, tiled=True
    ).reshape(rows_total, model_width)
    grad_down = lax.dot_general(
        activated, grad_mlp_rows, CONTRACT_ROWS, preferred_element_type=jnp.float32
    )
    grad_act = lax.dot_general(
        grad_mlp_rows, down_full, CONTRACT_COLUMNS, preferred_element_type=jnp.float32
    )
    grad_gate = grad_act * up_part * sigmoid_gate * (1.0 + gate_part * (1.0 - sigmoid_gate))
    grad_up = grad_act * silu_gate
    grad_gate_up = jnp.concatenate([grad_gate, grad_up], axis=1).astype(jnp.bfloat16)
    grad_gate_up_w = lax.dot_general(
        mlp_in, grad_gate_up, CONTRACT_ROWS, preferred_element_type=jnp.float32
    )
    grad_mlp_in = lax.dot_general(
        grad_gate_up, gate_up_full, CONTRACT_COLUMNS, preferred_element_type=jnp.float32
    ).astype(jnp.bfloat16)
    mlp_returned = lax.all_to_all(
        grad_mlp_in.reshape(experts, capacity, model_width),
        "ep",
        split_axis=0,
        concat_axis=0,
        tiled=True,
    ).reshape(rows_total, model_width)
    grad_normed_two = jnp.sum(pick_rows(mlp_returned, mlp_mine), axis=1)
    grad_inner_two, grad_gain_two = norm_backward(grad_normed_two, unit_two, inverse_two, gain_two)
    grad_residual = grad_final + grad_inner_two
    grad_att_ret = (
        (att_gates[:, :, None] * grad_residual[:, None, :])
        .astype(jnp.bfloat16)
        .reshape(-1, model_width)
    )
    send_grad_att = place_rows(grad_att_ret, att_mine, rows_total).reshape(
        experts, capacity, model_width
    )
    grad_att_rows = lax.all_to_all(
        send_grad_att, "ep", split_axis=0, concat_axis=0, tiled=True
    ).reshape(rows_total, model_width)
    grad_output_w = lax.dot_general(
        att_heads, grad_att_rows, CONTRACT_ROWS, preferred_element_type=jnp.float32
    )
    grad_heads_flat = lax.dot_general(
        grad_att_rows, output_full, CONTRACT_COLUMNS, preferred_element_type=jnp.float32
    ).astype(jnp.bfloat16)
    grad_head_major = grad_heads_flat.reshape(rows_total, HEADS, HEAD_DIM).transpose(1, 0, 2)

    def head_backward(operands):
        query_head, key_head, value_head, grad_head, logsum = operands
        scores = masked_scores(query_head, key_head, allowed, scaling)
        probs_full = jnp.exp(scores - logsum[:, None])
        grad_probs = lax.dot_general(
            grad_head, value_head, CONTRACT_COLUMNS, preferred_element_type=jnp.float32
        )
        correction = jnp.sum(probs_full * grad_probs, axis=1, keepdims=True)
        grad_scores = (probs_full * (grad_probs - correction)).astype(jnp.bfloat16)
        grad_query = jnp.dot(grad_scores, key_head, preferred_element_type=jnp.float32) * scaling
        grad_key = (
            lax.dot_general(
                grad_scores, query_head, CONTRACT_ROWS, preferred_element_type=jnp.float32
            )
            * scaling
        )
        grad_value = lax.dot_general(
            probs_full.astype(jnp.bfloat16),
            grad_head,
            CONTRACT_ROWS,
            preferred_element_type=jnp.float32,
        )
        return (grad_query, grad_key, grad_value)

    grad_query_heads, grad_key_heads, grad_value_heads = lax.map(
        head_backward, (query_heads, key_heads, value_heads, grad_head_major, logsums)
    )
    grad_queries = (
        grad_query_heads.transpose(1, 0, 2).reshape(rows_total, features).astype(jnp.bfloat16)
    )
    grad_kv_group = jnp.concatenate(
        [
            grad_key_heads.transpose(1, 0, 2).reshape(seq_len, features),
            grad_value_heads.transpose(1, 0, 2).reshape(seq_len, features),
        ],
        axis=1,
    )
    kv_sums = lax.psum_scatter(grad_kv_group, "ep", scatter_dimension=0, tiled=True)
    grad_query_w = lax.dot_general(
        att_in, grad_queries, CONTRACT_ROWS, preferred_element_type=jnp.float32
    )
    grad_att_in = lax.dot_general(
        grad_queries, query_full, CONTRACT_COLUMNS, preferred_element_type=jnp.float32
    ).astype(jnp.bfloat16)
    att_returned = lax.all_to_all(
        grad_att_in.reshape(experts, capacity, model_width),
        "ep",
        split_axis=0,
        concat_axis=0,
        tiled=True,
    ).reshape(rows_total, model_width)
    grad_kv_low = kv_sums.astype(jnp.bfloat16)
    grad_normed_one = jnp.sum(pick_rows(att_returned, att_mine), axis=1) + jnp.dot(
        grad_kv_low, kv_full, preferred_element_type=jnp.float32
    )
    grad_kv_w = lax.dot_general(
        grad_kv_low, normed_one, CONTRACT_ROWS, preferred_element_type=jnp.float32
    )
    grad_inner_one, grad_gain_one = norm_backward(grad_normed_one, unit_one, inverse_one, gain_one)
    grad_input = grad_residual + grad_inner_one
    grad_gains = jnp.stack([grad_gain_one, grad_gain_two])
    grad_kv_w, grad_gains = (
        lax.psum(grad_kv_w.astype(jnp.bfloat16), "ep").astype(jnp.float32),
        lax.psum(grad_gains.astype(jnp.bfloat16), "ep").astype(jnp.float32),
    )
    kv_grad, gains_grad, query_grad, output_grad, gate_up_grad, down_grad = (
        lax.psum_scatter(
            grad_kv_w.astype(jnp.bfloat16), "grp", scatter_dimension=1, tiled=True
        ).astype(jnp.float32),
        lax.psum_scatter(
            grad_gains.astype(jnp.bfloat16), "grp", scatter_dimension=1, tiled=True
        ).astype(jnp.float32),
        lax.psum_scatter(
            grad_query_w[None].astype(jnp.bfloat16), "grp", scatter_dimension=1, tiled=True
        ).astype(jnp.float32),
        lax.psum_scatter(
            grad_output_w[None].astype(jnp.bfloat16), "grp", scatter_dimension=1, tiled=True
        ).astype(jnp.float32),
        lax.psum_scatter(
            grad_gate_up_w[None].astype(jnp.bfloat16), "grp", scatter_dimension=1, tiled=True
        ).astype(jnp.float32),
        lax.psum_scatter(
            grad_down[None].astype(jnp.bfloat16), "grp", scatter_dimension=1, tiled=True
        ).astype(jnp.float32),
    )
    return (
        output,
        grad_input,
        kv_grad,
        gains_grad,
        query_grad,
        output_grad,
        gate_up_grad,
        down_grad,
    )


def solution(mesh):
    placed = (
        P(("grp", "ep"), None),
        P(None, "grp"),
        P(None, "grp"),
        P("ep", "grp", None),
        P("ep", "grp", None),
        P("ep", "grp", None),
        P("ep", "grp", None),
        P("grp", None, None),
        P(("grp", "ep"), None),
        P("grp", None, None),
        P(("grp", "ep"), None),
        P("grp", None),
        P(("grp", "ep"), None),
    )
    return jax.shard_map(
        local,
        mesh=mesh,
        in_specs=placed,
        out_specs=(
            P(("grp", "ep"), None),
            P(("grp", "ep"), None),
            P(None, "grp"),
            P(None, "grp"),
            P("ep", "grp", None),
            P("ep", "grp", None),
            P("ep", "grp", None),
            P("ep", "grp", None),
        ),
        check_vma=False,
    )
```

profile of v0, /device:TPU:0, one launch (start us, length us, event | category | flops | bytes accessed | tf_op | source)
XLA Modules:
  0.0 2518.2 jit_solution(2245460370316765393)
XLA Ops:
  24.6 82.5 %all-gather.9.cloned.1.call-done = bf16[4096,2048]{1,0:T(8,128)(2,1)} async-done(((bf16[4096,256]{1,0:T(8,128)(2,1)}), bf16[4096,2048]{1,0:T(8,128)(2,1)}) %all-gather.9.cloned.1.call-update) | async-done | bytes 16777232 | tf_op jit(solution)/shard_map/all_gather | solution.py:89
  107.1 18.0 convolution_convert_fusion.2
  187.9 134.5 %all-to-all-done = bf16[4,192,2048]{2,1,0:T(8,128)(2,1)S(1)} async-done(((bf16[4,192,2048]{2,1,0:T(8,128)(2,1)}), bf16[4,192,2048]{2,1,0:T(8,128)(2,1)S(1)}, u32[]{:S(2)}, u32[]{:S(2)}) %all-to-all-start) | async-done | bytes 3145760 | tf_op jit(solution)/shard_map/all_to_all | solution.py:127
  334.1 39.2 %all-gather.11.cloned.1.call-done = bf16[1024,4096]{1,0:T(8,128)(2,1)} async-done(((bf16[256,4096]{1,0:T(8,128)(2,1)}), bf16[1024,4096]{1,0:T(8,128)(2,1)}) %all-gather.11.cloned.1.call-update) | async-done | bytes 8388624 | tf_op jit(solution)/shard_map/all_gather | solution.py:121
  383.2 109.2 %while.28 = (s32[]{:T(128)}, bf16[16,768,128]{1,2,0:T(8,128)(2,1)}, f32[16,768]{1,0:T(8,128)}, bf16[16,768,128]{2,1,0:T(8,128)(2,1)S(1)}, bf16[16,1024,128]{2,1,...) while((s32[]{:T(128)}, bf16[16,768,128]{1,2,0:T(8,128)(2,1)}, ...), condition=%wide.region_9.10_spmd.clone, body=%wide.region_6.9_spmd.clone.sunk | while | flops 411401472 | bytes 11191425 | solution.py:145
  492.4 13.1 fusion.71
  509.8 71.0 %all-to-all-done.1 = bf16[4,192,2048]{2,1,0:T(8,128)(2,1)S(1)} async-done(((bf16[4,192,2048]{2,1,0:T(8,128)(2,1)}), bf16[4,192,2048]{2,1,0:T(8,128)(2,1)S(1)}, u32[]{:S(2)}, u32[]{:S(2)}) %all-to-all-start.1) | async-done | bytes 3145760 | tf_op jit(solution)/shard_map/all_to_all | solution.py:150
  638.1 52.5 %all-to-all-done.2 = bf16[4,192,2048]{2,1,0:T(8,128)(2,1)} async-done(((bf16[4,192,2048]{2,1,0:T(8,128)(2,1)}), bf16[4,192,2048]{2,1,0:T(8,128)(2,1)}, u32[]{:S(2)}, u32[]{:S(2)}) %all-to-all-start.2) | async-done | bytes 3145760 | tf_op jit(solution)/shard_map/all_to_all | solution.py:163
  694.5 47.8 %fusion.50 = f32[768,11264]{1,0:T(8,128)} fusion(bf16[768,2048]{1,0:T(8,128)(2,1)} %bitcast.24, bf16[1,2048,11264]{2,1,0:T(8,128)(2,1)} %all-gather.15.cloned.1.call-done), kind=kOutput, calls=%fused_computation.69 | convolution fusion | flops 35433480192 | bytes 83886080 | tf_op jit(solution)/shard_map/dot_general | solution.py:166
  742.3 22.2 all-to-all-done.4
  764.6 36.2 %multiply_convert_fusion.2 = (bf16[768,5632]{1,0:T(8,128)(2,1)}, bf16[768,5632]{1,0:T(8,128)(2,1)}, bf16[768,5632]{1,0:T(8,128)(2,1)}) fusion(f32[768,11264]{1,0:T(8,128)} %fusion.50, bf16[768,2048]{1,0:T(8,128)(2,1)S(1)} %bitcast.250, bf16[1,5632,2048]{2,1,0:T(8,128)(2,1)} %all-gather.17.cloned.1.call-done), kind=kOutput, calls=%fused_computation.79 | convolution fusion | flops 17781620736 | bytes 86769664 | tf_op jit(solution)/shard_map/dot_general | solution.py:199
  800.8 46.8 %fusion.65 = bf16[768,2048]{1,0:T(8,128)(2,1)} fusion(bf16[1,2048,11264]{2,1,0:T(8,128)(2,1)} %all-gather.15.cloned.1.call-done, bf16[768,5632]{1,0:T(8,128)(2,1)} %get-tuple-element.215, bf16[768,5632]{1,0:T(8,128)(2,1)} %get-tuple-element.214), kind=kOutput, calls=%fused_computation.104 | convolution fusion | flops 35469656064 | bytes 66584576 | tf_op jit(solution)/shard_map/dot_general | solution.py:208
  851.3 24.6 fusion.80
  875.9 45.5 %all-to-all-done.5 = bf16[4,192,2048]{2,1,0:T(8,128)(2,1)S(1)} async-done(((bf16[4,192,2048]{2,1,0:T(8,128)(2,1)}), bf16[4,192,2048]{2,1,0:T(8,128)(2,1)S(1)}, u32[]{:S(2)}, u32[]{:S(2)}) %all-to-all-start.5) | async-done | bytes 3145760 | tf_op jit(solution)/shard_map/all_to_all | solution.py:211
  930.1 66.7 %all-to-all-done.3 = bf16[4,192,2048]{2,1,0:T(8,128)(2,1)} async-done(((bf16[4,192,2048]{2,1,0:T(8,128)(2,1)}), bf16[4,192,2048]{2,1,0:T(8,128)(2,1)}, u32[]{:S(2)}, u32[]{:S(2)}) %all-to-all-start.3) | async-done | bytes 3145760 | tf_op jit(solution)/shard_map/all_to_all | solution.py:175
  1067.4 70.1 %all-to-all-done.6 = bf16[4,192,2048]{2,1,0:T(8,128)(2,1)S(1)} async-done(((bf16[4,192,2048]{2,1,0:T(8,128)(2,1)}), bf16[4,192,2048]{2,1,0:T(8,128)(2,1)S(1)}, u32[]{:S(2)}, u32[]{:S(2)}) %all-to-all-start.6) | async-done | bytes 3145760 | tf_op jit(solution)/shard_map/all_to_all | solution.py:229
  1149.2 246.7 %while.29 = (s32[]{:T(128)}, bf16[16,768,128]{1,2,0:T(8,128)(2,1)}, f32[16,1024,128]{1,2,0:T(8,128)}, f32[16,1024,128]{1,2,0:T(8,128)}, bf16[16,768,128]{2,1,0:T...) while((s32[]{:T(128)}, bf16[16,768,128]{1,2,0:T(8,128)(2,1)}, ...), condition=%wide.region_23.25_spmd.clone, body=%wide.region_21.24_spmd.clone.sunk | while | flops 1016397056 | bytes 67074284 | solution.py:264
  1396.0 11.5 pad_maximum_fusion.1
  1407.5 278.3 %reduce-scatter.12.cloned.1.call-done = f32[256,4096]{0,1:T(8,128)} async-done(((f32[1024,4096]{0,1:T(8,128)}), f32[256,4096]{0,1:T(8,128)}) %reduce-scatter.12.cloned.1.call-update) | async-done | bytes 4194320 | tf_op jit(solution)/shard_map/reduce_scatter | solution.py:277
  1685.8 10.8 convolution_convert_fusion.1
  1698.5 11.1 convert_bitcast_fusion.2
  1712.1 11.5 convert_bitcast_fusion.1
  1725.6 25.0 convert_bitcast_fusion
  1767.9 70.8 %all-to-all-done.7 = bf16[4,192,2048]{2,1,0:T(8,128)(2,1)S(1)} async-done(((bf16[4,192,2048]{2,1,0:T(8,128)(2,1)}), bf16[4,192,2048]{2,1,0:T(8,128)(2,1)S(1)}, u32[]{:S(2)}, u32[]{:S(2)}) %all-to-all-start.7) | async-done | bytes 3145760 | tf_op jit(solution)/shard_map/all_to_all | solution.py:284
  1859.8 13.4 fusion.92
  1874.4 45.2 %convolution_convert_fusion = bf16[2048,11264]{1,0:T(8,128)(2,1)} fusion(bf16[768,2048]{1,0:T(8,128)(2,1)} %bitcast.24, bf16[768,5632]{1,0:T(8,128)(2,1)} %get-tuple-element.215, bf16[768,5632]{1,0:T(8,128)(2,1)} %get-tuple-element.214), kind=kOutput, calls=%fused_computation.71 | convolution fusion | flops 35491151872 | bytes 66584576 | tf_op jit(solution)/shard_map/dot_general | solution.py:205
  1923.0 40.3 %reduce-scatter.16.cloned.1.call-done = bf16[1,256,2048]{2,1,0:T(8,128)(2,1)} async-done(((bf16[1,2048,2048]{2,1,0:T(8,128)(2,1)}), bf16[1,256,2048]{2,1,0:T(8,128)(2,1)}) %reduce-scatter.16.cloned.1.call-update) | async-done | bytes 1048592 | tf_op jit(solution)/shard_map/reduce_scatter | solution.py:315
  1966.0 147.2 %reduce-scatter.18.cloned.1.call-done = bf16[1,704,2048]{2,1,0:T(8,128)(2,1)} async-done(((bf16[1,5632,2048]{2,1,0:T(8,128)(2,1)}), bf16[1,704,2048]{2,1,0:T(8,128)(2,1)}) %reduce-scatter.18.cloned.1.call-update) | async-done | bytes 2883600 | tf_op jit(solution)/shard_map/reduce_scatter | solution.py:321
  2120.4 30.2 %reduce-scatter.24.cloned.1.call-done = bf16[256,2]{1,0:T(8,128)(2,1)} async-done(((bf16[2048,2]{1,0:T(8,128)(2,1)}), bf16[256,2]{1,0:T(8,128)(2,1)}) %reduce-scatter.24.cloned.1.call-update) | async-done | bytes 1040
  2151.5 11.7 psum.17
  2163.8 254.8 %reduce-scatter.22.cloned.1.call-done = bf16[1,16,180224]{2,1,0:T(8,128)(2,1)} async-done(((bf16[1,128,180224]{2,1,0:T(8,128)(2,1)}), bf16[1,16,180224]{2,1,0:T(8,128)(2,1)}) %reduce-scatter.22.cloned.1.call-update) | async-done | bytes 5767184
  2427.0 80.5 %all-reduce.2.cloned.1.call-done = bf16[4096,256]{1,0:T(8,128)(2,1)} async-done(((bf16[4096,256]{1,0:T(8,128)(2,1)}), bf16[4096,256]{1,0:T(8,128)(2,1)}) %all-reduce.2.cloned.1.call-update) | async-done | bytes 2097168 | tf_op jit(solution)/shard_map/psum | solution.py:302
  (664 shorter events, 689.0 us)
Async XLA Ops:
  7.2 99.9 %all-gather.9.cloned.1.call-start = ((), (), s32[]{:S(2)}) async-start(), calls=%async_computation.16 | async-start | bytes 18874368 | tf_op jit(solution)/shard_map/all_gather | solution.py:89
  11.1 311.3 %all-gather.7.cloned.1.call-start = ((), (), s32[]{:S(2)}) async-start(), calls=%async_computation.15 | async-start | bytes 9437184 | tf_op jit(solution)/shard_map/all_gather | solution.py:91
  12.3 361.0 %all-gather.11.cloned.1.call-start = ((), (), s32[]{:S(2)}) async-start(), calls=%async_computation.17 | async-start | bytes 10485760 | tf_op jit(solution)/shard_map/all_gather | solution.py:121
  24.5 126.0 %copy-start.11 = (bf16[256,2048]{1,0:T(8,128)(2,1)}, bf16[256,2048]{1,0:T(8,128)(2,1)S(1)}, u32[]{:S(2)}) copy-start(bf16[256,2048]{1,0:T(8,128)(2,1)S(1)} %fusion.87) | copy-start | bytes 3145732
  125.1 367.3 %all-gather.13.cloned.1.call-start = ((), (), s32[]{:S(2)}) async-start(), calls=%async_computation.18 | async-start | bytes 9437184 | tf_op jit(solution)/shard_map/all_gather | solution.py:92
  127.9 566.6 %all-gather.15.cloned.1.call-start = ((), (), s32[]{:S(2)}) async-start(), calls=%async_computation.19 | async-start | bytes 51904512 | tf_op jit(solution)/shard_map/all_gather | solution.py:93
  162.3 160.1 %all-to-all-start = ((bf16[4,192,2048]{2,1,0:T(8,128)(2,1)}), bf16[4,192,2048]{2,1,0:T(8,128)(2,1)S(1)}, u32[]{:S(2)}, u32[]{:S(2)}) async-start(bf16[4,192,2048]{2,1,0:T(8,128)(2,1)} %bitcast.5), calls=%async_computation | async-start | bytes 6291456 | tf_op jit(solution)/shard_map/all_to_all | solution.py:127
  166.9 597.7 %all-gather.17.cloned.1.call-start = ((), (), s32[]{:S(2)}) async-start(), calls=%async_computation.20 | async-start | bytes 25952256 | tf_op jit(solution)/shard_map/all_gather | solution.py:94
  171.6 11.9 copy-start
  492.4 13.1 copy-start.17
  505.5 75.3 %all-to-all-start.1 = ((bf16[4,192,2048]{2,1,0:T(8,128)(2,1)}), bf16[4,192,2048]{2,1,0:T(8,128)(2,1)S(1)}, u32[]{:S(2)}, u32[]{:S(2)}) async-start(bf16[4,192,2048]{2,1,0:T(8,128)(2,1)} %bitcast.256), calls=%async_computation.1 | async-start | bytes 6291456 | tf_op jit(solution)/shard_map/all_to_all | solution.py:150
  509.7 84.1 %copy-start.27 = (f32[256,2]{1,0:T(8,128)}, f32[256,2]{1,0:T(8,128)S(1)}, u32[]{:S(2)}) copy-start(f32[256,2]{1,0:T(8,128)S(1)} %copy.44) | copy-start | bytes 6148
  509.7 74.3 %copy-start.42 = (s32[1024]{0:T(1024)}, s32[1024]{0:T(1024)S(1)}, u32[]{:S(2)}) copy-start(s32[1024]{0:T(1024)S(1)} %pad_clamp_fusion.1) | copy-start | bytes 12292
  509.7 74.3 %copy-start.45 = (pred[512]{0:T(512)(128)(4,1)}, pred[512]{0:T(512)(128)(4,1)S(1)}, u32[]{:S(2)}) copy-start(pred[512]{0:T(512)(128)(4,1)S(1)} %compare_and_fusion.1) | copy-start | bytes 1540
  615.4 75.2 %all-to-all-start.2 = ((bf16[4,192,2048]{2,1,0:T(8,128)(2,1)}), bf16[4,192,2048]{2,1,0:T(8,128)(2,1)}, u32[]{:S(2)}, u32[]{:S(2)}) async-start(bf16[4,192,2048]{2,1,0:T(8,128)(2,1)} %bitcast.23), calls=%async_computation.2 | async-start | bytes 6291456 | tf_op jit(solution)/shard_map/all_to_all | solution.py:163
  690.6 74.0 %all-to-all-start.4 = ((bf16[4,192,2048]{2,1,0:T(8,128)(2,1)}), bf16[4,192,2048]{2,1,0:T(8,128)(2,1)S(1)}, u32[]{:S(2)}, u32[]{:S(2)}) async-start(bf16[4,192,2048]{2,1,0:T(8,128)(2,1)} %bitcast.29), calls=%async_computation.4 | async-start | bytes 6291456 | tf_op jit(solution)/shard_map/all_to_all | solution.py:193
  764.6 36.2 %copy-start.22 = (bf16[4,192,2048]{2,1,0:T(8,128)(2,1)}, bf16[4,192,2048]{2,1,0:T(8,128)(2,1)S(1)}, u32[]{:S(2)}) copy-start(bf16[4,192,2048]{2,1,0:T(8,128)(2,1)S(1)} %all-to-all-done.4) | copy-start | bytes 9437188
  847.6 73.8 %all-to-all-start.5 = ((bf16[4,192,2048]{2,1,0:T(8,128)(2,1)}), bf16[4,192,2048]{2,1,0:T(8,128)(2,1)S(1)}, u32[]{:S(2)}, u32[]{:S(2)}) async-start(bf16[4,192,2048]{2,1,0:T(8,128)(2,1)} %bitcast.257), calls=%async_computation.5 | async-start | bytes 6291456 | tf_op jit(solution)/shard_map/all_to_all | solution.py:211
  921.4 75.4 %all-to-all-start.3 = ((bf16[4,192,2048]{2,1,0:T(8,128)(2,1)}), bf16[4,192,2048]{2,1,0:T(8,128)(2,1)}, u32[]{:S(2)}, u32[]{:S(2)}) async-start(bf16[4,192,2048]{2,1,0:T(8,128)(2,1)} %bitcast.254), calls=%async_computation.3 | async-start | bytes 6291456 | tf_op jit(solution)/shard_map/all_to_all | solution.py:175
  1063.6 73.8 %all-to-all-start.6 = ((bf16[4,192,2048]{2,1,0:T(8,128)(2,1)}), bf16[4,192,2048]{2,1,0:T(8,128)(2,1)S(1)}, u32[]{:S(2)}, u32[]{:S(2)}) async-start(bf16[4,192,2048]{2,1,0:T(8,128)(2,1)} %bitcast.33), calls=%async_computation.6 | async-start | bytes 6291456 | tf_op jit(solution)/shard_map/all_to_all | solution.py:229
  1067.3 618.5 %reduce-scatter.12.cloned.1.call-start = ((), (), s32[]{:S(2)}) async-start(), calls=%async_computation.21 | async-start | bytes 20971520 | tf_op jit(solution)/shard_map/reduce_scatter | solution.py:277
  1407.4 278.4 %copy-start.12 = (bf16[256,2048]{1,0:T(8,128)(2,1)S(1)}, bf16[256,2048]{1,0:T(8,128)(2,1)}, u32[]{:S(2)}) copy-start(bf16[256,2048]{1,0:T(8,128)(2,1)} %copy-done.11) | copy-start | bytes 3145732
  1407.5 512.2 %reduce-scatter.20.cloned.1.call-start = ((), (), s32[]{:S(2)}) async-start(), calls=%async_computation.25 | async-start | bytes 18874368 | tf_op jit(solution)/shard_map/reduce_scatter | solution.py:306
  1696.6 223.6 %reduce-scatter.14.cloned.1.call-start = ((), (), s32[]{:S(2)}) async-start(), calls=%async_computation.22 | async-start | bytes 9437184 | tf_op jit(solution)/shard_map/reduce_scatter | solution.py:312
  1709.6 253.6 %reduce-scatter.16.cloned.1.call-start = ((), (), s32[]{:S(2)}) async-start(), calls=%async_computation.23 | async-start | bytes 9437184 | tf_op jit(solution)/shard_map/reduce_scatter | solution.py:315
  1723.6 389.6 %reduce-scatter.18.cloned.1.call-start = ((), (), s32[]{:S(2)}) async-start(), calls=%async_computation.24 | async-start | bytes 25952256 | tf_op jit(solution)/shard_map/reduce_scatter | solution.py:321
  1763.3 75.4 %copy-start.43 = (s32[1024]{0:T(1024)S(1)}, s32[1024]{0:T(1024)}, u32[]{:S(2)}) copy-start(s32[1024]{0:T(1024)} %copy-done.42) | copy-start | bytes 12292
  1763.3 75.4 %all-to-all-start.7 = ((bf16[4,192,2048]{2,1,0:T(8,128)(2,1)}), bf16[4,192,2048]{2,1,0:T(8,128)(2,1)S(1)}, u32[]{:S(2)}, u32[]{:S(2)}) async-start(bf16[4,192,2048]{2,1,0:T(8,128)(2,1)} %bitcast.255), calls=%async_computation.7 | async-start | bytes 6291456 | tf_op jit(solution)/shard_map/all_to_all | solution.py:284
  1767.9 382.8 %reduce-scatter.24.cloned.1.call-start = ((), (), s32[]{:S(2)}) async-start(), calls=%async_computation.28 | async-start | bytes 589824
  1874.3 544.3 %reduce-scatter.22.cloned.1.call-start = ((), (), s32[]{:S(2)}) async-start(), calls=%async_computation.27 | async-start | bytes 51904512
  1919.6 587.9 %all-reduce.2.cloned.1.call-start = ((), (), s32[]{:S(2)}) async-start(), calls=%async_computation.26 | async-start | bytes 4194304 | tf_op jit(solution)/shard_map/psum | solution.py:302
  1966.0 152.4 %copy-start.9 = (f32[256,2048]{1,0:T(8,128)S(1)}, f32[256,2048]{1,0:T(8,128)}, u32[]{:S(2)}) copy-start(f32[256,2048]{1,0:T(8,128)} %copy-done.8) | copy-start | bytes 6291460
  (89 other events, 352.0 us)
Sparse Core Ops, SparseCore 0:
  11.2 95.8 all-gather.8
  109.5 54.3 all-gather.6
  166.1 207.1 all-gather.10
  375.6 52.5 all-gather.12
  430.5 214.6 all-gather.14
  647.0 116.4 all-gather.16
  1407.6 278.2 reduce-scatter.11
  1696.7 116.6 reduce-scatter.19
  1817.3 71.2 reduce-scatter.13
  1891.9 71.2 reduce-scatter.15
  1967.3 145.8 reduce-scatter.17
  2116.4 34.1 reduce-scatter.23
  2154.2 264.3 reduce-scatter.21
  2421.0 86.4 all-reduce.1
where the time goes:
time: 2530 us; the launch traced here: 2520 us
  waiting for transfers between devices  1490 us (59%)
  matrix products  568 us (22%)
  local copies, waits for them, and re-layouts  229 us (9%)
  other arithmetic  160 us (6%)
  starting transfers between devices  35.4 us (1%)
    unnamed x16, waiting for transfers between devices  286 us
    reduce_scatter x1, waiting for transfers between devices, local(): lax.psum_scatter(grad_kv_group, 'ep', scatter_dimension=0, tiled=True)  278 us
    reduce_scatter x1, waiting for transfers between devices, local(): lax.psum_scatter(grad_down[None].astype(jnp.bfloat16), 'grp', scatter_dim...  147 us
    all_to_all x1, waiting for transfers between devices, local(): lax.all_to_all(send_att, 'ep', split_axis=0, concat_axis=0, tiled=True)  134 us
    all_gather x1, waiting for transfers between devices, local(): lax.all_gather(kv_weight.astype(jnp.bfloat16), 'grp', axis=1, tiled=True)  82.5 us
    dot_general x32, matrix products, masked_scores(): lax.dot_general(query_head, key_head, CONTRACT_COLUMNS, preferred_element...  80.6 us
    psum x1, waiting for transfers between devices, local(): lax.psum(grad_kv_w.astype(jnp.bfloat16), 'ep').astype(jnp.float32)  80.5 us
    all_to_all x1, waiting for transfers between devices, local(): lax.all_to_all(att_rows.reshape(experts, capacity, model_width), 'ep', sp...  71 us
  transfers between devices with their start and end apart: 22, of which 16 were waited for; matrix products, arithmetic and copies ran while one was open for 20% of the time, Pallas kernels for 0%

commit v1 on v0

v1 whole, which is shorter than its diff:
```python
import functools

import jax
import jax.numpy as jnp
from jax import lax
from jax.experimental import pallas as pl
from jax.experimental.pallas import tpu as pltpu
from jax.sharding import PartitionSpec as P

HEADS = 16
HEAD_DIM = 128
TOP = 2


EPSILON = 1e-06
NEGATIVE = -1e30
CONTRACT_ROWS = (((0,), (0,)), ((), ()))
CONTRACT_COLUMNS = (((1,), (1,)), ((), ()))
BF16 = jnp.bfloat16
F32 = jnp.float32
VMEM_BYTES = 56 * 2**20
TILE = 512


def normalize(values):
    inverse = lax.rsqrt(jnp.mean(values * values, axis=-1, keepdims=True) + EPSILON)
    return (inverse, values * inverse)


def norm_backward(grad_normed, unit, inverse, gain):
    grad_unit = grad_normed * gain
    inner = jnp.mean(grad_unit * unit, axis=-1, keepdims=True)
    return (inverse * (grad_unit - unit * inner), jnp.sum(grad_normed * unit, axis=0))


def dot(left, right, dims=(((1,), (0,)), ((), ()))):
    return lax.dot_general(left, right, dims, preferred_element_type=F32)


def high_low(values):
    high = values.astype(BF16)
    return high, (values - high.astype(F32)).astype(BF16)


def expert_places(routes, experts):
    tokens = routes.shape[1]
    ids = jnp.arange(experts, dtype=jnp.int32)
    named = jnp.any(routes[:, None, :, :] == ids[None, :, None, None], axis=3)
    before = (jnp.arange(tokens)[:, None] < jnp.arange(tokens)[None, :]).astype(BF16)
    place = lax.dot_general(
        named.astype(BF16), before, (((2,), (0,)), ((), ())), preferred_element_type=F32
    )
    return named, place.astype(jnp.int32)


def one_hot(named, place, capacity):
    rows = jnp.arange(capacity, dtype=jnp.int32)[:, None]
    return named[..., None, :] & (place[..., None, :] == rows)


def attend_forward_kernel(sources, query_ref, key_ref, value_ref, bounds_ref, out_ref, logsum_ref):
    head = pl.program_id(0)
    capacity = query_ref.shape[0] // sources
    tokens = key_ref.shape[0] // sources
    scaling = HEAD_DIM ** (-0.5)

    @pl.when(head == 0)
    def _():
        logsum_ref[...] = jnp.zeros_like(logsum_ref)

    for source in range(sources):
        rows = slice(source * capacity, (source + 1) * capacity)
        span = (source + 1) * tokens
        first = bounds_ref[rows, 0:1]
        last = bounds_ref[rows, 1:2]
        scores = dot(query_ref[rows, :], key_ref[:span, :], CONTRACT_COLUMNS) * scaling
        places = lax.broadcasted_iota(jnp.int32, scores.shape, 1)
        scores = jnp.where((places >= first) & (places <= last), scores, NEGATIVE)
        peak = jnp.max(scores, axis=1, keepdims=True)
        exponent = jnp.exp(scores - peak)
        total = jnp.sum(exponent, axis=1, keepdims=True)
        probs = (exponent * (1.0 / total)).astype(BF16)
        out_ref[rows, :] = dot(probs, value_ref[:span, :]).astype(BF16)
        lanes = lax.broadcasted_iota(jnp.int32, (capacity, 128), 1)
        logsum_ref[rows, :] = jnp.where(lanes == head, peak + jnp.log(total), logsum_ref[rows, :])


def attend_forward(queries, keys_values, bounds, sources):
    rows, features = queries.shape
    seq = keys_values.shape[0]
    pairs = (sources + 1) / (2 * sources)
    return pl.pallas_call(
        functools.partial(attend_forward_kernel, sources),
        grid=(HEADS,),
        in_specs=[
            pl.BlockSpec((rows, HEAD_DIM), lambda h: (0, h)),
            pl.BlockSpec((seq, HEAD_DIM), lambda h: (0, h)),
            pl.BlockSpec((seq, HEAD_DIM), lambda h: (0, h + HEADS)),
            pl.BlockSpec((rows, 2), lambda h: (0, 0)),
        ],
        out_specs=[
            pl.BlockSpec((rows, HEAD_DIM), lambda h: (0, h)),
            pl.BlockSpec((rows, 128), lambda h: (0, 0)),
        ],
        out_shape=[
            jax.ShapeDtypeStruct((rows, features), BF16),
            jax.ShapeDtypeStruct((rows, 128), F32),
        ],
        compiler_params=pltpu.CompilerParams(vmem_limit_bytes=VMEM_BYTES),
        cost_estimate=pl.CostEstimate(
            flops=int(4 * rows * seq * features * pairs),
            bytes_accessed=4 * (rows + seq) * features,
            transcendentals=int(HEADS * rows * seq * pairs),
        ),
        name="attend_forward",
    )(queries, keys_values, keys_values, bounds)


def attend_backward_kernel(
    sources,
    start,
    query_ref,
    key_ref,
    value_ref,
    grad_ref,
    bounds_ref,
    logsum_ref,
    grad_query_ref,
    grad_key_ref,
    grad_value_ref,
    key_total,
    value_total,
):
    head = pl.program_id(0) + start
    capacity = query_ref.shape[0] // sources
    tokens = key_ref.shape[0] // sources
    scaling = HEAD_DIM ** (-0.5)
    for source in reversed(range(sources)):
        rows = slice(source * capacity, (source + 1) * capacity)
        span = (source + 1) * tokens
        first = bounds_ref[rows, 0:1]
        last = bounds_ref[rows, 1:2]
        query = query_ref[rows, :]
        grad = grad_ref[rows, :]
        lanes = lax.broadcasted_iota(jnp.int32, (capacity, 128), 1)
        logsum = jnp.sum(
            jnp.where(lanes == head, logsum_ref[rows, :], 0.0), axis=1, keepdims=True
        )
        scores = dot(query, key_ref[:span, :], CONTRACT_COLUMNS) * scaling
        places = lax.broadcasted_iota(jnp.int32, scores.shape, 1)
        scores = jnp.where((places >= first) & (places <= last), scores, NEGATIVE)
        probs = jnp.exp(scores - logsum)
        grad_probs = dot(grad, value_ref[:span, :], CONTRACT_COLUMNS)
        weighted = probs * grad_probs
        correction = jnp.sum(weighted, axis=1, keepdims=True)
        grad_scores = (weighted - probs * correction).astype(BF16)
        grad_query_ref[rows, :] = (dot(grad_scores, key_ref[:span, :]) * scaling).astype(BF16)
        key_part = dot(grad_scores, query, CONTRACT_ROWS)
        value_part = dot(probs.astype(BF16), grad, CONTRACT_ROWS)
        if source == sources - 1:
            key_total[...] = key_part
            value_total[...] = value_part
        else:
            key_total[:span, :] += key_part
            value_total[:span, :] += value_part
    grad_key_ref[...] = (key_total[...] * scaling).astype(BF16)
    grad_value_ref[...] = value_total[...].astype(BF16)


def attend_backward(queries, keys_values, grads, bounds, logsums, sources, start, heads):
    rows = queries.shape[0]
    features = heads * HEAD_DIM
    seq = keys_values.shape[0]
    pairs = (sources + 1) / (2 * sources)
    return pl.pallas_call(
        functools.partial(attend_backward_kernel, sources, start),
        grid=(heads,),
        in_specs=[
            pl.BlockSpec((rows, HEAD_DIM), lambda h: (0, h + start)),
            pl.BlockSpec((seq, HEAD_DIM), lambda h: (0, h + start)),
            pl.BlockSpec((seq, HEAD_DIM), lambda h: (0, h + start + HEADS)),
            pl.BlockSpec((rows, HEAD_DIM), lambda h: (0, h + start)),
            pl.BlockSpec((rows, 2), lambda h: (0, 0)),
            pl.BlockSpec((rows, 128), lambda h: (0, 0)),
        ],
        out_specs=[
            pl.BlockSpec((rows, HEAD_DIM), lambda h: (0, h)),
            pl.BlockSpec((seq, HEAD_DIM), lambda h: (0, h)),
            pl.BlockSpec((seq, HEAD_DIM), lambda h: (0, h)),
        ],
        out_shape=[
            jax.ShapeDtypeStruct((rows, features), BF16),
            jax.ShapeDtypeStruct((seq, features), BF16),
            jax.ShapeDtypeStruct((seq, features), BF16),
        ],
        scratch_shapes=[pltpu.VMEM((seq, HEAD_DIM), F32), pltpu.VMEM((seq, HEAD_DIM), F32)],
        compiler_params=pltpu.CompilerParams(vmem_limit_bytes=VMEM_BYTES),
        cost_estimate=pl.CostEstimate(
            flops=int(10 * rows * seq * features * pairs),
            bytes_accessed=8 * (rows + seq) * features,
            transcendentals=int(heads * rows * seq * pairs),
        ),
        name="attend_backward",
    )(queries, keys_values, keys_values, grads, bounds, logsums)


def feed_kernel(in_ref, grad_ref, gate_up_ref, down_ref, act_ref, grad_gate_up_ref):
    rows = in_ref.shape[0]
    step = rows // 3
    units = down_ref.shape[0]

    @pl.loop(0, 3)
    def _(part):
        here = pl.ds(pl.multiple_of(part * step, step), step)
        inputs = in_ref[here, :]
        gate = dot(inputs, gate_up_ref[:, :units])
        up = dot(inputs, gate_up_ref[:, units:])
        grad_act = dot(grad_ref[here, :], down_ref[...], CONTRACT_COLUMNS)
        sigmoid = jax.nn.sigmoid(gate)
        silu = gate * sigmoid
        act_ref[here, :] = (silu * up).astype(BF16)
        grad_gate_up_ref[here, :units] = (
            grad_act * up * sigmoid * (1.0 + gate * (1.0 - sigmoid))
        ).astype(BF16)
        grad_gate_up_ref[here, units:] = (grad_act * silu).astype(BF16)


def feed(inputs, grads, gate_up, down, offset):
    rows, width = inputs.shape
    units = gate_up.shape[1] // 2
    tiles = units // TILE
    start = offset // TILE
    return pl.pallas_call(
        feed_kernel,
        grid=(tiles,),
        in_specs=[
            pl.BlockSpec((rows, width), lambda j: (0, 0)),
            pl.BlockSpec((rows, width), lambda j: (0, 0)),
            pl.BlockSpec((width, 2 * TILE), lambda j: (0, j)),
            pl.BlockSpec((TILE, width), lambda j: (j + start, 0)),
        ],
        out_specs=[
            pl.BlockSpec((rows, TILE), lambda j: (0, j)),
            pl.BlockSpec((rows, 2 * TILE), lambda j: (0, j)),
        ],
        out_shape=[
            jax.ShapeDtypeStruct((rows, units), BF16),
            jax.ShapeDtypeStruct((rows, 2 * units), BF16),
        ],
        compiler_params=pltpu.CompilerParams(vmem_limit_bytes=VMEM_BYTES),
        cost_estimate=pl.CostEstimate(
            flops=6 * rows * width * units,
            bytes_accessed=6 * width * units + 4 * rows * width,
            transcendentals=rows * units,
        ),
        name="feed",
    )(inputs, grads, gate_up, down)


def assemble_kernel(tiles, per_chunk, *refs):
    out_ref = refs[-1]
    chunk = lax.rem(pl.program_id(0), tiles) // per_chunk
    for index, ref in enumerate(refs[:-1]):

        @pl.when(chunk == index)
        def _():
            out_ref[...] = ref[...].astype(F32)


def assemble(chunks, per_chunk):
    rows = chunks[0].shape[0]
    tiles = sum(chunk.shape[1] for chunk in chunks) // (2 * TILE)

    def place(index):
        count = chunks[index].shape[1] // (2 * TILE)

        def block(j):
            tile = j % tiles - index * per_chunk
            return (0, jnp.clip(tile, 0, count - 1) * 2 + j // tiles)

        return block

    return pl.pallas_call(
        functools.partial(assemble_kernel, tiles, per_chunk),
        grid=(2 * tiles,),
        in_specs=[pl.BlockSpec((rows, TILE), place(index)) for index in range(len(chunks))],
        out_specs=pl.BlockSpec((rows, TILE), lambda j: (0, j)),
        out_shape=jax.ShapeDtypeStruct((rows, 2 * tiles * TILE), F32),
        cost_estimate=pl.CostEstimate(
            flops=0, bytes_accessed=12 * rows * tiles * TILE, transcendentals=0
        ),
        name="assemble",
    )(*chunks)


def transpose_kernel(each, first_ref, second_ref, out_ref):
    second = lax.rem(lax.div(pl.program_id(0), each), 2)

    @pl.when(second == 0)
    def _():
        out_ref[...] = first_ref[...].astype(F32).T

    @pl.when(second == 1)
    def _():
        out_ref[...] = second_ref[...].astype(F32).T


def transpose(first, second):
    rows, columns = first.shape
    each = columns // 2 // TILE
    spec = pl.BlockSpec((rows, TILE), lambda j: (0, j // (2 * each) * each + j % each))
    return pl.pallas_call(
        functools.partial(transpose_kernel, each),
        grid=(4 * each,),
        in_specs=[spec, spec],
        out_specs=pl.BlockSpec((TILE, rows), lambda j: (j, 0)),
        out_shape=jax.ShapeDtypeStruct((2 * columns, rows), F32),
        cost_estimate=pl.CostEstimate(
            flops=0, bytes_accessed=12 * rows * columns, transcendentals=0
        ),
        name="transpose",
    )(first, second)


def rotate_gather(block, axis):
    size = lax.axis_size(axis)
    me = lax.axis_index(axis)
    parts = [block]
    for shift in range(1, size):
        parts.append(lax.ppermute(block, axis, [(i, (i + shift) % size) for i in range(size)]))
    stacked = jnp.stack(parts[::-1])
    doubled = jnp.concatenate([stacked, stacked])
    return lax.dynamic_slice_in_dim(doubled, size - 1 - me, size, 0)


def after(values, *tokens):
    return lax.optimization_barrier((values, *tokens))[0]


def flip(values, bit):
    size = lax.axis_size("grp")
    return lax.ppermute(values, "grp", [(i, i ^ (1 << bit)) for i in range(size)])


class Gather:
    def __init__(self, shards, orders):
        self.pieces = [{0: shard} for shard in shards]
        self.orders = [list(order) for order in orders]

    def step(self, *tokens):
        for pieces, order in zip(self.pieces, self.orders):
            bit = order.pop(0)
            for place, piece in list(pieces.items()):
                if tokens:
                    piece = after(piece, *tokens)
                pieces[place ^ (1 << bit)] = flip(piece, bit)

    def finish(self, *tokens):
        size = lax.axis_size("grp")
        me = lax.axis_index("grp")
        rows = [pieces[0].shape[0] for pieces in self.pieces]
        whole = jnp.zeros((size, sum(rows), self.pieces[0][0].shape[1]), BF16)
        offset = 0
        for pieces, count in zip(self.pieces, rows):
            for place, piece in pieces.items():
                if tokens:
                    piece = after(piece, *tokens)
                whole = lax.dynamic_update_slice(whole, piece[None], (me ^ place, offset, 0))
            offset += count
        return whole.reshape(size * sum(rows), -1)


def gather_gains(gains):
    size = lax.axis_size("grp")
    me = lax.axis_index("grp")
    for bit in range(size.bit_length() - 1):
        other = flip(gains, bit)
        upper = (me >> bit) & 1
        gains = jnp.where(
            upper == 0,
            jnp.concatenate([gains, other], axis=1),
            jnp.concatenate([other, gains], axis=1),
        )
    return gains


class Scatter:
    def __init__(self, terms, order):
        self.terms = terms
        self.order = list(order)

    def step(self, *tokens):
        if not self.order:
            return
        bit = self.order.pop(0)
        axis = sum(other > bit for other in self.order)
        mine = (lax.axis_index("grp") >> bit) & 1
        terms = self.terms
        if tokens:
            terms = [after(term, *tokens) for term in terms]

        def part(term, which):
            return lax.dynamic_index_in_dim(term, which, axis, keepdims=False)

        self.sent = sum(part(term, 1 - mine).astype(F32) for term in terms).astype(BF16)
        self.terms = [part(term, mine) for term in terms] + [flip(self.sent, bit)]

    def finish(self):
        while self.order:
            self.step()
        return sum(term.astype(F32) for term in self.terms)


def core_split(values, groups):
    rows, columns = values.shape
    n = columns // groups
    mine = lax.axis_index("grp") & 1
    even = jnp.concatenate([values[:, i * n : (i + 1) * n] for i in range(0, groups, 2)], axis=1)
    odd = jnp.concatenate([values[:, i * n : (i + 1) * n] for i in range(1, groups, 2)], axis=1)
    return jnp.where(mine == 0, even, odd), jnp.where(mine == 0, odd, even)


def scatter_product(split, rights, groups, first=0):
    bits = groups.bit_length() - 1
    results = []
    for place, right in enumerate(rights):
        order = list(range(1, bits))
        if (place + first) % 2:
            order = order[::-1]
        sent = dot(split[1], right, CONTRACT_ROWS).astype(BF16)
        got = flip(sent, 0)
        kept = dot(split[0], right, CONTRACT_ROWS).astype(BF16)
        shape = (2,) * (bits - 1) + (-1, right.shape[1])
        results.append(Scatter([kept.reshape(shape), got.reshape(shape)], order))
        results[-1].sent = sent
    return results


def steps(scatters, *tokens):
    for scatter in scatters:
        scatter.step(*tokens)


def finish(scatters):
    return jnp.concatenate([scatter.finish() for scatter in scatters], axis=1)


def halves(values):
    middle = values.shape[1] // 2
    return values[:, :middle], values[:, middle:]


def exchange(values, experts):
    rows, width = values.shape
    return lax.all_to_all(
        values.reshape(experts, rows // experts, width),
        "ep",
        split_axis=0,
        concat_axis=0,
        tiled=True,
    ).reshape(rows, width)


def local(
    layer_input,
    kv_weight,
    norm_gains,
    query_maps,
    output_maps,
    gate_up_maps,
    down_maps,
    att_routes,
    att_gates,
    mlp_routes,
    mlp_gates,
    segments,
    cotangent,
):
    experts = lax.axis_size("ep")
    groups = lax.axis_size("grp")
    bits = groups.bit_length() - 1
    me_index = lax.axis_index("ep")
    tok_dev = layer_input.shape[0]
    model_width = layer_input.shape[1]
    capacity = 3 * tok_dev // experts
    rows_total = experts * capacity
    hidden = gate_up_maps.shape[2] // 2

    def gather(shard):
        return lax.all_gather(shard, "grp", axis=0, tiled=True)

    gains_full = gather_gains(norm_gains.astype(BF16))
    gain_one = gains_full[0].astype(F32)
    gain_two = gains_full[1].astype(F32)
    xfloat = layer_input.astype(F32)
    inverse_one, unit_one = normalize(xfloat)
    normed_one = (unit_one * gain_one).astype(BF16)
    normed_all = rotate_gather(normed_one, "ep")

    orders = list(range(1, bits)) + [0], list(range(1, bits))[::-1] + [0]
    kv_shard = kv_weight.T.astype(BF16)
    query_shard = after(query_maps[0], normed_one).astype(BF16)
    output_shard = after(output_maps[0], query_shard).astype(BF16)
    kv_full = gather(kv_shard)
    query_gather = Gather([query_shard], orders[:1])
    output_gather = Gather([output_shard], orders[1:])
    query_gather.step()
    output_gather.step()
    units = TILE * 4
    cuts = [(start, min(units, hidden - start)) for start in range(0, hidden, units)]

    def tiles_of(start, size):
        return [
            slice(at, at + TILE)
            for tile in range(start, start + size, TILE)
            for at in (tile, hidden + tile)
        ]

    gate_up_full = []
    shard = output_shard
    for index, cut in enumerate(cuts):
        maps = after(gate_up_maps, shard)
        shard = jnp.concatenate([maps[0, :, here] for here in tiles_of(*cut)], axis=1).astype(BF16)
        gate_up_full.append(gather(shard))
        if index == 0:
            query_gather.step(shard)
            output_gather.step(shard)
            shard = after(down_maps[0], shard).astype(BF16)
            down_full = gather(shard)
    while query_gather.orders[0]:
        query_gather.step(normed_all)
        output_gather.step(normed_all)

    att_named, att_place = expert_places(att_routes[0].reshape(experts, tok_dev, TOP), experts)
    mlp_named, mlp_place = expert_places(mlp_routes[0].reshape(experts, tok_dev, TOP), experts)

    def mine(values, axis):
        return lax.dynamic_index_in_dim(values, me_index, axis, keepdims=False)

    att_pick = one_hot(mine(att_named, 1), mine(att_place, 1), capacity)
    att_send = one_hot(mine(att_named, 0), mine(att_place, 0), capacity).reshape(
        rows_total, tok_dev
    )
    mlp_send = one_hot(mine(mlp_named, 0), mine(mlp_place, 0), capacity).reshape(
        rows_total, tok_dev
    )

    def gates_at(send, routes, gates):
        ids = jnp.arange(experts, dtype=jnp.int32)
        routes = mine(routes.reshape(experts, tok_dev, TOP), 0)
        per_expert = jnp.sum(jnp.where(routes[None] == ids[:, None, None], gates[None], 0.0), axis=2)
        spread = jnp.where(
            send.reshape(experts, capacity, tok_dev), per_expert[:, None, :], 0.0
        ).reshape(rows_total, tok_dev)
        return high_low(spread)

    att_high, att_low = gates_at(att_send, att_routes, att_gates)
    mlp_high, mlp_low = gates_at(mlp_send, mlp_routes, mlp_gates)
    mlp_send = mlp_send.astype(BF16)
    places = jnp.arange(experts * tok_dev, dtype=jnp.int32).reshape(experts, 1, tok_dev)
    starts = segments[0].reshape(experts, 1, tok_dev)
    bounds = jnp.stack(
        [
            jnp.sum(jnp.where(att_pick, starts, 0), axis=2).reshape(-1),
            jnp.sum(jnp.where(att_pick, places, 0), axis=2).reshape(-1),
        ],
        axis=1,
    )
    att_pick = att_pick.astype(BF16)

    cotangent_send = (dot(mlp_high, cotangent) + dot(mlp_low, cotangent)).astype(BF16)
    cotangent_send = after(cotangent_send, normed_all)
    grad_mlp_rows = exchange(cotangent_send, experts)
    att_in = (
        jnp.einsum(
            "sct,std->scd", att_pick, after(normed_all, cotangent_send), preferred_element_type=F32
        )
        .astype(BF16)
        .reshape(rows_total, model_width)
    )
    normed_all = normed_all.reshape(experts * tok_dev, model_width)
    keys_values = dot(after(normed_all, att_in), kv_full).astype(BF16)
    query_full = query_gather.finish(keys_values)
    queries = dot(after(att_in, keys_values), query_full).astype(BF16)
    output_full = output_gather.finish(queries)
    att_heads, logsums = attend_forward(queries, keys_values, bounds, experts)
    att_rows = dot(after(att_heads, grad_mlp_rows), output_full).astype(BF16)
    att_back = exchange(att_rows, experts)
    residual_one = (
        xfloat + dot(att_high, att_back, CONTRACT_ROWS) + dot(att_low, att_back, CONTRACT_ROWS)
    )

    inverse_two, unit_two = normalize(residual_one)
    normed_two = (unit_two * gain_two).astype(BF16)
    mlp_given = dot(mlp_send, normed_two).astype(BF16)
    mlp_in = exchange(mlp_given, experts)
    grad_mlp_in = 0.0
    acts, weight_grads = [], []
    feed_in = mlp_in
    for (start, size), gate_up in zip(cuts, gate_up_full):
        act, grad_gate_up = feed(feed_in, grad_mlp_rows, gate_up, down_full, start)
        grad_mlp_in = grad_mlp_in + dot(grad_gate_up, gate_up, CONTRACT_COLUMNS)
        acts.append(act)
        if start + size == hidden:
            grad_mlp_in = grad_mlp_in.astype(BF16)
            break
        weight_grad = dot(mlp_in, after(grad_gate_up, grad_mlp_in), CONTRACT_ROWS).astype(BF16)
        weight_grads.append(
            lax.psum_scatter(weight_grad, "grp", scatter_dimension=0, tiled=True)
        )
        feed_in = after(mlp_in, weight_grad)
    activated = after(jnp.concatenate(acts, axis=1), grad_mlp_in)
    down_scatter = scatter_product(core_split(activated, groups), halves(grad_mlp_rows), groups)
    mlp_returned = after(
        exchange(grad_mlp_in, experts),
        *[scatter.terms[0] for scatter in down_scatter],
        *[scatter.sent for scatter in down_scatter],
    )

    grad_final = cotangent.astype(F32)
    grad_normed_two = dot(mlp_send, mlp_returned, CONTRACT_ROWS)
    grad_inner_two, grad_gain_two = norm_backward(grad_normed_two, unit_two, inverse_two, gain_two)
    grad_residual = grad_final + grad_inner_two

    res_high, res_low = high_low(grad_residual)
    sent_four = (
        dot(att_high, res_high) + dot(att_low, res_high) + dot(att_high, res_low)
    ).astype(BF16)
    mlp_rows = dot(after(activated, sent_four), down_full).astype(BF16)
    weight_grad = dot(mlp_in, after(grad_gate_up, mlp_rows), CONTRACT_ROWS).astype(BF16)
    weight_grads.append(lax.psum_scatter(weight_grad, "grp", scatter_dimension=0, tiled=True))
    steps(down_scatter, mlp_rows)
    grad_att_rows = after(
        exchange(sent_four, experts),
        mlp_rows,
        weight_grad,
        *[scatter.sent for scatter in down_scatter],
    )
    mlp_back = exchange(after(mlp_rows, grad_att_rows), experts)
    grad_heads = dot(grad_att_rows, output_full, CONTRACT_COLUMNS).astype(BF16)
    normed_split = core_split(normed_all, groups)
    att_split = core_split(att_in, groups)
    half = HEADS // 2
    grad_one, keys_one, values_one = attend_backward(
        queries, keys_values, grad_heads, bounds, logsums, experts, 0, half
    )
    keys_one = after(keys_one, weight_grads[0], weight_grads[1])
    kv_one = scatter_product(normed_split, [keys_one, values_one], groups)
    grad_two, keys_two, values_two = attend_backward(
        after(queries, *[scatter.terms[0] for scatter in kv_one]),
        keys_values,
        grad_heads,
        bounds,
        logsums,
        experts,
        half,
        HEADS - half,
    )
    keys_two = after(keys_two, mlp_back)
    steps(down_scatter, keys_two)
    steps(kv_one, keys_two)
    ready = [scatter.sent for scatter in kv_one + down_scatter]
    query_one, query_two = halves(query_full)
    grad_att_in = (
        dot(after(grad_one, *ready), query_one, CONTRACT_COLUMNS)
        + dot(grad_two, query_two, CONTRACT_COLUMNS)
    ).astype(BF16)
    features = HEADS * HEAD_DIM
    middle = half * HEAD_DIM
    grad_all = (
        jnp.einsum(
            "sct,scd->std",
            att_pick,
            grad_att_in.reshape(experts, capacity, model_width),
            preferred_element_type=F32,
        ).reshape(experts * tok_dev, model_width)
        + dot(keys_one, kv_full[:, :middle], CONTRACT_COLUMNS)
        + dot(keys_two, kv_full[:, middle:features], CONTRACT_COLUMNS)
        + dot(values_one, kv_full[:, features : features + middle], CONTRACT_COLUMNS)
        + dot(values_two, kv_full[:, features + middle :], CONTRACT_COLUMNS)
    ).astype(BF16)
    grad_back = exchange(grad_all, experts)
    steps(kv_one, grad_all, weight_grads[-1])
    ready = [scatter.sent for scatter in kv_one]
    kv_two = scatter_product(normed_split, [after(keys_two, *ready), values_two], groups)
    ready = [scatter.terms[0] for scatter in kv_two]
    part_one = after(finish(kv_one), *ready).astype(BF16)
    kv_grad_one = lax.psum(part_one, "ep")
    steps(kv_two, part_one)
    ready = [scatter.sent for scatter in kv_two]
    query_scatter = scatter_product(att_split, [after(grad_one, *ready)], groups)
    query_scatter += scatter_product(att_split, [after(grad_two, *ready)], groups, 1)
    ready = [scatter.terms[0] for scatter in query_scatter]
    steps(kv_two, *ready)
    ready = [scatter.sent for scatter in kv_two]
    steps(query_scatter, *ready)
    ready = [scatter.sent for scatter in query_scatter]
    output_scatter = scatter_product(
        core_split(att_heads, groups), halves(after(grad_att_rows, *ready)), groups
    )
    ready = [scatter.terms[0] for scatter in output_scatter]
    part_two = after(finish(kv_two), *ready, grad_back).astype(BF16)
    kv_grad_two = lax.psum(after(part_two, kv_grad_one), "ep")
    steps(output_scatter, part_two)
    ready = [scatter.sent for scatter in output_scatter]
    down_grad = finish(down_scatter)[None]
    mlp_back = after(mlp_back, *ready)
    output = (
        residual_one + dot(mlp_high, mlp_back, CONTRACT_ROWS) + dot(mlp_low, mlp_back, CONTRACT_ROWS)
    ).astype(BF16)
    steps(query_scatter, output)
    weight_grads = [after(part, output) for part in weight_grads]
    ready = [scatter.sent for scatter in query_scatter]
    steps(output_scatter, *ready)
    ready = [scatter.sent for scatter in output_scatter]
    grad_normed_one = jnp.sum(
        after(grad_back, *ready).reshape(experts, tok_dev, model_width).astype(F32), axis=0
    )
    query_grad = finish(query_scatter)[None]
    output_grad = finish(output_scatter)[None]
    kv_grad = transpose(kv_grad_one, kv_grad_two)
    gate_up_grad = assemble(weight_grads, units // TILE)[None]
    grad_inner_one, grad_gain_one = norm_backward(grad_normed_one, unit_one, inverse_one, gain_one)
    grad_input = grad_residual + grad_inner_one

    gains_grad = jnp.stack([grad_gain_one, grad_gain_two])
    gains_grad = gains_grad.reshape((2,) + (2,) * bits + (-1,))
    for bit in reversed(range(bits)):
        mine_bit = (lax.axis_index("grp") >> bit) & 1
        kept = lax.dynamic_index_in_dim(gains_grad, mine_bit, 1, keepdims=False)
        sent = lax.dynamic_index_in_dim(gains_grad, 1 - mine_bit, 1, keepdims=False)
        gains_grad = kept + lax.ppermute(
            sent, "grp", [(i, i ^ (1 << bit)) for i in range(groups)]
        )
    for bit in range(experts.bit_length() - 1):
        gains_grad = gains_grad + lax.ppermute(
            gains_grad, "ep", [(i, i ^ (1 << bit)) for i in range(experts)]
        )
    return (
        output,
        grad_input,
        kv_grad,
        gains_grad,
        query_grad,
        output_grad,
        gate_up_grad,
        down_grad,
    )


def solution(mesh):
    placed = (
        P(("grp", "ep"), None),
        P(None, "grp"),
        P(None, "grp"),
        P("ep", "grp", None),
        P("ep", "grp", None),
        P("ep", "grp", None),
        P("ep", "grp", None),
        P("grp", None, None),
        P(("grp", "ep"), None),
        P("grp", None, None),
        P(("grp", "ep"), None),
        P("grp", None),
        P(("grp", "ep"), None),
    )
    return jax.shard_map(
        local,
        mesh=mesh,
        in_specs=placed,
        out_specs=(
            P(("grp", "ep"), None),
            P(("grp", "ep"), None),
            P(None, "grp"),
            P(None, "grp"),
            P("ep", "grp", None),
            P("ep", "grp", None),
            P("ep", "grp", None),
            P("ep", "grp", None),
        ),
        check_vma=False,
    )
```

time: 2530 us -> 1250 us (0.49)
  waiting for transfers between devices: 1490 us -> 275 us
  Pallas kernels: 0 us -> 195 us
  matrix products: 568 us -> 394 us
  local copies, waits for them, and re-layouts: 229 us -> 126 us
  starting transfers between devices: 35.4 us -> 104 us
    reduce_scatter x5 -> x3, waiting for transfers between devices: 466 us -> 0.01 us  [local(): lax.psum_scatter(weight_grad, 'grp', scatter_dimension=0, tiled=True)]
    all_to_all x8 -> x7, waiting for transfers between devices: 533 us -> 189 us  [exchange(): lax.all_to_all(values.reshape(experts, rows // experts, width), 'ep', spl...]
    unnamed x16 -> x10, waiting for transfers between devices: 286 us -> 0.17 us
    pallas_call x0 -> x8, Pallas kernels: none -> 195 us  [the longest x3 82 us: feed(): pl.pallas_call(feed_kernel, grid=(tiles,), in_specs=[pl.BlockSpec((rows,...]
    dot_general x127 -> x52, matrix products: 568 us -> 394 us  [the longest x48 384 us: dot(): return lax.dot_general(left, right, dims, preferred_element_type=F32)]
    all_gather x6 -> x5, waiting for transfers between devices: 122 us -> 0.04 us  [gather(): return lax.all_gather(shard, 'grp', axis=0, tiled=True)]
    ppermute x0 -> x55, waiting for transfers between devices: none -> 80.2 us  [the longest x47 54.6 us: flip(): return lax.ppermute(values, 'grp', [(i, i ^ 1 << bit) for i in range(size)])]
    psum x1 -> x2, waiting for transfers between devices: 80.5 us -> 5.03 us  [the longest x1 5.03 us: local(): kv_grad_one = lax.psum(part_one, 'ep')]
  transfers between devices with their start and end apart: 22 -> 72, of which waited for: 16 -> 22; matrix products, arithmetic and copies ran while one was open for 20% -> 51% of each run, Pallas kernels for 0% -> 16%
where the time goes in v1:
time: 1250 us
  matrix products  394 us (32%)
  waiting for transfers between devices  275 us (22%)
  Pallas kernels  195 us (16%)
  other arithmetic  138 us (11%)
  local copies, waits for them, and re-layouts  126 us (10%)
  starting transfers between devices  104 us (8%)
  between operations  16.4 us (1%)
    dot_general x48, matrix products, dot(): return lax.dot_general(left, right, dims, preferred_element_type=F32)  384 us
    all_to_all x7, waiting for transfers between devices, exchange(): lax.all_to_all(values.reshape(experts, rows // experts, width), 'ep', spl...  189 us
    pallas_call x3, Pallas kernels, feed(): pl.pallas_call(feed_kernel, grid=(tiles,), in_specs=[pl.BlockSpec((rows,...  82 us
    all_to_all x7, starting transfers between devices, exchange(): lax.all_to_all(values.reshape(experts, rows // experts, width), 'ep', spl...  57.9 us
    convert_element_type x20, other arithmetic, step(): sum((part(term, 1 - mine).astype(F32) for term in terms)).astype(BF16)  55.5 us
    ppermute x47, waiting for transfers between devices, flip(): return lax.ppermute(values, 'grp', [(i, i ^ 1 << bit) for i in range(size)])  54.6 us
    pallas_call x2, Pallas kernels, attend_backward(): pl.pallas_call(functools.partial(attend_backward_kernel, sources, start),...  52.3 us
    pallas_call x1, Pallas kernels, attend_forward(): pl.pallas_call(functools.partial(attend_forward_kernel, sources), grid=(H...  38.3 us
  transfers between devices with their start and end apart: 72, of which 22 were waited for; matrix products, arithmetic and copies ran while one was open for 51% of the time, Pallas kernels for 16%

profile of v1, /device:TPU:0, one launch (start us, length us, event | category | flops | bytes accessed | tf_op | source)
XLA Modules:
  0.0 1247.9 jit_solution(173689792196153882)
XLA Ops:
  91.5 28.7 %collective-permute-done.13 = bf16[256,2048]{1,0:T(8,128)(2,1)} collective-permute-done((bf16[256,2048]{1,0:T(8,128)(2,1)S(1)}, bf16[256,2048]{1,0:T(8,128)(2,1)}, u32[]{:S(2)}, u32[]{:S(2)}) %collective-permute-start.13) | collective-permute-done | bytes 1048608 | tf_op jit(solution)/shard_map/ppermute | solution.py:342
  123.8 19.3 %collective-permute-done.3 = bf16[256,2048]{1,0:T(8,128)(2,1)} collective-permute-done((bf16[256,2048]{1,0:T(8,128)(2,1)}, bf16[256,2048]{1,0:T(8,128)(2,1)}, u32[]{:S(2)}, u32[]{:S(2)}) %collective-permute-start.3) | collective-permute-done | bytes 1048608 | tf_op jit(solution)/shard_map/ppermute | solution.py:330
  154.5 26.4 %all-to-all-start = ((bf16[4,192,2048]{2,1,0:T(8,128)(2,1)}), bf16[4,192,2048]{2,1,0:T(8,128)(2,1)}, u32[]{:S(2)}, u32[]{:S(2)}) async-start(bf16[4,192,2048]{2,1,0:T(8,128)(2,1)} %bitcast.479), calls=%async_computation | async-start | bytes 6291456 | tf_op jit(solution)/shard_map/all_to_all | solution.py:455
  191.6 23.0 %convolution_convert_fusion.3.key_ref.value_ref = bf16[1024,4096]{1,0:T(8,128)(2,1)} fusion(bf16[1024,2048]{1,0:T(8,128)(2,1)} %bitcast.470, bf16[2048,4096]{0,1:T(8,128)(2,1)} %all-gather.6.cloned.1.call-done), kind=kOutput, calls=%fused_computation.10 | convolution fusion | flops 17184063488 | bytes 29360128 | tf_op jit(solution)/shard_map/dot_general | solution.py:37
  236.5 38.3 %attend_forward.1 = (bf16[768,2048]{1,0:T(8,128)(2,1)}, f32[768,128]{1,0:T(8,128)}) custom-call(bf16[768,2048]{1,0:T(8,128)(2,1)} %convolution_convert_fusion.10.query_ref, bf16[1024,4096]{1,0:T(8,128)(2,1)} %convolution_convert_fusion.3.key_ref.value_ref, bf16[1024,4096]{1,0:T(8,128)(2,1)} %convolution_convert_fusion.3.key_ref.value_ref, ...), custom_call_target="tpu_custom_call" | custom-call | flops 4026531840 | bytes 14680064 | tf_op jit(solution)/shard_map/attend_forward/pallas_call | solution.py:92
  298.9 71.2 %all-to-all-done.1 = bf16[4,192,2048]{2,1,0:T(8,128)(2,1)} async-done(((bf16[4,192,2048]{2,1,0:T(8,128)(2,1)}), bf16[4,192,2048]{2,1,0:T(8,128)(2,1)}, u32[]{:S(2)}, u32[]{:S(2)}) %all-to-all-start.1) | async-done | bytes 3145760 | tf_op jit(solution)/shard_map/all_to_all | solution.py:455
  385.7 70.7 %all-to-all-done.2 = bf16[4,192,2048]{2,1,0:T(8,128)(2,1)S(1)} async-done(((bf16[4,192,2048]{2,1,0:T(8,128)(2,1)}), bf16[4,192,2048]{2,1,0:T(8,128)(2,1)S(1)}, u32[]{:S(2)}, u32[]{:S(2)}) %all-to-all-start.2) | async-done | bytes 3145760 | tf_op jit(solution)/shard_map/all_to_all | solution.py:455
  458.1 28.8 %feed.3 = (bf16[768,2048]{1,0:T(8,128)(2,1)}, bf16[768,4096]{1,0:T(8,128)(2,1)}) custom-call(bf16[768,2048]{1,0:T(8,128)(2,1)} %bitcast.499, bf16[768,2048]{1,0:T(8,128)(2,1)} %bitcast.42.grad_ref, bf16[2048,4096]{1,0:T(8,128)(2,1)} %all-gather.8.cloned.1.call-done.gate_up_ref, bf16[5632,2048]{1,0:T(8,128)(2,1)} %all-gather.10.cloned.1.call-done.down_ref), custom_call_target="tpu_custom_call" | custom-call | flops 19327352832 | bytes 31457280 | tf_op jit(solution)/shard_map/feed/pallas_call | solution.py:233
  486.9 20.4 %fusion.148 = f32[768,2048]{1,0:T(8,128)} fusion(bf16[768,4096]{1,0:T(8,128)(2,1)} %get-tuple-element.177, bf16[2048,4096]{1,0:T(8,128)(2,1)} %all-gather.8.cloned.1.call-done.gate_up_ref), kind=kOutput, calls=%fused_computation.354 | convolution fusion | flops 12884901888 | bytes 29360128 | tf_op jit(solution)/shard_map/dot_general | solution.py:37
  507.4 18.8 %convolution_convert_fusion.1 = bf16[2048,4096]{1,0:T(8,128)(2,1)} fusion(bf16[768,2048]{1,0:T(8,128)(2,1)S(1)} %bitcast.502, bf16[768,4096]{1,0:T(8,128)(2,1)} %get-tuple-element.177), kind=kOutput, calls=%fused_computation.1 | convolution fusion | flops 12893290496 | bytes 26214400 | tf_op jit(solution)/shard_map/dot_general | solution.py:37
  526.3 29.3 %feed.4 = (bf16[768,2048]{1,0:T(8,128)(2,1)}, bf16[768,4096]{1,0:T(8,128)(2,1)}) custom-call(bf16[768,2048]{1,0:T(8,128)(2,1)} %bitcast.500, bf16[768,2048]{1,0:T(8,128)(2,1)} %bitcast.42.grad_ref, bf16[2048,4096]{1,0:T(8,128)(2,1)} %all-gather.12.cloned.1.call-done.gate_up_ref, bf16[5632,2048]{1,0:T(8,128)(2,1)} %all-gather.10.cloned.1.call-done.down_ref), custom_call_target="tpu_custom_call" | custom-call | flops 19327352832 | bytes 31457280 | tf_op jit(solution)/shard_map/feed/pallas_call | solution.py:233
  555.6 23.2 %convolution_add_fusion = f32[768,2048]{1,0:T(8,128)} fusion(f32[768,2048]{1,0:T(8,128)} %fusion.148, bf16[768,4096]{1,0:T(8,128)(2,1)} %get-tuple-element.182, bf16[2048,4096]{1,0:T(8,128)(2,1)} %all-gather.12.cloned.1.call-done.gate_up_ref), kind=kOutput, calls=%fused_computation.36 | convolution fusion | flops 12886474752 | bytes 35651584 | tf_op jit(solution)/shard_map/dot_general | solution.py:37
  578.8 18.9 %convolution_convert_fusion = bf16[2048,4096]{1,0:T(8,128)(2,1)} fusion(bf16[768,2048]{1,0:T(8,128)(2,1)S(1)} %bitcast.503, bf16[768,4096]{1,0:T(8,128)(2,1)} %get-tuple-element.182), kind=kOutput, calls=%fused_computation | convolution fusion | flops 12893290496 | bytes 26214400 | tf_op jit(solution)/shard_map/dot_general | solution.py:37
  597.8 23.9 %feed.5 = (bf16[768,1536]{1,0:T(8,128)(2,1)}, bf16[768,3072]{1,0:T(8,128)(2,1)}) custom-call(bf16[768,2048]{1,0:T(8,128)(2,1)} %bitcast.501, bf16[768,2048]{1,0:T(8,128)(2,1)} %bitcast.42.grad_ref, bf16[2048,3072]{1,0:T(8,128)(2,1)} %all-gather.14.cloned.1.call-done.gate_up_ref, bf16[5632,2048]{1,0:T(8,128)(2,1)} %all-gather.10.cloned.1.call-done.down_ref), custom_call_target="tpu_custom_call" | custom-call | flops 14495514624 | bytes 25165824 | tf_op jit(solution)/shard_map/feed/pallas_call | solution.py:233
  628.2 15.5 %add_convert_fusion.2 = bf16[768,2048]{1,0:T(8,128)(2,1)} fusion(f32[768,2048]{1,0:T(8,128)} %convolution_add_fusion, bf16[768,3072]{1,0:T(8,128)(2,1)S(1)} %copy-done.139, bf16[2048,3072]{1,0:T(8,128)(2,1)} %all-gather.14.cloned.1.call-done.gate_up_ref), kind=kOutput, calls=%fused_computation.13 | convolution fusion | flops 9666822144 | bytes 26738688 | tf_op jit(solution)/shard_map/dot_general | solution.py:37
  655.2 8.4 concatenate.89
  671.0 11.1 convolution_convert_fusion.5
  698.6 8.5 convolution_convert_fusion.7
  707.1 11.6 all-to-all-done.3
  730.0 22.0 %convolution_convert_fusion.13 = bf16[768,2048]{1,0:T(8,128)(2,1)} fusion(bf16[768,5632]{1,0:T(8,128)(2,1)S(1)} %bitcast.473, bf16[5632,2048]{1,0:T(8,128)(2,1)} %all-gather.10.cloned.1.call-done.down_ref), kind=kOutput, calls=%fused_computation.42 | convolution fusion | flops 17718312960 | bytes 34865152 | tf_op jit(solution)/shard_map/dot_general | solution.py:37
  757.0 15.4 %convolution_convert_fusion.2 = bf16[2048,3072]{1,0:T(8,128)(2,1)} fusion(bf16[768,2048]{1,0:T(8,128)(2,1)S(1)} %bitcast.504, bf16[768,3072]{1,0:T(8,128)(2,1)} %get-tuple-element.190), kind=kOutput, calls=%fused_computation.2 | convolution fusion | flops 9669967872 | bytes 20447232 | tf_op jit(solution)/shard_map/dot_general | solution.py:37
  809.9 17.2 %all-to-all-done.4 = bf16[4,192,2048]{2,1,0:T(8,128)(2,1)} async-done(((bf16[4,192,2048]{2,1,0:T(8,128)(2,1)}), bf16[4,192,2048]{2,1,0:T(8,128)(2,1)}, u32[]{:S(2)}, u32[]{:S(2)}) %all-to-all-start.4) | async-done | bytes 3145760 | tf_op jit(solution)/shard_map/all_to_all | solution.py:455
  831.1 11.9 convolution_convert_fusion.8.grad_ref
  843.0 26.0 %attend_backward.2 = (bf16[768,1024]{1,0:T(8,128)(2,1)}, bf16[1024,1024]{1,0:T(8,128)(2,1)}, bf16[1024,1024]{1,0:T(8,128)(2,1)}) custom-call(bf16[768,2048]{1,0:T(8,128)(2,1)} %convolution_convert_fusion.10.query_ref, bf16[1024,4096]{1,0:T(8,128)(2,1)} %convolution_convert_fusion.3.key_ref.value_ref, ...), custom_call_target="tpu_custom_call" | custom-call | flops 5033164800 | bytes 14680064 | tf_op jit(solution)/shard_map/attend_backward/pallas_call | solution.py:175
  874.5 9.2 fusion.6
  893.4 26.3 %attend_backward.3 = (bf16[768,1024]{1,0:T(8,128)(2,1)}, bf16[1024,1024]{1,0:T(8,128)(2,1)}, bf16[1024,1024]{1,0:T(8,128)(2,1)}) custom-call(bf16[768,2048]{1,0:T(8,128)(2,1)} %convolution_convert_fusion.10.query_ref, bf16[1024,4096]{1,0:T(8,128)(2,1)} %convolution_convert_fusion.3.key_ref.value_ref, ...), custom_call_target="tpu_custom_call" | custom-call | flops 5033164800 | bytes 14680064 | tf_op jit(solution)/shard_map/attend_backward/pallas_call | solution.py:175
  944.1 15.3 %fusion.12 = f32[768,2048]{1,0:T(8,128)S(1)} fusion(bf16[768,1024]{1,0:T(8,128)(2,1)S(1)} %copy-done.137, bf16[2048,2048]{1,0:T(8,128)(2,1)S(1)} %bitcast.486), kind=kOutput, calls=%fused_computation.32 | convolution fusion | flops 3221225472 | bytes 12058624 | tf_op jit(solution)/shard_map/dot_general | solution.py:37
  961.6 9.4 fusion.4
  970.9 8.9 fusion.8
  991.4 19.5 %fusion.3 = bf16[1024,2048]{1,0:T(8,128)(2,1)} fusion(f32[1024,2048]{1,0:T(8,128)} %fusion.4, f32[1024,2048]{1,0:T(8,128)} %fusion.6, f32[1024,2048]{1,0:T(8,128)} %fusion.8, f32[4,256,2048]{2,1,0:T(8,128)} %fusion.64, bf16[1024,1024]{1,0:T(8,128)(2,1)} %get-tuple-element.200, bf16[2048,4096]{0,1:T(8,128)(2,1)} %all-gather.6.cloned.1.call-done), kind=kOutput, calls=%fused_computation.9 | convolution fusion | flops 4305453056 | bytes 44040192 | tf_op jit(solution)/shard_map/dot_general | solution.py:37
  1139.0 18.6 %all-to-all-done.6 = bf16[4,256,2048]{2,1,0:T(8,128)(2,1)} async-done(((bf16[4,256,2048]{2,1,0:T(8,128)(2,1)}), bf16[4,256,2048]{2,1,0:T(8,128)(2,1)}, u32[]{:S(2)}, u32[]{:S(2)}) %all-to-all-start.6) | async-done | bytes 4194336 | tf_op jit(solution)/shard_map/all_to_all | solution.py:455
  1187.4 15.2 %assemble.1 = f32[256,11264]{1,0:T(8,128)} custom-call(bf16[256,4096]{1,0:T(8,128)(2,1)} %reduce-scatter.4.cloned.1.call-done.refs_0_, bf16[256,4096]{1,0:T(8,128)(2,1)} %reduce-scatter.6.cloned.1.call-done.refs_1_, bf16[256,3072]{1,0:T(8,128)(2,1)} %reduce-scatter.8.cloned.1.call-done.refs_2_), custom_call_target="tpu_custom_call" | custom-call | bytes 17301504 | tf_op jit(solution)/shard_map/assemble/pallas_call | solution.py:283
  (652 shorter events, 520.4 us)
Async XLA Ops:
  7.2 184.4 %all-gather.6.cloned.1.call-start = ((), (), s32[]{:S(2)}) async-start(), calls=%async_computation.10 | async-start | bytes 18874368 | tf_op jit(solution)/shard_map/all_gather | solution.py:490
  11.1 374.7 %all-gather.8.cloned.1.call-start = ((), (), s32[]{:S(2)}) async-start(), calls=%async_computation.11 | async-start | bytes 18874368 | tf_op jit(solution)/shard_map/all_gather | solution.py:490
  35.0 421.4 %all-gather.10.cloned.1.call-start = ((), (), s32[]{:S(2)}) async-start(), calls=%async_computation.12 | async-start | bytes 25952256 | tf_op jit(solution)/shard_map/all_gather | solution.py:490
  39.8 486.5 %all-gather.12.cloned.1.call-start = ((), (), s32[]{:S(2)}) async-start(), calls=%async_computation.13 | async-start | bytes 18874368 | tf_op jit(solution)/shard_map/all_gather | solution.py:490
  50.7 547.1 %all-gather.14.cloned.1.call-start = ((), (), s32[]{:S(2)}) async-start(), calls=%async_computation.14 | async-start | bytes 14155776 | tf_op jit(solution)/shard_map/all_gather | solution.py:490
  76.0 71.8 %collective-permute-start.5 = (bf16[256,2048]{1,0:T(8,128)(2,1)}, bf16[256,2048]{1,0:T(8,128)(2,1)S(1)}, u32[]{:S(2)}, u32[]{:S(2)}) collective-permute-start(bf16[256,2048]{1,0:T(8,128)(2,1)} %fusion.28), channel_id=1, source_target_pairs={{0,1},{1,2},{2,3},{3,0},{4,5},{5,6},{6,7},{7,4},{8,9},{9,10},{10,1... | collective-permute-start | bytes 3145736 | tf_op jit(solution)/shard_map/ppermute | solution.py:330
  77.6 68.4 %collective-permute-start.4 = (bf16[256,2048]{1,0:T(8,128)(2,1)}, bf16[256,2048]{1,0:T(8,128)(2,1)}, u32[]{:S(2)}, u32[]{:S(2)}) collective-permute-start(bf16[256,2048]{1,0:T(8,128)(2,1)} %fusion.28), channel_id=1, source_target_pairs={{0,2},{1,3},{2,0},{3,1},{4,6},{5,7},{6,4},{7,5},{8,10},{9,11},{10,... | collective-permute-start | bytes 3145736 | tf_op jit(solution)/shard_map/ppermute | solution.py:330
  80.1 63.0 %collective-permute-start.3 = (bf16[256,2048]{1,0:T(8,128)(2,1)}, bf16[256,2048]{1,0:T(8,128)(2,1)}, u32[]{:S(2)}, u32[]{:S(2)}) collective-permute-start(bf16[256,2048]{1,0:T(8,128)(2,1)} %fusion.28), channel_id=1, source_target_pairs={{0,3},{1,0},{2,1},{3,2},{4,7},{5,4},{6,5},{7,6},{8,11},{9,8},{10,9... | collective-permute-start | bytes 3145736 | tf_op jit(solution)/shard_map/ppermute | solution.py:330
  154.5 120.3 %all-to-all-start = ((bf16[4,192,2048]{2,1,0:T(8,128)(2,1)}), bf16[4,192,2048]{2,1,0:T(8,128)(2,1)}, u32[]{:S(2)}, u32[]{:S(2)}) async-start(bf16[4,192,2048]{2,1,0:T(8,128)(2,1)} %bitcast.479), calls=%async_computation | async-start | bytes 6291456 | tf_op jit(solution)/shard_map/all_to_all | solution.py:455
  290.6 79.6 %all-to-all-start.1 = ((bf16[4,192,2048]{2,1,0:T(8,128)(2,1)}), bf16[4,192,2048]{2,1,0:T(8,128)(2,1)}, u32[]{:S(2)}, u32[]{:S(2)}) async-start(bf16[4,192,2048]{2,1,0:T(8,128)(2,1)} %bitcast.505), calls=%async_computation.1 | async-start | bytes 6291456 | tf_op jit(solution)/shard_map/all_to_all | solution.py:455
  380.9 75.6 %all-to-all-start.2 = ((bf16[4,192,2048]{2,1,0:T(8,128)(2,1)}), bf16[4,192,2048]{2,1,0:T(8,128)(2,1)S(1)}, u32[]{:S(2)}, u32[]{:S(2)}) async-start(bf16[4,192,2048]{2,1,0:T(8,128)(2,1)} %bitcast.56), calls=%async_computation.2 | async-start | bytes 6291456 | tf_op jit(solution)/shard_map/all_to_all | solution.py:455
  385.7 501.8 %reduce-scatter.4.cloned.1.call-start = ((), (), s32[]{:S(2)}) async-start(), calls=%async_computation.15 | async-start | bytes 18874368 | tf_op jit(solution)/shard_map/reduce_scatter | solution.py:609
  526.2 361.3 %reduce-scatter.6.cloned.1.call-start = ((), (), s32[]{:S(2)}) async-start(), calls=%async_computation.16 | async-start | bytes 18874368 | tf_op jit(solution)/shard_map/reduce_scatter | solution.py:609
  643.7 75.0 %all-to-all-start.3 = ((bf16[4,192,2048]{2,1,0:T(8,128)(2,1)}), bf16[4,192,2048]{2,1,0:T(8,128)(2,1)}, u32[]{:S(2)}, u32[]{:S(2)}) async-start(bf16[4,192,2048]{2,1,0:T(8,128)(2,1)} %bitcast.76), calls=%async_computation.3 | async-start | bytes 6291456 | tf_op jit(solution)/shard_map/all_to_all | solution.py:455
  682.1 109.3 %collective-permute-start.20 = (bf16[2816,1024]{1,0:T(8,128)(2,1)}, bf16[2816,1024]{1,0:T(8,128)(2,1)}, u32[]{:S(2)}, u32[]{:S(2)}) collective-permute-start(bf16[2816,1024]{1,0:T(8,128)(2,1)} %convolution_convert_fusion.5), channel_id=1, source_target_pairs={{0,4},{4,0},{8,12},{12,8},{16,20},{20,16},{24,28},{28,24},{1,5},{5... | collective-permute-start | bytes 17301512 | tf_op jit(solution)/shard_map/ppermute | solution.py:342
  690.1 101.2 %collective-permute-start.21 = (bf16[2816,1024]{1,0:T(8,128)(2,1)}, bf16[2816,1024]{1,0:T(8,128)(2,1)}, u32[]{:S(2)}, u32[]{:S(2)}) collective-permute-start(bf16[2816,1024]{1,0:T(8,128)(2,1)} %convolution_convert_fusion.4), channel_id=1, source_target_pairs={{0,4},{4,0},{8,12},{12,8},{16,20},{20,16},{24,28},{28,24},{1,5},{5... | collective-permute-start | bytes 17301512 | tf_op jit(solution)/shard_map/ppermute | solution.py:342
  752.0 75.1 %all-to-all-start.4 = ((bf16[4,192,2048]{2,1,0:T(8,128)(2,1)}), bf16[4,192,2048]{2,1,0:T(8,128)(2,1)}, u32[]{:S(2)}, u32[]{:S(2)}) async-start(bf16[4,192,2048]{2,1,0:T(8,128)(2,1)} %bitcast.80), calls=%async_computation.4 | async-start | bytes 6291456 | tf_op jit(solution)/shard_map/all_to_all | solution.py:455
  757.0 253.9 %reduce-scatter.8.cloned.1.call-start = ((), (), s32[]{:S(2)}) async-start(), calls=%async_computation.17 | async-start | bytes 14155776 | tf_op jit(solution)/shard_map/reduce_scatter | solution.py:631
  796.3 123.5 %collective-permute-start.25 = (bf16[2,704,1024]{2,1,0:T(8,128)(2,1)}, bf16[2,704,1024]{2,1,0:T(8,128)(2,1)}, u32[]{:S(2)}, u32[]{:S(2)}) collective-permute-start(bf16[2,704,1024]{2,1,0:T(8,128)(2,1)} %fusion.23), channel_id=1, source_target_pairs={{0,16},{4,20},{8,24},{12,28},{16,0},{20,4},{24,8},{28,12},{1,17},{... | collective-permute-start | bytes 8650760 | tf_op jit(solution)/shard_map/ppermute | solution.py:342
  802.5 117.3 %collective-permute-start.24 = (bf16[2,704,1024]{2,1,0:T(8,128)(2,1)}, bf16[2,704,1024]{2,1,0:T(8,128)(2,1)}, u32[]{:S(2)}, u32[]{:S(2)}) collective-permute-start(bf16[2,704,1024]{2,1,0:T(8,128)(2,1)} %fusion.22), channel_id=1, source_target_pairs={{0,8},{4,12},{8,0},{12,4},{16,24},{20,28},{24,16},{28,20},{1,9},{5... | collective-permute-start | bytes 8650760 | tf_op jit(solution)/shard_map/ppermute | solution.py:342
  827.2 92.6 %all-to-all-start.5 = ((bf16[4,192,2048]{2,1,0:T(8,128)(2,1)}), bf16[4,192,2048]{2,1,0:T(8,128)(2,1)S(1)}, u32[]{:S(2)}, u32[]{:S(2)}) async-start(bf16[4,192,2048]{2,1,0:T(8,128)(2,1)} %bitcast.498), calls=%async_computation.5 | async-start | bytes 6291456 | tf_op jit(solution)/shard_map/all_to_all | solution.py:455
  874.5 59.6 %collective-permute-start.23 = (bf16[1024,1024]{1,0:T(8,128)(2,1)}, bf16[1024,1024]{1,0:T(8,128)(2,1)}, u32[]{:S(2)}, u32[]{:S(2)}) collective-permute-start(bf16[1024,1024]{1,0:T(8,128)(2,1)} %convolution_convert_fusion.18), channel_id=1, source_target_pairs={{0,4},{4,0},{8,12},{12,8},{16,20},{20,16},{24,28},{28,24},{1,5},{5... | collective-permute-start | bytes 6291464 | tf_op jit(solution)/shard_map/ppermute | solution.py:342
  925.3 95.9 %collective-permute-start.54 = (bf16[704,1024]{1,0:T(8,128)(2,1)}, bf16[704,1024]{1,0:T(8,128)(2,1)}, u32[]{:S(2)}, u32[]{:S(2)}) collective-permute-start(bf16[704,1024]{1,0:T(8,128)(2,1)} %fusion.36), channel_id=1, source_target_pairs={{0,8},{4,12},{8,0},{12,4},{16,24},{20,28},{24,16},{28,20},{1,9},{5... | collective-permute-start | bytes 4325384 | tf_op jit(solution)/shard_map/ppermute | solution.py:342
  928.9 95.5 %collective-permute-start.53 = (bf16[704,1024]{1,0:T(8,128)(2,1)}, bf16[704,1024]{1,0:T(8,128)(2,1)}, u32[]{:S(2)}, u32[]{:S(2)}) collective-permute-start(bf16[704,1024]{1,0:T(8,128)(2,1)} %fusion.35), channel_id=1, source_target_pairs={{0,16},{4,20},{8,24},{12,28},{16,0},{20,4},{24,8},{28,12},{1,17},{... | collective-permute-start | bytes 4325384 | tf_op jit(solution)/shard_map/ppermute | solution.py:342
  934.1 119.4 %collective-permute-start.31 = (bf16[1024,1024]{1,0:T(8,128)(2,1)}, bf16[1024,1024]{1,0:T(8,128)(2,1)}, u32[]{:S(2)}, u32[]{:S(2)}) collective-permute-start(bf16[1024,1024]{1,0:T(8,128)(2,1)} %convolution_convert_fusion.14), channel_id=1, source_target_pairs={{0,4},{4,0},{8,12},{12,8},{16,20},{20,16},{24,28},{28,24},{1,5},{5... | collective-permute-start | bytes 6291464 | tf_op jit(solution)/shard_map/ppermute | solution.py:342
  960.7 50.1 %collective-permute-start.27 = (bf16[2,256,1024]{2,1,0:T(8,128)(2,1)}, bf16[2,256,1024]{2,1,0:T(8,128)(2,1)}, u32[]{:S(2)}, u32[]{:S(2)}) collective-permute-start(bf16[2,256,1024]{2,1,0:T(8,128)(2,1)} %fusion.46), channel_id=1, source_target_pairs={{0,16},{4,20},{8,24},{12,28},{16,0},{20,4},{24,8},{28,12},{1,17},{... | collective-permute-start | bytes 3145736 | tf_op jit(solution)/shard_map/ppermute | solution.py:342
  1029.4 128.3 %all-to-all-start.6 = ((bf16[4,256,2048]{2,1,0:T(8,128)(2,1)}), bf16[4,256,2048]{2,1,0:T(8,128)(2,1)}, u32[]{:S(2)}, u32[]{:S(2)}) async-start(bf16[4,256,2048]{2,1,0:T(8,128)(2,1)} %bitcast.478), calls=%async_computation.9 | async-start | bytes 8388608 | tf_op jit(solution)/shard_map/all_to_all | solution.py:455
  1034.4 128.2 %all-reduce.3.cloned.1.call-start = ((), (), s32[]{:S(2)}) async-start(), calls=%async_computation.18 | async-start | bytes 2097152 | tf_op jit(solution)/shard_map/psum | solution.py:688
  1085.7 143.0 %all-reduce.5.cloned.1.call-start = ((), (), s32[]{:S(2)}) async-start(), calls=%async_computation.19 | async-start | bytes 2097152 | tf_op jit(solution)/shard_map/psum | solution.py:703
  1115.4 50.0 %collective-permute-start.39 = (bf16[1024,1024]{1,0:T(8,128)(2,1)}, bf16[1024,1024]{1,0:T(8,128)(2,1)}, u32[]{:S(2)}, u32[]{:S(2)}) collective-permute-start(bf16[1024,1024]{1,0:T(8,128)(2,1)} %convolution_convert_fusion.22), channel_id=1, source_target_pairs={{0,4},{4,0},{8,12},{12,8},{16,20},{20,16},{24,28},{28,24},{1,5},{5... | collective-permute-start | bytes 6291464 | tf_op jit(solution)/shard_map/ppermute | solution.py:342
  1122.5 53.8 %collective-permute-start.41 = (bf16[2,256,1024]{2,1,0:T(8,128)(2,1)}, bf16[2,256,1024]{2,1,0:T(8,128)(2,1)}, u32[]{:S(2)}, u32[]{:S(2)}) collective-permute-start(bf16[2,256,1024]{2,1,0:T(8,128)(2,1)} %fusion.50), channel_id=1, source_target_pairs={{0,16},{4,20},{8,24},{12,28},{16,0},{20,4},{24,8},{28,12},{1,17},{... | collective-permute-start | bytes 3145736 | tf_op jit(solution)/shard_map/ppermute | solution.py:342
  1123.2 53.1 %collective-permute-start.40 = (bf16[2,256,1024]{2,1,0:T(8,128)(2,1)}, bf16[2,256,1024]{2,1,0:T(8,128)(2,1)}, u32[]{:S(2)}, u32[]{:S(2)}) collective-permute-start(bf16[2,256,1024]{2,1,0:T(8,128)(2,1)} %fusion.49), channel_id=1, source_target_pairs={{0,8},{4,12},{8,0},{12,4},{16,24},{20,28},{24,16},{28,20},{1,9},{5... | collective-permute-start | bytes 3145736 | tf_op jit(solution)/shard_map/ppermute | solution.py:342
  (189 other events, 2768.8 us)
Sparse Core Ops, SparseCore 0:
  11.2 120.2 all-gather.5
  133.9 111.4 all-gather.7
  247.9 116.4 all-gather.9
  366.7 89.8 all-gather.11
  458.3 72.1 all-gather.13
  533.9 115.9 reduce-scatter.3
  653.5 115.9 reduce-scatter.5
  773.0 142.9 reduce-scatter.7
  1085.8 76.7 all-reduce.2
  1176.4 50.0 all-reduce.4

commit v2 on v1

--- a/solution.py
+++ b/solution.py
@@ -94,8 +94,8 @@
         grid=(HEADS,),
         in_specs=[
             pl.BlockSpec((rows, HEAD_DIM), lambda h: (0, h)),
-            pl.BlockSpec((seq, HEAD_DIM), lambda h: (0, h)),
-            pl.BlockSpec((seq, HEAD_DIM), lambda h: (0, h + HEADS)),
+            pl.BlockSpec((seq, HEAD_DIM), lambda h: (0, 2 * h)),
+            pl.BlockSpec((seq, HEAD_DIM), lambda h: (0, 2 * h + 1)),
             pl.BlockSpec((rows, 2), lambda h: (0, 0)),
         ],
         out_specs=[
@@ -126,8 +126,7 @@
     bounds_ref,
     logsum_ref,
     grad_query_ref,
-    grad_key_ref,
-    grad_value_ref,
+    grad_both_ref,
     key_total,
     value_total,
 ):
@@ -163,8 +162,8 @@
         else:
             key_total[:span, :] += key_part
             value_total[:span, :] += value_part
-    grad_key_ref[...] = (key_total[...] * scaling).astype(BF16)
-    grad_value_ref[...] = value_total[...].astype(BF16)
+    grad_both_ref[:, :HEAD_DIM] = (key_total[...] * scaling).astype(BF16)
+    grad_both_ref[:, HEAD_DIM:] = value_total[...].astype(BF16)
 
 
 def attend_backward(queries, keys_values, grads, bounds, logsums, sources, start, heads):
@@ -177,21 +176,19 @@
         grid=(heads,),
         in_specs=[
             pl.BlockSpec((rows, HEAD_DIM), lambda h: (0, h + start)),
-            pl.BlockSpec((seq, HEAD_DIM), lambda h: (0, h + start)),
-            pl.BlockSpec((seq, HEAD_DIM), lambda h: (0, h + start + HEADS)),
+            pl.BlockSpec((seq, HEAD_DIM), lambda h: (0, 2 * (h + start))),
+            pl.BlockSpec((seq, HEAD_DIM), lambda h: (0, 2 * (h + start) + 1)),
             pl.BlockSpec((rows, HEAD_DIM), lambda h: (0, h + start)),
             pl.BlockSpec((rows, 2), lambda h: (0, 0)),
             pl.BlockSpec((rows, 128), lambda h: (0, 0)),
         ],
         out_specs=[
             pl.BlockSpec((rows, HEAD_DIM), lambda h: (0, h)),
-            pl.BlockSpec((seq, HEAD_DIM), lambda h: (0, h)),
-            pl.BlockSpec((seq, HEAD_DIM), lambda h: (0, h)),
+            pl.BlockSpec((seq, 2 * HEAD_DIM), lambda h: (0, h)),
         ],
         out_shape=[
             jax.ShapeDtypeStruct((rows, features), BF16),
-            jax.ShapeDtypeStruct((seq, features), BF16),
-            jax.ShapeDtypeStruct((seq, features), BF16),
+            jax.ShapeDtypeStruct((seq, 2 * features), BF16),
         ],
         scratch_shapes=[pltpu.VMEM((seq, HEAD_DIM), F32), pltpu.VMEM((seq, HEAD_DIM), F32)],
         compiler_params=pltpu.CompilerParams(vmem_limit_bytes=VMEM_BYTES),
@@ -257,31 +254,33 @@
     )(inputs, grads, gate_up, down)
 
 
-def assemble_kernel(tiles, per_chunk, *refs):
+def assemble_kernel(starts, *refs):
     out_ref = refs[-1]
-    chunk = lax.rem(pl.program_id(0), tiles) // per_chunk
+    tile = lax.rem(pl.program_id(0), starts[-1])
     for index, ref in enumerate(refs[:-1]):
 
-        @pl.when(chunk == index)
+        @pl.when((tile >= starts[index]) & (tile < starts[index + 1]))
         def _():
             out_ref[...] = ref[...].astype(F32)
 
 
-def assemble(chunks, per_chunk):
+def assemble(chunks):
     rows = chunks[0].shape[0]
-    tiles = sum(chunk.shape[1] for chunk in chunks) // (2 * TILE)
+    starts = [0]
+    for chunk in chunks:
+        starts.append(starts[-1] + chunk.shape[1] // (2 * TILE))
+    tiles = starts[-1]
 
     def place(index):
-        count = chunks[index].shape[1] // (2 * TILE)
+        last = starts[index + 1] - starts[index] - 1
 
         def block(j):
-            tile = j % tiles - index * per_chunk
-            return (0, jnp.clip(tile, 0, count - 1) * 2 + j // tiles)
+            return (0, jnp.clip(j % tiles - starts[index], 0, last) * 2 + j // tiles)
 
         return block
 
     return pl.pallas_call(
-        functools.partial(assemble_kernel, tiles, per_chunk),
+        functools.partial(assemble_kernel, starts),
         grid=(2 * tiles,),
         in_specs=[pl.BlockSpec((rows, TILE), place(index)) for index in range(len(chunks))],
         out_specs=pl.BlockSpec((rows, TILE), lambda j: (0, j)),
@@ -294,26 +293,26 @@
 
 
 def transpose_kernel(each, first_ref, second_ref, out_ref):
-    second = lax.rem(lax.div(pl.program_id(0), each), 2)
-
-    @pl.when(second == 0)
+    head = lax.rem(pl.program_id(0), 2 * each)
+
+    @pl.when(head < each)
     def _():
         out_ref[...] = first_ref[...].astype(F32).T
 
-    @pl.when(second == 1)
+    @pl.when(head >= each)
     def _():
         out_ref[...] = second_ref[...].astype(F32).T
 
 
 def transpose(first, second):
     rows, columns = first.shape
-    each = columns // 2 // TILE
-    spec = pl.BlockSpec((rows, TILE), lambda j: (0, j // (2 * each) * each + j % each))
+    each = columns // (2 * HEAD_DIM)
+    spec = pl.BlockSpec((rows, HEAD_DIM), lambda j: (0, j % each * 2 + j // (2 * each)))
     return pl.pallas_call(
         functools.partial(transpose_kernel, each),
         grid=(4 * each,),
         in_specs=[spec, spec],
-        out_specs=pl.BlockSpec((TILE, rows), lambda j: (j, 0)),
+        out_specs=pl.BlockSpec((HEAD_DIM, rows), lambda j: (j, 0)),
         out_shape=jax.ShapeDtypeStruct((2 * columns, rows), F32),
         cost_estimate=pl.CostEstimate(
             flops=0, bytes_accessed=12 * rows * columns, transcendentals=0
@@ -322,15 +321,284 @@
     )(first, second)
 
 
-def rotate_gather(block, axis):
-    size = lax.axis_size(axis)
-    me = lax.axis_index(axis)
-    parts = [block]
-    for shift in range(1, size):
-        parts.append(lax.ppermute(block, axis, [(i, (i + shift) % size) for i in range(size)]))
-    stacked = jnp.stack(parts[::-1])
-    doubled = jnp.concatenate([stacked, stacked])
-    return lax.dynamic_slice_in_dim(doubled, size - 1 - me, size, 0)
+MESH = pl.DeviceIdType.MESH
+
+
+def greet(devices, extra=0):
+    barrier = pltpu.get_barrier_semaphore()
+    for device in devices:
+        pl.semaphore_signal(barrier, inc=1, device_id=device, device_id_type=MESH)
+    return barrier
+
+
+class WeightGather:
+    def __init__(self, bits, shard_ref, full_ref, sent, got):
+        self.me, self.place = lax.axis_index("grp"), lax.axis_index("ep")
+        self.bits, self.rows = bits, shard_ref.shape[0] // 2
+        self.shard_ref, self.full_ref, self.sent, self.got = shard_ref, full_ref, sent, got
+        self.orders = list(range(1, bits)) + [0], list(range(1, bits))[::-1] + [0]
+        self.moves = []
+        for index in range(1, 1 << (bits - 1)):
+            for part in range(2):
+                order = self.orders[part]
+                far = sum(1 << bit for at, bit in enumerate(order[:-1]) if index >> at & 1)
+                self.moves.append((part, far, order[index.bit_length() :]))
+
+    def neighbours(self):
+        return [(self.me ^ (1 << bit), self.place) for bit in range(self.bits)]
+
+    def piece(self, part, far, bit):
+        here = pl.ds(part * self.rows, self.rows)
+        block = self.full_ref.at[self.me ^ far, here]
+        return pltpu.make_async_remote_copy(
+            src_ref=self.shard_ref.at[here] if far == 0 else block,
+            dst_ref=block,
+            send_sem=self.sent.at[part, far, bit],
+            recv_sem=self.got.at[part, far ^ (1 << bit)],
+            device_id=(self.me ^ (1 << bit), self.place),
+            device_id_type=MESH,
+        )
+
+    def wait_piece(self, part, far):
+        block = self.full_ref.at[self.me ^ far, pl.ds(part * self.rows, self.rows)]
+        pltpu.make_async_remote_copy(
+            src_ref=block,
+            dst_ref=block,
+            send_sem=self.sent.at[part, far, 0],
+            recv_sem=self.got.at[part, far],
+            device_id=(self.me ^ 1, self.place),
+            device_id_type=MESH,
+        ).wait_recv()
+
+    def first(self):
+        for part in range(2):
+            for bit in self.orders[part]:
+                self.piece(part, 0, bit).start()
+
+    def forward(self, part, far, later):
+        self.wait_piece(part, far)
+        for bit in later:
+            self.piece(part, far, bit).start()
+
+    def finish(self):
+        for part in range(2):
+            for far in range(1 << (self.bits - 1)):
+                self.wait_piece(part, 2 * far + 1)
+        for part in range(2):
+            for bit in self.orders[part]:
+                self.piece(part, 0, bit).wait_send()
+        for part, far, later in self.moves:
+            for bit in later:
+                self.piece(part, far, bit).wait_send()
+
+
+def weight_gather_semaphores(groups):
+    bits = groups.bit_length() - 1
+    return [pltpu.SemaphoreType.DMA((2, groups, bits)), pltpu.SemaphoreType.DMA((2, groups))]
+
+
+def opening_kernel(bits, count, chunks, *refs):
+    (tokens_ref, shard_ref, gate_up_ref, down_ref, all_ref, full_ref), refs = refs[:6], refs[6:]
+    low_refs, refs = refs[:chunks], refs[chunks:]
+    down_low_ref, local, up_send, up_got, down_send, down_got, sent, got = refs
+    me = lax.axis_index("grp")
+    place = lax.axis_index("ep")
+    weights = WeightGather(bits, shard_ref, full_ref, sent, got)
+
+    barrier = greet(weights.neighbours())
+
+    @pl.when(place > 0)
+    def _():
+        pl.semaphore_signal(barrier, inc=1, device_id=(me, place - 1), device_id_type=MESH)
+
+    @pl.when(place < count - 1)
+    def _():
+        pl.semaphore_signal(barrier, inc=1, device_id=(me, place + 1), device_id_type=MESH)
+
+    ends = jnp.where(place > 0, 1, 0) + jnp.where(place < count - 1, 1, 0)
+    pl.semaphore_wait(barrier, bits + ends)
+
+    def upward(hop):
+        block = all_ref.at[jnp.maximum(place - hop, 0)]
+        return pltpu.make_async_remote_copy(
+            src_ref=tokens_ref if hop == 0 else block,
+            dst_ref=block,
+            send_sem=up_send.at[hop],
+            recv_sem=up_got.at[hop],
+            device_id=(me, jnp.minimum(place + 1, count - 1)),
+            device_id_type=MESH,
+        )
+
+    def downward(hop):
+        block = all_ref.at[jnp.minimum(place + hop, count - 1)]
+        return pltpu.make_async_remote_copy(
+            src_ref=tokens_ref if hop == 0 else block,
+            dst_ref=block,
+            send_sem=down_send.at[hop],
+            recv_sem=down_got.at[hop],
+            device_id=(me, jnp.maximum(place - 1, 0)),
+            device_id_type=MESH,
+        )
+
+    def lines(hop, act):
+        @pl.when((place + 1 < count) & (place - hop >= 0))
+        def _():
+            act(upward(hop))
+
+        @pl.when((place - 1 >= 0) & (place + hop < count))
+        def _():
+            act(downward(hop))
+
+    def line_got(hop):
+        @pl.when(place - hop - 1 >= 0)
+        def _():
+            upward(hop).wait_recv()
+
+        @pl.when(place + hop + 1 < count)
+        def _():
+            downward(hop).wait_recv()
+
+    lines(0, lambda copy: copy.start())
+    weights.first()
+    own = [
+        pltpu.make_async_copy(tokens_ref, all_ref.at[place], local.at[0]),
+        pltpu.make_async_copy(shard_ref, full_ref.at[me], local.at[1]),
+    ]
+    for copy in own:
+        copy.start()
+
+    def round_block(in_ref, out_ref):
+        out_ref[...] = in_ref[...].astype(BF16)
+
+    shard_rows, columns = gate_up_ref.shape
+    tiles = columns // (2 * TILE)
+    start = 0
+    for low_ref in low_refs:
+        blocks = low_ref.shape[1] // TILE
+        pltpu.emit_pipeline(
+            round_block,
+            grid=(blocks,),
+            in_specs=[
+                pl.BlockSpec(
+                    (shard_rows, TILE), lambda j, start=start: (0, start + j // 2 + j % 2 * tiles)
+                )
+            ],
+            out_specs=[pl.BlockSpec((shard_rows, TILE), lambda j: (0, j))],
+        )(gate_up_ref, low_ref)
+        start += blocks // 2
+    down_rows, width = down_ref.shape
+    step = 176
+    pltpu.emit_pipeline(
+        round_block,
+        grid=(down_rows // step,),
+        in_specs=[pl.BlockSpec((step, width), lambda j: (j, 0))],
+        out_specs=[pl.BlockSpec((step, width), lambda j: (j, 0))],
+    )(down_ref, down_low_ref)
+
+    coming = list(weights.moves)
+    hops = list(range(count - 1))
+    while hops or coming:
+        if hops:
+            hop = hops.pop(0)
+            line_got(hop)
+            if hop + 1 < count - 1:
+                lines(hop + 1, lambda copy: copy.start())
+        for move in coming[:4]:
+            weights.forward(*move)
+        coming = coming[4:]
+    weights.finish()
+    for hop in range(count - 1):
+        lines(hop, lambda copy: copy.wait_send())
+    for copy in own:
+        copy.wait()
+
+
+def opening(tokens, shard, gate_up, down, cuts):
+    groups, count = lax.axis_size("grp"), lax.axis_size("ep")
+    bits = groups.bit_length() - 1
+    whole, full, *lows = pl.pallas_call(
+        functools.partial(opening_kernel, bits, count, len(cuts)),
+        in_specs=[pl.BlockSpec(memory_space=pl.ANY)] * 4,
+        out_specs=[pl.BlockSpec(memory_space=pl.ANY)] * (3 + len(cuts)),
+        out_shape=[
+            jax.ShapeDtypeStruct((count, *tokens.shape), BF16),
+            jax.ShapeDtypeStruct((groups, *shard.shape), BF16),
+            *[jax.ShapeDtypeStruct((gate_up.shape[0], 2 * size), BF16) for _, size in cuts],
+            jax.ShapeDtypeStruct(down.shape, BF16),
+        ],
+        scratch_shapes=[
+            pltpu.SemaphoreType.DMA((2,)),
+            *[pltpu.SemaphoreType.DMA((count - 1,))] * 4,
+            *weight_gather_semaphores(groups),
+        ],
+        compiler_params=pltpu.CompilerParams(
+            collective_id=0, has_side_effects=True, vmem_limit_bytes=VMEM_BYTES
+        ),
+        name="opening",
+    )(tokens, shard, gate_up, down)
+    return whole, full.reshape(-1, full.shape[2]), lows[:-1], lows[-1]
+
+
+def exchange_kernel(
+    bits, count, values_ref, shard_ref, back_ref, full_ref, local, out_sent, out_got, sent, got
+):
+    me = lax.axis_index("grp")
+    place = lax.axis_index("ep")
+    weights = WeightGather(bits, shard_ref, full_ref, sent, got)
+    others = [lax.rem(place + shift, count) for shift in range(1, count)]
+    barrier = greet(weights.neighbours() + [(me, other) for other in others])
+    pl.semaphore_wait(barrier, bits + count - 1)
+    copies = [
+        pltpu.make_async_remote_copy(
+            src_ref=values_ref.at[other],
+            dst_ref=back_ref.at[place],
+            send_sem=out_sent.at[index],
+            recv_sem=out_got.at[index],
+            device_id=(me, other),
+            device_id_type=MESH,
+        )
+        for index, other in enumerate(others)
+    ]
+    own = [
+        pltpu.make_async_copy(values_ref.at[place], back_ref.at[place], local.at[0]),
+        pltpu.make_async_copy(shard_ref, full_ref.at[me], local.at[1]),
+    ]
+    for copy in copies:
+        copy.start()
+    weights.first()
+    for copy in own:
+        copy.start()
+    for move in weights.moves:
+        weights.forward(*move)
+    weights.finish()
+    for copy in copies:
+        copy.wait()
+    for copy in own:
+        copy.wait()
+
+
+def exchange_and_gather(values, shard, collective_id):
+    groups, count = lax.axis_size("grp"), lax.axis_size("ep")
+    bits = groups.bit_length() - 1
+    rows, width = values.shape
+    shape = (count, rows // count, width)
+    back, full = pl.pallas_call(
+        functools.partial(exchange_kernel, bits, count),
+        in_specs=[pl.BlockSpec(memory_space=pl.ANY)] * 2,
+        out_specs=[pl.BlockSpec(memory_space=pl.ANY)] * 2,
+        out_shape=[
+            jax.ShapeDtypeStruct(shape, BF16),
+            jax.ShapeDtypeStruct((groups, *shard.shape), BF16),
+        ],
+        scratch_shapes=[
+            pltpu.SemaphoreType.DMA((2,)),
+            *[pltpu.SemaphoreType.DMA((count - 1,))] * 2,
+            *weight_gather_semaphores(groups),
+        ],
+        compiler_params=pltpu.CompilerParams(collective_id=collective_id, has_side_effects=True),
+        name="exchange_and_gather",
+    )(values.reshape(shape), shard)
+    return back.reshape(rows, width), full.reshape(-1, full.shape[2])
 
 
 def after(values, *tokens):
@@ -340,34 +608,6 @@
 def flip(values, bit):
     size = lax.axis_size("grp")
     return lax.ppermute(values, "grp", [(i, i ^ (1 << bit)) for i in range(size)])
-
-
-class Gather:
-    def __init__(self, shards, orders):
-        self.pieces = [{0: shard} for shard in shards]
-        self.orders = [list(order) for order in orders]
-
-    def step(self, *tokens):
-        for pieces, order in zip(self.pieces, self.orders):
-            bit = order.pop(0)
-            for place, piece in list(pieces.items()):
-                if tokens:
-                    piece = after(piece, *tokens)
-                pieces[place ^ (1 << bit)] = flip(piece, bit)
-
-    def finish(self, *tokens):
-        size = lax.axis_size("grp")
-        me = lax.axis_index("grp")
-        rows = [pieces[0].shape[0] for pieces in self.pieces]
-        whole = jnp.zeros((size, sum(rows), self.pieces[0][0].shape[1]), BF16)
-        offset = 0
-        for pieces, count in zip(self.pieces, rows):
-            for place, piece in pieces.items():
-                if tokens:
-                    piece = after(piece, *tokens)
-                whole = lax.dynamic_update_slice(whole, piece[None], (me ^ place, offset, 0))
-            offset += count
-        return whole.reshape(size * sum(rows), -1)
 
 
 def gather_gains(gains):
@@ -495,41 +735,28 @@
     xfloat = layer_input.astype(F32)
     inverse_one, unit_one = normalize(xfloat)
     normed_one = (unit_one * gain_one).astype(BF16)
-    normed_all = rotate_gather(normed_one, "ep")
-
-    orders = list(range(1, bits)) + [0], list(range(1, bits))[::-1] + [0]
-    kv_shard = kv_weight.T.astype(BF16)
-    query_shard = after(query_maps[0], normed_one).astype(BF16)
-    output_shard = after(output_maps[0], query_shard).astype(BF16)
+
+    kv_heads = kv_weight.reshape(2, HEADS, HEAD_DIM, -1).transpose(1, 0, 2, 3)
+    kv_shard = kv_heads.reshape(kv_weight.shape).T.astype(BF16)
+    cuts = []
+    for count in (4, 2, 2, hidden // TILE - 8):
+        cuts.append((sum(size for _, size in cuts), count * TILE))
+
+    def gather(shard):
+        return lax.all_gather(shard, "grp", axis=0, tiled=True)
+
+    output_shard = output_maps[0].astype(BF16)
     kv_full = gather(kv_shard)
-    query_gather = Gather([query_shard], orders[:1])
-    output_gather = Gather([output_shard], orders[1:])
-    query_gather.step()
-    output_gather.step()
-    units = TILE * 4
-    cuts = [(start, min(units, hidden - start)) for start in range(0, hidden, units)]
-
-    def tiles_of(start, size):
-        return [
-            slice(at, at + TILE)
-            for tile in range(start, start + size, TILE)
-            for at in (tile, hidden + tile)
-        ]
-
-    gate_up_full = []
-    shard = output_shard
-    for index, cut in enumerate(cuts):
-        maps = after(gate_up_maps, shard)
-        shard = jnp.concatenate([maps[0, :, here] for here in tiles_of(*cut)], axis=1).astype(BF16)
-        gate_up_full.append(gather(shard))
-        if index == 0:
-            query_gather.step(shard)
-            output_gather.step(shard)
-            shard = after(down_maps[0], shard).astype(BF16)
-            down_full = gather(shard)
-    while query_gather.orders[0]:
-        query_gather.step(normed_all)
-        output_gather.step(normed_all)
+    output_full = gather(output_shard)
+    normed_all, query_full, gate_up_low, down_low = opening(
+        after(normed_one, output_shard),
+        query_maps[0].astype(BF16),
+        gate_up_maps[0],
+        down_maps[0],
+        cuts,
+    )
+    down_full = gather(down_low)
+    gate_up_full = [gather(gate_up_low[0]), None, None, gather(gate_up_low[3])]
 
     att_named, att_place = expert_places(att_routes[0].reshape(experts, tok_dev, TOP), experts)
     mlp_named, mlp_place = expert_places(mlp_routes[0].reshape(experts, tok_dev, TOP), experts)
@@ -579,13 +806,11 @@
         .reshape(rows_total, model_width)
     )
     normed_all = normed_all.reshape(experts * tok_dev, model_width)
-    keys_values = dot(after(normed_all, att_in), kv_full).astype(BF16)
-    query_full = query_gather.finish(keys_values)
-    queries = dot(after(att_in, keys_values), query_full).astype(BF16)
-    output_full = output_gather.finish(queries)
+    queries = dot(att_in, query_full).astype(BF16)
+    keys_values = dot(after(normed_all, queries), kv_full).astype(BF16)
     att_heads, logsums = attend_forward(queries, keys_values, bounds, experts)
     att_rows = dot(after(att_heads, grad_mlp_rows), output_full).astype(BF16)
-    att_back = exchange(att_rows, experts)
+    att_back, gate_up_full[1] = exchange_and_gather(att_rows, gate_up_low[1], 1)
     residual_one = (
         xfloat + dot(att_high, att_back, CONTRACT_ROWS) + dot(att_low, att_back, CONTRACT_ROWS)
     )
@@ -593,28 +818,42 @@
     inverse_two, unit_two = normalize(residual_one)
     normed_two = (unit_two * gain_two).astype(BF16)
     mlp_given = dot(mlp_send, normed_two).astype(BF16)
-    mlp_in = exchange(mlp_given, experts)
-    grad_mlp_in = 0.0
-    acts, weight_grads = [], []
-    feed_in = mlp_in
-    for (start, size), gate_up in zip(cuts, gate_up_full):
-        act, grad_gate_up = feed(feed_in, grad_mlp_rows, gate_up, down_full, start)
-        grad_mlp_in = grad_mlp_in + dot(grad_gate_up, gate_up, CONTRACT_COLUMNS)
-        acts.append(act)
-        if start + size == hidden:
-            grad_mlp_in = grad_mlp_in.astype(BF16)
-            break
-        weight_grad = dot(mlp_in, after(grad_gate_up, grad_mlp_in), CONTRACT_ROWS).astype(BF16)
-        weight_grads.append(
-            lax.psum_scatter(weight_grad, "grp", scatter_dimension=0, tiled=True)
+    mlp_in, gate_up_full[2] = exchange_and_gather(mlp_given, gate_up_low[2], 2)
+    mlp_split = core_split(mlp_in, groups)
+    acts = [None] * len(cuts)
+    grads = [None] * len(cuts)
+
+    def feed_chunk(index, feed_in, total):
+        gate_up = gate_up_full[index]
+        acts[index], grads[index] = feed(
+            feed_in, grad_mlp_rows, gate_up, down_full, cuts[index][0]
         )
-        feed_in = after(mlp_in, weight_grad)
+        return total + dot(grads[index], gate_up, CONTRACT_COLUMNS)
+
+    grad_mlp_in = feed_chunk(1, mlp_in, 0.0)
+    grad_mlp_in = feed_chunk(2, after(mlp_in, grad_mlp_in), grad_mlp_in)
+    middle_scatter = scatter_product(mlp_split, [after(grads[1], grad_mlp_in), grads[2]], groups)
+    ready = [scatter.terms[0] for scatter in middle_scatter]
+    grad_mlp_in = feed_chunk(0, after(mlp_in, *ready), grad_mlp_in)
+    steps(middle_scatter, grad_mlp_in)
+    first_grad = dot(
+        mlp_in,
+        after(grads[0], grad_mlp_in, *[scatter.sent for scatter in middle_scatter]),
+        CONTRACT_ROWS,
+    ).astype(BF16)
+    first_grad_sum = lax.psum_scatter(first_grad, "grp", scatter_dimension=0, tiled=True)
+    grad_mlp_in = feed_chunk(3, after(mlp_in, first_grad), grad_mlp_in).astype(BF16)
+
     activated = after(jnp.concatenate(acts, axis=1), grad_mlp_in)
-    down_scatter = scatter_product(core_split(activated, groups), halves(grad_mlp_rows), groups)
+    mlp_rows = dot(activated, down_full).astype(BF16)
+    last_grad = dot(mlp_in, after(grads[3], mlp_rows), CONTRACT_ROWS).astype(BF16)
+    last_grad_sum = lax.psum_scatter(last_grad, "grp", scatter_dimension=0, tiled=True)
+    steps(middle_scatter, last_grad)
     mlp_returned = after(
         exchange(grad_mlp_in, experts),
-        *[scatter.terms[0] for scatter in down_scatter],
-        *[scatter.sent for scatter in down_scatter],
+        mlp_rows,
+        last_grad,
+        *[scatter.sent for scatter in middle_scatter],
     )
 
     grad_final = cotangent.astype(F32)
@@ -626,28 +865,22 @@
     sent_four = (
         dot(att_high, res_high) + dot(att_low, res_high) + dot(att_high, res_low)
     ).astype(BF16)
-    mlp_rows = dot(after(activated, sent_four), down_full).astype(BF16)
-    weight_grad = dot(mlp_in, after(grad_gate_up, mlp_rows), CONTRACT_ROWS).astype(BF16)
-    weight_grads.append(lax.psum_scatter(weight_grad, "grp", scatter_dimension=0, tiled=True))
-    steps(down_scatter, mlp_rows)
-    grad_att_rows = after(
-        exchange(sent_four, experts),
-        mlp_rows,
-        weight_grad,
-        *[scatter.sent for scatter in down_scatter],
-    )
+    down_grad = dot(after(activated, sent_four), grad_mlp_rows, CONTRACT_ROWS).astype(BF16)
+    down_grad_sum = lax.psum_scatter(down_grad, "grp", scatter_dimension=0, tiled=True)
+    grad_att_rows = after(exchange(sent_four, experts), down_grad)
     mlp_back = exchange(after(mlp_rows, grad_att_rows), experts)
     grad_heads = dot(grad_att_rows, output_full, CONTRACT_COLUMNS).astype(BF16)
     normed_split = core_split(normed_all, groups)
     att_split = core_split(att_in, groups)
+    normed_split = core_split(normed_all, groups)
+    att_split = core_split(att_in, groups)
     half = HEADS // 2
-    grad_one, keys_one, values_one = attend_backward(
+    grad_one, both_one = attend_backward(
         queries, keys_values, grad_heads, bounds, logsums, experts, 0, half
     )
-    keys_one = after(keys_one, weight_grads[0], weight_grads[1])
-    kv_one = scatter_product(normed_split, [keys_one, values_one], groups)
-    grad_two, keys_two, values_two = attend_backward(
-        after(queries, *[scatter.terms[0] for scatter in kv_one]),
+    both_one = after(both_one, first_grad_sum)
+    grad_two, both_two = attend_backward(
+        after(queries, both_one),
         keys_values,
         grad_heads,
         bounds,
@@ -656,17 +889,13 @@
         half,
         HEADS - half,
     )
-    keys_two = after(keys_two, mlp_back)
-    steps(down_scatter, keys_two)
-    steps(kv_one, keys_two)
-    ready = [scatter.sent for scatter in kv_one + down_scatter]
+    both_two = after(both_two, mlp_back, last_grad_sum)
     query_one, query_two = halves(query_full)
+    kv_full_one, kv_full_two = halves(kv_full)
     grad_att_in = (
-        dot(after(grad_one, *ready), query_one, CONTRACT_COLUMNS)
+        dot(after(grad_one, both_two), query_one, CONTRACT_COLUMNS)
         + dot(grad_two, query_two, CONTRACT_COLUMNS)
     ).astype(BF16)
-    features = HEADS * HEAD_DIM
-    middle = half * HEAD_DIM
     grad_all = (
         jnp.einsum(
             "sct,scd->std",
@@ -674,24 +903,25 @@
             grad_att_in.reshape(experts, capacity, model_width),
             preferred_element_type=F32,
         ).reshape(experts * tok_dev, model_width)
-        + dot(keys_one, kv_full[:, :middle], CONTRACT_COLUMNS)
-        + dot(keys_two, kv_full[:, middle:features], CONTRACT_COLUMNS)
-        + dot(values_one, kv_full[:, features : features + middle], CONTRACT_COLUMNS)
-        + dot(values_two, kv_full[:, features + middle :], CONTRACT_COLUMNS)
+        + dot(both_one, kv_full_one, CONTRACT_COLUMNS)
+        + dot(both_two, kv_full_two, CONTRACT_COLUMNS)
     ).astype(BF16)
     grad_back = exchange(grad_all, experts)
-    steps(kv_one, grad_all, weight_grads[-1])
+    kv_one = scatter_product(normed_split, halves(after(both_one, grad_all)), groups)
+    ready = [scatter.terms[0] for scatter in kv_one]
+    steps(kv_one, *ready)
     ready = [scatter.sent for scatter in kv_one]
-    kv_two = scatter_product(normed_split, [after(keys_two, *ready), values_two], groups)
+    kv_two = scatter_product(normed_split, halves(after(both_two, *ready)), groups)
     ready = [scatter.terms[0] for scatter in kv_two]
-    part_one = after(finish(kv_one), *ready).astype(BF16)
-    kv_grad_one = lax.psum(part_one, "ep")
-    steps(kv_two, part_one)
+    steps(kv_one, *ready)
+    steps(kv_two, *[scatter.sent for scatter in kv_one])
     ready = [scatter.sent for scatter in kv_two]
     query_scatter = scatter_product(att_split, [after(grad_one, *ready)], groups)
     query_scatter += scatter_product(att_split, [after(grad_two, *ready)], groups, 1)
     ready = [scatter.terms[0] for scatter in query_scatter]
-    steps(kv_two, *ready)
+    part_one = after(finish(kv_one), *ready, down_grad_sum).astype(BF16)
+    kv_grad_one = lax.psum(part_one, "ep")
+    steps(kv_two, part_one)
     ready = [scatter.sent for scatter in kv_two]
     steps(query_scatter, *ready)
     ready = [scatter.sent for scatter in query_scatter]
@@ -703,13 +933,16 @@
     kv_grad_two = lax.psum(after(part_two, kv_grad_one), "ep")
     steps(output_scatter, part_two)
     ready = [scatter.sent for scatter in output_scatter]
-    down_grad = finish(down_scatter)[None]
     mlp_back = after(mlp_back, *ready)
     output = (
         residual_one + dot(mlp_high, mlp_back, CONTRACT_ROWS) + dot(mlp_low, mlp_back, CONTRACT_ROWS)
     ).astype(BF16)
     steps(query_scatter, output)
-    weight_grads = [after(part, output) for part in weight_grads]
+    weight_grads = [
+        after(part, output)
+        for part in (first_grad_sum, *[scatter.finish() for scatter in middle_scatter], last_grad_sum)
+    ]
+    down_grad = after(down_grad_sum, output).astype(F32)[None]
     ready = [scatter.sent for scatter in query_scatter]
     steps(output_scatter, *ready)
     ready = [scatter.sent for scatter in output_scatter]
@@ -719,7 +952,7 @@
     query_grad = finish(query_scatter)[None]
     output_grad = finish(output_scatter)[None]
     kv_grad = transpose(kv_grad_one, kv_grad_two)
-    gate_up_grad = assemble(weight_grads, units // TILE)[None]
+    gate_up_grad = assemble(weight_grads)[None]
     grad_inner_one, grad_gain_one = norm_backward(grad_normed_one, unit_one, inverse_one, gain_one)
     grad_input = grad_residual + grad_inner_one
 

time: 1250 us -> 1220 us (0.976)
  Pallas kernels: 195 us -> 435 us
  waiting for transfers between devices: 275 us -> 123 us
  local copies, waits for them, and re-layouts: 126 us -> 50.4 us
  blocking collectives: 0 us -> 74.9 us
  starting transfers between devices: 104 us -> 53.8 us
  other arithmetic: 138 us -> 94.8 us
  matrix products: 394 us -> 363 us
    pallas_call x1 -> x4, Pallas kernels: 15.2 us -> 240 us  [the longest x2 150 us: exchange_and_gather(): pl.pallas_call(functools.partial(exchange_kernel, bits, count), in_specs=...]
    all_to_all x7 -> x4, waiting for transfers between devices: 189 us -> 0.01 us  [exchange(): lax.all_to_all(values.reshape(experts, rows // experts, width), 'ep', spl...]
    all_to_all x0 -> x1, blocking collectives: none -> 74.9 us  [exchange(): lax.all_to_all(values.reshape(experts, rows // experts, width), 'ep', spl...]
    ppermute x47 -> x33, waiting for transfers between devices: 54.6 us -> 95.5 us  [flip(): return lax.ppermute(values, 'grp', [(i, i ^ 1 << bit) for i in range(size)])]
    all_to_all x7 -> x4, starting transfers between devices: 57.9 us -> 17.4 us  [exchange(): lax.all_to_all(values.reshape(experts, rows // experts, width), 'ep', spl...]
    unnamed x326 -> x237, local copies, waits for them, and re-layouts: 37.6 us -> 11 us
    dot_general x48 -> x47, matrix products: 384 us -> 358 us  [dot(): return lax.dot_general(left, right, dims, preferred_element_type=F32)]
    ppermute x3 -> x0, waiting for transfers between devices: 20.1 us -> none  [rotate_gather(): lax.ppermute(block, axis, [(i, (i + shift) % size) for i in range(size)])]
  transfers between devices with their start and end apart: 72 -> 52, of which waited for: 22 -> 15; matrix products, arithmetic and copies ran while one was open for 51% -> 41% of each run, Pallas kernels for 16% -> 36%
where the time goes in v2:
time: 1220 us; the launch traced here: 1210 us
  Pallas kernels  435 us (36%)
  matrix products  363 us (30%)
  waiting for transfers between devices  123 us (10%)
  other arithmetic  94.8 us (8%)
  blocking collectives  74.9 us (6%)
  starting transfers between devices  53.8 us (4%)
  local copies, waits for them, and re-layouts  50.4 us (4%)
  between operations  16.3 us (1%)
    dot_general x47, matrix products, dot(): return lax.dot_general(left, right, dims, preferred_element_type=F32)  358 us
    pallas_call x2, Pallas kernels, exchange_and_gather(): pl.pallas_call(functools.partial(exchange_kernel, bits, count), in_specs=...  150 us
    ppermute x33, waiting for transfers between devices, flip(): return lax.ppermute(values, 'grp', [(i, i ^ 1 << bit) for i in range(size)])  95.5 us
    pallas_call x4, Pallas kernels, feed(): pl.pallas_call(feed_kernel, grid=(tiles,), in_specs=[pl.BlockSpec((rows,...  86.8 us
    all_to_all x1, blocking collectives, exchange(): lax.all_to_all(values.reshape(experts, rows // experts, width), 'ep', spl...  74.9 us
    pallas_call x1, Pallas kernels, opening(): pl.pallas_call(functools.partial(opening_kernel, bits, count, len(cuts)),...  73.4 us
    pallas_call x2, Pallas kernels, attend_backward(): pl.pallas_call(functools.partial(attend_backward_kernel, sources, start),...  51.5 us
    convert_element_type x20, other arithmetic, step(): sum((part(term, 1 - mine).astype(F32) for term in terms)).astype(BF16)  42.3 us
  transfers between devices with their start and end apart: 52, of which 15 were waited for; matrix products, arithmetic and copies ran while one was open for 41% of the time, Pallas kernels for 36%

profile of v2, /device:TPU:0, one launch (start us, length us, event | category | flops | bytes accessed | tf_op | source)
XLA Modules:
  0.0 1210.4 jit_solution(10862311218139227770)
XLA Ops:
  25.7 73.4 %opening.1 = (bf16[4,256,2048]{2,1,0:T(8,128)(2,1)}, bf16[8,256,2048]{2,1,0:T(8,128)(2,1)}, bf16[256,4096]{1,0:T(8,128)(2,1)}, bf16[256,2048]{1,0:T(8,128)(2,1)}...) custom-call(bf16[256,2048]{1,0:T(8,128)(2,1)} %fusion.30.refs_0_, ...), custom_call_target="tpu_custom_call" | custom-call | tf_op jit(solution)/shard_map/opening/pallas_call | solution.py:519
  116.4 11.4 convolution_convert_fusion.8.query_ref
  133.2 23.0 %convolution_convert_fusion.3.key_ref.value_ref = bf16[1024,4096]{1,0:T(8,128)(2,1)} fusion(bf16[1024,2048]{1,0:T(8,128)(2,1)} %bitcast.358, bf16[2048,4096]{0,1:T(8,128)(2,1)} %all-gather.7.cloned.1.call-done), kind=kOutput, calls=%fused_computation.16 | convolution fusion | flops 17184063488 | bytes 29360128 | tf_op jit(solution)/shard_map/dot_general | solution.py:37
  156.2 37.9 %attend_forward.1 = (bf16[768,2048]{1,0:T(8,128)(2,1)}, f32[768,128]{1,0:T(8,128)}) custom-call(bf16[768,2048]{1,0:T(8,128)(2,1)} %convolution_convert_fusion.8.query_ref, bf16[1024,4096]{1,0:T(8,128)(2,1)} %convolution_convert_fusion.3.key_ref.value_ref, bf16[1024,4096]{1,0:T(8,128)(2,1)} %convolution_convert_fusion.3.key_ref.value_ref, ...), custom_call_target="tpu_custom_call" | custom-call | flops 4026531840 | bytes 14680064 | tf_op jit(solution)/shard_map/attend_forward/pallas_call | solution.py:92
  194.1 13.4 %fusion.16 = bf16[768,2048]{1,0:T(8,128)(2,1)} fusion(bf16[768,2048]{1,0:T(8,128)(2,1)} %get-tuple-element.125, bf16[1,2048,2048]{2,1,0:T(8,128)(2,1)} %all-gather.15.cloned.1.call-done), kind=kOutput, calls=%fused_computation.36 | convolution fusion | flops 6444023808 | bytes 14680064 | tf_op jit(solution)/shard_map/dot_general | solution.py:37
  207.6 69.2 %exchange_and_gather.2 = (bf16[4,192,2048]{2,1,0:T(8,128)(2,1)}, bf16[8,256,2048]{2,1,0:T(8,128)(2,1)}) custom-call(bf16[4,192,2048]{2,1,0:T(8,128)(2,1)} %bitcast.386, bf16[256,2048]{1,0:T(8,128)(2,1)} %get-tuple-element.126.shard_ref), custom_call_target="tpu_custom_call" | custom-call | tf_op jit(solution)/shard_map/exchange_and_gather/pallas_call | solution.py:585
  285.2 80.5 %exchange_and_gather.3 = (bf16[4,192,2048]{2,1,0:T(8,128)(2,1)}, bf16[8,256,2048]{2,1,0:T(8,128)(2,1)}) custom-call(bf16[4,192,2048]{2,1,0:T(8,128)(2,1)} %bitcast.362, bf16[256,2048]{1,0:T(8,128)(2,1)} %get-tuple-element.128.shard_ref), custom_call_target="tpu_custom_call" | custom-call | tf_op jit(solution)/shard_map/exchange_and_gather/pallas_call | solution.py:585
  368.3 17.5 %feed.4 = (bf16[768,1024]{1,0:T(8,128)(2,1)}, bf16[768,2048]{1,0:T(8,128)(2,1)}) custom-call(bf16[768,2048]{1,0:T(8,128)(2,1)} %bitcast.350, bf16[768,2048]{1,0:T(8,128)(2,1)} %bitcast.344, bf16[2048,2048]{1,0:T(8,128)(2,1)} %bitcast.369, bf16[5632,2048]{1,0:T(8,128)(2,1)} %all-gather.9.cloned.1.call-done.down_ref), custom_call_target="tpu_custom_call" | custom-call | flops 9663676416 | bytes 18874368 | tf_op jit(solution)/shard_map/feed/pallas_call | solution.py:230
  385.8 11.7 fusion.134
  397.5 17.3 %feed.5 = (bf16[768,1024]{1,0:T(8,128)(2,1)}, bf16[768,2048]{1,0:T(8,128)(2,1)}) custom-call(bf16[768,2048]{1,0:T(8,128)(2,1)} %bitcast.351, bf16[768,2048]{1,0:T(8,128)(2,1)} %bitcast.345, bf16[2048,2048]{1,0:T(8,128)(2,1)} %bitcast.371, bf16[5632,2048]{1,0:T(8,128)(2,1)} %all-gather.9.cloned.1.call-done.down_ref), custom_call_target="tpu_custom_call" | custom-call | flops 9663676416 | bytes 18874368 | tf_op jit(solution)/shard_map/feed/pallas_call | solution.py:230
  414.8 13.6 %convolution_add_fusion.1 = f32[768,2048]{1,0:T(8,128)} fusion(f32[768,2048]{1,0:T(8,128)} %fusion.134, bf16[768,2048]{1,0:T(8,128)(2,1)} %get-tuple-element.135, bf16[2048,2048]{1,0:T(8,128)(2,1)} %bitcast.372), kind=kOutput, calls=%fused_computation.32 | convolution fusion | flops 6444023808 | bytes 24117248 | tf_op jit(solution)/shard_map/dot_general | solution.py:37
  462.6 28.6 %feed.6 = (bf16[768,2048]{1,0:T(8,128)(2,1)}, bf16[768,4096]{1,0:T(8,128)(2,1)}) custom-call(bf16[768,2048]{1,0:T(8,128)(2,1)} %bitcast.352, bf16[768,2048]{1,0:T(8,128)(2,1)} %bitcast.346, bf16[2048,4096]{1,0:T(8,128)(2,1)} %all-gather.11.cloned.1.call-done.gate_up_ref, bf16[5632,2048]{1,0:T(8,128)(2,1)} %all-gather.9.cloned.1.call-done.down_ref), custom_call_target="tpu_custom_call" | custom-call | flops 19327352832 | bytes 31457280 | tf_op jit(solution)/shard_map/feed/pallas_call | solution.py:230
  491.3 21.7 %convolution_add_fusion = f32[768,2048]{1,0:T(8,128)} fusion(f32[768,2048]{1,0:T(8,128)} %convolution_add_fusion.1, bf16[768,4096]{1,0:T(8,128)(2,1)} %get-tuple-element.147, bf16[2048,4096]{1,0:T(8,128)(2,1)} %all-gather.11.cloned.1.call-done.gate_up_ref), kind=kOutput, calls=%fused_computation.27 | convolution fusion | flops 12886474752 | bytes 35651584 | tf_op jit(solution)/shard_map/dot_general | solution.py:37
  521.7 18.9 %convolution_convert_fusion.1 = bf16[2048,4096]{1,0:T(8,128)(2,1)} fusion(bf16[768,2048]{1,0:T(8,128)(2,1)S(1)} %bitcast.354, bf16[768,4096]{1,0:T(8,128)(2,1)} %get-tuple-element.147), kind=kOutput, calls=%fused_computation.1 | convolution fusion | flops 12893290496 | bytes 26214400 | tf_op jit(solution)/shard_map/dot_general | solution.py:37
  540.7 23.3 %feed.7 = (bf16[768,1536]{1,0:T(8,128)(2,1)}, bf16[768,3072]{1,0:T(8,128)(2,1)}) custom-call(bf16[768,2048]{1,0:T(8,128)(2,1)} %bitcast.353, bf16[768,2048]{1,0:T(8,128)(2,1)} %bitcast.347, bf16[2048,3072]{1,0:T(8,128)(2,1)} %all-gather.13.cloned.1.call-done.gate_up_ref, bf16[5632,2048]{1,0:T(8,128)(2,1)} %all-gather.9.cloned.1.call-done.down_ref), custom_call_target="tpu_custom_call" | custom-call | flops 14495514624 | bytes 25165824 | tf_op jit(solution)/shard_map/feed/pallas_call | solution.py:230
  568.0 19.6 %add_convert_fusion.2 = bf16[768,2048]{1,0:T(8,128)(2,1)} fusion(f32[768,2048]{1,0:T(8,128)} %convolution_add_fusion, bf16[768,3072]{1,0:T(8,128)(2,1)} %get-tuple-element.153, bf16[2048,3072]{1,0:T(8,128)(2,1)} %all-gather.13.cloned.1.call-done.gate_up_ref), kind=kOutput, calls=%fused_computation.19 | convolution fusion | flops 9666822144 | bytes 26738688 | tf_op jit(solution)/shard_map/dot_general | solution.py:37
  587.7 22.5 %convolution_convert_fusion.11 = bf16[768,2048]{1,0:T(8,128)(2,1)} fusion(bf16[768,5632]{1,0:T(8,128)(2,1)S(1)} %pad_maximum_fusion, bf16[5632,2048]{1,0:T(8,128)(2,1)} %all-gather.9.cloned.1.call-done.down_ref), kind=kOutput, calls=%fused_computation.38 | convolution fusion | flops 17718312960 | bytes 34865152 | tf_op jit(solution)/shard_map/dot_general | solution.py:37
  610.2 15.0 %convolution_convert_fusion.2 = bf16[2048,3072]{1,0:T(8,128)(2,1)} fusion(bf16[768,2048]{1,0:T(8,128)(2,1)S(1)} %bitcast.355, bf16[768,3072]{1,0:T(8,128)(2,1)} %get-tuple-element.153), kind=kOutput, calls=%fused_computation.2 | convolution fusion | flops 9669967872 | bytes 20447232 | tf_op jit(solution)/shard_map/dot_general | solution.py:37
  641.2 58.9 %collective-permute-done.6 = bf16[2,256,2048]{2,1,0:T(8,128)(2,1)} collective-permute-done((bf16[2,256,2048]{2,1,0:T(8,128)(2,1)}, bf16[2,256,2048]{2,1,0:T(8,128)(2,1)}, u32[]{:S(2)}, u32[]{:S(2)}) %collective-permute-start.6) | collective-permute-done | bytes 2097184 | tf_op jit(solution)/shard_map/ppermute | solution.py:610
  716.0 25.1 %convolution_convert_fusion = bf16[5632,2048]{1,0:T(8,128)(2,1)} fusion(bf16[768,5632]{1,0:T(8,128)(2,1)} %copy-done.20, bf16[768,2048]{1,0:T(8,128)(2,1)S(1)} %bitcast.348), kind=kOutput, calls=%fused_computation | convolution fusion | flops 17728274432 | bytes 34865152 | tf_op jit(solution)/shard_map/dot_general | solution.py:37
  743.0 74.9 %all_to_all.25 = bf16[4,192,2048]{2,1,0:T(8,128)(2,1)} all-to-all(bf16[4,192,2048]{2,1,0:T(8,128)(2,1)S(1)} %bitcast.364), channel_id=1, replica_groups=mesh['grp'=8,'ep'=4] {'ep'}, dimensions={0} | all-to-all | bytes 6291456 | tf_op jit(solution)/shard_map/all_to_all | solution.py:695
  833.0 10.6 fusion.19.grad_ref
  843.6 25.7 %attend_backward.2 = (bf16[768,1024]{1,0:T(8,128)(2,1)}, bf16[1024,2048]{1,0:T(8,128)(2,1)}) custom-call(bf16[768,2048]{1,0:T(8,128)(2,1)} %convolution_convert_fusion.8.query_ref, bf16[1024,4096]{1,0:T(8,128)(2,1)} %convolution_convert_fusion.3.key_ref.value_ref, bf16[1024,4096]{1,0:T(8,128)(2,1)} %convolution_convert_fusion.3.key_ref.value_ref, ...), custom_call_target="tpu_custom_call" | custom-call | flops 5033164800 | bytes 14680064 | tf_op jit(solution)/shard_map/attend_backward/pallas_call | solution.py:174
  869.3 25.8 %attend_backward.3 = (bf16[768,1024]{1,0:T(8,128)(2,1)}, bf16[1024,2048]{1,0:T(8,128)(2,1)}) custom-call(bf16[768,2048]{1,0:T(8,128)(2,1)} %convolution_convert_fusion.8.query_ref, bf16[1024,4096]{1,0:T(8,128)(2,1)} %convolution_convert_fusion.3.key_ref.value_ref, bf16[1024,4096]{1,0:T(8,128)(2,1)} %convolution_convert_fusion.3.key_ref.value_ref, ...), custom_call_target="tpu_custom_call" | custom-call | flops 5033164800 | bytes 14680064 | tf_op jit(solution)/shard_map/attend_backward/pallas_call | solution.py:174
  910.4 14.1 %fusion = f32[1024,2048]{1,0:T(8,128)} fusion(bf16[1024,2048]{1,0:T(8,128)(2,1)S(1)} %copy-done.107, bf16[2048,4096]{0,1:T(8,128)(2,1)} %all-gather.7.cloned.1.call-done), kind=kOutput, calls=%fused_computation.4 | convolution fusion | flops 8589934592 | bytes 20971520 | tf_op jit(solution)/shard_map/dot_general | solution.py:37
  924.4 15.8 %fusion.5 = bf16[1024,2048]{1,0:T(8,128)(2,1)} fusion(f32[1024,2048]{1,0:T(8,128)} %fusion, f32[4,256,2048]{2,1,0:T(8,128)S(1)} %fusion.72, bf16[1024,2048]{1,0:T(8,128)(2,1)} %get-tuple-element.173, bf16[2048,4096]{0,1:T(8,128)(2,1)} %all-gather.7.cloned.1.call-done), kind=kOutput, calls=%fused_computation.11 | convolution fusion | flops 8596226048 | bytes 33554432 | tf_op jit(solution)/shard_map/dot_general | solution.py:37
  988.3 11.5 collective-permute-done.10
  1002.6 10.6 collective-permute-done.14
  1044.1 10.2 collective-permute-done.16
  1097.4 9.7 all-reduce.3.cloned.1.call-done.first_ref
  1129.4 16.9 %assemble.1 = f32[256,11264]{1,0:T(8,128)} custom-call(bf16[256,4096]{1,0:T(8,128)(2,1)} %reduce-scatter.4.cloned.1.call-done.refs_0_, f32[256,2048]{1,0:T(8,128)} %bitcast_add_fusion.2.refs_1_, f32[256,2048]{1,0:T(8,128)} %bitcast_add_fusion.1.refs_2_, bf16[256,3072]{1,0:T(8,128)(2,1)} %reduce-scatter.6.cloned.1.call-done.refs_3_), custom_call_target="tpu_custom_call" | custom-call | bytes 17301504 | tf_op jit(solution)/shard_map/assemble/pallas_call | solution.py:282
  1179.3 18.6 %transpose.38 = f32[4096,256]{1,0:T(8,128)} custom-call(bf16[256,2048]{1,0:T(8,128)(2,1)} %all-reduce.3.cloned.1.call-done.first_ref, bf16[256,2048]{1,0:T(8,128)(2,1)} %all-reduce.5.cloned.1.call-done.second_ref), custom_call_target="tpu_custom_call" | custom-call | bytes 6291456 | tf_op jit(solution)/shard_map/transpose/pallas_call | solution.py:311
  (494 shorter events, 346.8 us)
Async XLA Ops:
  7.2 126.0 %all-gather.7.cloned.1.call-start = ((), (), s32[]{:S(2)}) async-start(), calls=%async_computation.8 | async-start | bytes 18874368 | tf_op jit(solution)/shard_map/all_gather | solution.py:746
  11.1 183.0 %all-gather.15.cloned.1.call-start = ((), (), s32[]{:S(2)}) async-start(), calls=%async_computation.17 | async-start | bytes 9437184 | tf_op jit(solution)/shard_map/all_gather | solution.py:746
  13.1 355.2 %all-gather.9.cloned.1.call-start = ((), (), s32[]{:S(2)}) async-start(), calls=%async_computation.9 | async-start | bytes 25952256 | tf_op jit(solution)/shard_map/all_gather | solution.py:746
  99.2 363.4 %all-gather.11.cloned.1.call-start = ((), (), s32[]{:S(2)}) async-start(), calls=%async_computation.10 | async-start | bytes 18874368 | tf_op jit(solution)/shard_map/all_gather | solution.py:746
  109.4 84.7 %all-to-all-start = ((bf16[4,192,2048]{2,1,0:T(8,128)(2,1)}), bf16[4,192,2048]{2,1,0:T(8,128)(2,1)S(1)}, u32[]{:S(2)}, u32[]{:S(2)}) async-start(bf16[4,192,2048]{2,1,0:T(8,128)(2,1)} %bitcast.363), calls=%async_computation | async-start | bytes 6291456 | tf_op jit(solution)/shard_map/all_to_all | solution.py:695
  113.1 427.5 %all-gather.13.cloned.1.call-start = ((), (), s32[]{:S(2)}) async-start(), calls=%async_computation.11 | async-start | bytes 14155776 | tf_op jit(solution)/shard_map/all_gather | solution.py:746
  127.9 741.4 %reduce-scatter.4.cloned.1.call-start = ((), (), s32[]{:S(2)}) async-start(), calls=%async_computation.12 | async-start | bytes 18874368 | tf_op jit(solution)/shard_map/reduce_scatter | solution.py:844
  447.6 65.4 %collective-permute-start.4 = (bf16[1024,2048]{1,0:T(8,128)(2,1)}, bf16[1024,2048]{1,0:T(8,128)(2,1)}, u32[]{:S(2)}, u32[]{:S(2)}) collective-permute-start(bf16[1024,2048]{1,0:T(8,128)(2,1)} %convolution_convert_fusion.4), channel_id=1, source_target_pairs={{0,4},{4,0},{8,12},{12,8},{16,20},{20,16},{24,28},{28,24},{1,5},{5... | collective-permute-start | bytes 12582920 | tf_op jit(solution)/shard_map/ppermute | solution.py:610
  454.2 58.7 %collective-permute-start.3 = (bf16[1024,2048]{1,0:T(8,128)(2,1)}, bf16[1024,2048]{1,0:T(8,128)(2,1)}, u32[]{:S(2)}, u32[]{:S(2)}) collective-permute-start(bf16[1024,2048]{1,0:T(8,128)(2,1)} %convolution_convert_fusion.5), channel_id=1, source_target_pairs={{0,4},{4,0},{8,12},{12,8},{16,20},{20,16},{24,28},{28,24},{1,5},{5... | collective-permute-start | bytes 12582920 | tf_op jit(solution)/shard_map/ppermute | solution.py:610
  540.6 354.5 %reduce-scatter.6.cloned.1.call-start = ((), (), s32[]{:S(2)}) async-start(), calls=%async_computation.13 | async-start | bytes 14155776 | tf_op jit(solution)/shard_map/reduce_scatter | solution.py:850
  625.2 80.7 %all-to-all-start.1 = ((bf16[4,192,2048]{2,1,0:T(8,128)(2,1)}), bf16[4,192,2048]{2,1,0:T(8,128)(2,1)}, u32[]{:S(2)}, u32[]{:S(2)}) async-start(bf16[4,192,2048]{2,1,0:T(8,128)(2,1)} %bitcast.45), calls=%async_computation.1 | async-start | bytes 6291456 | tf_op jit(solution)/shard_map/all_to_all | solution.py:695
  629.9 414.2 %reduce-scatter.8.cloned.1.call-start = ((), (), s32[]{:S(2)}) async-start(), calls=%async_computation.14 | async-start | bytes 25952256 | tf_op jit(solution)/shard_map/reduce_scatter | solution.py:869
  630.2 70.0 %collective-permute-start.6 = (bf16[2,256,2048]{2,1,0:T(8,128)(2,1)}, bf16[2,256,2048]{2,1,0:T(8,128)(2,1)}, u32[]{:S(2)}, u32[]{:S(2)}) collective-permute-start(bf16[2,256,2048]{2,1,0:T(8,128)(2,1)} %fusion.38), channel_id=1, source_target_pairs={{0,16},{4,20},{8,24},{12,28},{16,0},{20,4},{24,8},{28,12},{1,17},{... | collective-permute-start | bytes 6291464 | tf_op jit(solution)/shard_map/ppermute | solution.py:610
  631.7 68.5 %collective-permute-start.5 = (bf16[2,256,2048]{2,1,0:T(8,128)(2,1)}, bf16[2,256,2048]{2,1,0:T(8,128)(2,1)S(1)}, u32[]{:S(2)}, u32[]{:S(2)}) collective-permute-start(bf16[2,256,2048]{2,1,0:T(8,128)(2,1)} %fusion.37), channel_id=1, source_target_pairs={{0,8},{4,12},{8,0},{12,4},{16,24},{20,28},{24,16},{28,20},{1,9},{5... | collective-permute-start | bytes 6291464 | tf_op jit(solution)/shard_map/ppermute | solution.py:610
  817.9 77.2 %all-to-all-start.3 = ((bf16[4,192,2048]{2,1,0:T(8,128)(2,1)}), bf16[4,192,2048]{2,1,0:T(8,128)(2,1)S(1)}, u32[]{:S(2)}, u32[]{:S(2)}) async-start(bf16[4,192,2048]{2,1,0:T(8,128)(2,1)} %bitcast.385), calls=%async_computation.3 | async-start | bytes 6291456 | tf_op jit(solution)/shard_map/all_to_all | solution.py:695
  831.0 119.0 %collective-permute-start.37 = (bf16[256,2048]{1,0:T(8,128)(2,1)}, bf16[256,2048]{1,0:T(8,128)(2,1)}, u32[]{:S(2)}, u32[]{:S(2)}) collective-permute-start(bf16[256,2048]{1,0:T(8,128)(2,1)} %fusion.52), channel_id=1, source_target_pairs={{0,8},{4,12},{8,0},{12,4},{16,24},{20,28},{24,16},{28,20},{1,9},{5... | collective-permute-start | bytes 3145736 | tf_op jit(solution)/shard_map/ppermute | solution.py:610
  832.3 121.5 %collective-permute-start.36 = (bf16[256,2048]{1,0:T(8,128)(2,1)}, bf16[256,2048]{1,0:T(8,128)(2,1)}, u32[]{:S(2)}, u32[]{:S(2)}) collective-permute-start(bf16[256,2048]{1,0:T(8,128)(2,1)} %fusion.51), channel_id=1, source_target_pairs={{0,16},{4,20},{8,24},{12,28},{16,0},{20,4},{24,8},{28,12},{1,17},{... | collective-permute-start | bytes 3145736 | tf_op jit(solution)/shard_map/ppermute | solution.py:610
  964.7 130.0 %all-to-all-start.4 = ((bf16[4,256,2048]{2,1,0:T(8,128)(2,1)}), bf16[4,256,2048]{2,1,0:T(8,128)(2,1)}, u32[]{:S(2)}, u32[]{:S(2)}) async-start(bf16[4,256,2048]{2,1,0:T(8,128)(2,1)} %bitcast.379), calls=%async_computation.7 | async-start | bytes 8388608 | tf_op jit(solution)/shard_map/all_to_all | solution.py:695
  969.6 137.4 %all-reduce.3.cloned.1.call-start = ((), (), s32[]{:S(2)}) async-start(), calls=%async_computation.15 | async-start | bytes 2097152 | tf_op jit(solution)/shard_map/psum | solution.py:923
  979.0 35.5 %collective-permute-start.12 = (bf16[1024,1024]{1,0:T(8,128)(2,1)S(1)}, bf16[1024,1024]{1,0:T(8,128)(2,1)S(1)}, u32[]{:S(2)}, u32[]{:S(2)}) collective-permute-start(bf16[1024,1024]{1,0:T(8,128)(2,1)S(1)} %convolution_convert_fusion.12), channel_id=1, source_target_pairs={{0,4},{4,0},{8,12},{12,8},{16,20},{20,16},{24,28},{28,24},{1,5},{5... | collective-permute-start | bytes 6291464 | tf_op jit(solution)/shard_map/ppermute | solution.py:610
  981.6 33.0 %collective-permute-start.11 = (bf16[1024,1024]{1,0:T(8,128)(2,1)S(1)}, bf16[1024,1024]{1,0:T(8,128)(2,1)S(1)}, u32[]{:S(2)}, u32[]{:S(2)}) collective-permute-start(bf16[1024,1024]{1,0:T(8,128)(2,1)S(1)} %convolution_convert_fusion.13), channel_id=1, source_target_pairs={{0,4},{4,0},{8,12},{12,8},{16,20},{20,16},{24,28},{28,24},{1,5},{5... | collective-permute-start | bytes 6291464 | tf_op jit(solution)/shard_map/ppermute | solution.py:610
  1023.2 37.3 %collective-permute-start.18 = (bf16[1024,1024]{1,0:T(8,128)(2,1)}, bf16[1024,1024]{1,0:T(8,128)(2,1)}, u32[]{:S(2)}, u32[]{:S(2)}) collective-permute-start(bf16[1024,1024]{1,0:T(8,128)(2,1)} %convolution_convert_fusion.24), channel_id=1, source_target_pairs={{0,4},{4,0},{8,12},{12,8},{16,20},{20,16},{24,28},{28,24},{1,5},{5... | collective-permute-start | bytes 6291464 | tf_op jit(solution)/shard_map/ppermute | solution.py:610
  1027.4 36.9 %collective-permute-start.17 = (bf16[1024,1024]{1,0:T(8,128)(2,1)}, bf16[1024,1024]{1,0:T(8,128)(2,1)}, u32[]{:S(2)}, u32[]{:S(2)}) collective-permute-start(bf16[1024,1024]{1,0:T(8,128)(2,1)} %convolution_convert_fusion.25), channel_id=1, source_target_pairs={{0,4},{4,0},{8,12},{12,8},{16,20},{20,16},{24,28},{28,24},{1,5},{5... | collective-permute-start | bytes 6291464 | tf_op jit(solution)/shard_map/ppermute | solution.py:610
  1055.0 124.4 %all-reduce.5.cloned.1.call-start = ((), (), s32[]{:S(2)}) async-start(), calls=%async_computation.16 | async-start | bytes 2097152 | tf_op jit(solution)/shard_map/psum | solution.py:933
  1059.3 32.9 %collective-permute-start.19 = (bf16[256,1024]{1,0:T(8,128)(2,1)S(1)}, bf16[256,1024]{1,0:T(8,128)(2,1)S(1)}, u32[]{:S(2)}, u32[]{:S(2)}) collective-permute-start(bf16[256,1024]{1,0:T(8,128)(2,1)S(1)} %fusion.79), channel_id=1, source_target_pairs={{0,16},{4,20},{8,24},{12,28},{16,0},{20,4},{24,8},{28,12},{1,17},{... | collective-permute-start | bytes 1572872 | tf_op jit(solution)/shard_map/ppermute | solution.py:610
  1063.4 55.6 %collective-permute-start.24 = (bf16[2,256,1024]{2,1,0:T(8,128)(2,1)}, bf16[2,256,1024]{2,1,0:T(8,128)(2,1)}, u32[]{:S(2)}, u32[]{:S(2)}) collective-permute-start(bf16[2,256,1024]{2,1,0:T(8,128)(2,1)} %fusion.58), channel_id=1, source_target_pairs={{0,16},{4,20},{8,24},{12,28},{16,0},{20,4},{24,8},{28,12},{1,17},{... | collective-permute-start | bytes 3145736 | tf_op jit(solution)/shard_map/ppermute | solution.py:610
  1071.4 35.7 %collective-permute-start.22 = (bf16[1024,1024]{1,0:T(8,128)(2,1)}, bf16[1024,1024]{1,0:T(8,128)(2,1)}, u32[]{:S(2)}, u32[]{:S(2)}) collective-permute-start(bf16[1024,1024]{1,0:T(8,128)(2,1)} %convolution_convert_fusion.20), channel_id=1, source_target_pairs={{0,4},{4,0},{8,12},{12,8},{16,20},{20,16},{24,28},{28,24},{1,5},{5... | collective-permute-start | bytes 6291464 | tf_op jit(solution)/shard_map/ppermute | solution.py:610
  1075.5 36.1 %collective-permute-start.21 = (bf16[1024,1024]{1,0:T(8,128)(2,1)}, bf16[1024,1024]{1,0:T(8,128)(2,1)}, u32[]{:S(2)}, u32[]{:S(2)}) collective-permute-start(bf16[1024,1024]{1,0:T(8,128)(2,1)} %convolution_convert_fusion.21), channel_id=1, source_target_pairs={{0,4},{4,0},{8,12},{12,8},{16,20},{20,16},{24,28},{28,24},{1,5},{5... | collective-permute-start | bytes 6291464 | tf_op jit(solution)/shard_map/ppermute | solution.py:610
  1110.1 41.6 %collective-permute-start.26 = (bf16[2,256,1024]{2,1,0:T(8,128)(2,1)}, bf16[2,256,1024]{2,1,0:T(8,128)(2,1)}, u32[]{:S(2)}, u32[]{:S(2)}) collective-permute-start(bf16[2,256,1024]{2,1,0:T(8,128)(2,1)} %fusion.60), channel_id=1, source_target_pairs={{0,16},{4,20},{8,24},{12,28},{16,0},{20,4},{24,8},{28,12},{1,17},{... | collective-permute-start | bytes 3145736 | tf_op jit(solution)/shard_map/ppermute | solution.py:610
  1114.5 37.2 %collective-permute-start.25 = (bf16[2,256,1024]{2,1,0:T(8,128)(2,1)}, bf16[2,256,1024]{2,1,0:T(8,128)(2,1)}, u32[]{:S(2)}, u32[]{:S(2)}) collective-permute-start(bf16[2,256,1024]{2,1,0:T(8,128)(2,1)} %fusion.59), channel_id=1, source_target_pairs={{0,8},{4,12},{8,0},{12,4},{16,24},{20,28},{24,16},{28,20},{1,9},{5... | collective-permute-start | bytes 3145736 | tf_op jit(solution)/shard_map/ppermute | solution.py:610
  1121.4 40.2 %collective-permute-start.33 = (bf16[256,1024]{1,0:T(8,128)(2,1)}, bf16[256,1024]{1,0:T(8,128)(2,1)}, u32[]{:S(2)}, u32[]{:S(2)}) collective-permute-start(bf16[256,1024]{1,0:T(8,128)(2,1)} %fusion.82), channel_id=1, source_target_pairs={{0,8},{4,12},{8,0},{12,4},{16,24},{20,28},{24,16},{28,20},{1,9},{5... | collective-permute-start | bytes 1572872 | tf_op jit(solution)/shard_map/ppermute | solution.py:610
  1124.3 41.1 %collective-permute-start.32 = (bf16[256,1024]{1,0:T(8,128)(2,1)}, bf16[256,1024]{1,0:T(8,128)(2,1)}, u32[]{:S(2)}, u32[]{:S(2)}) collective-permute-start(bf16[256,1024]{1,0:T(8,128)(2,1)} %fusion.81), channel_id=1, source_target_pairs={{0,16},{4,20},{8,24},{12,28},{16,0},{20,4},{24,8},{28,12},{1,17},{... | collective-permute-start | bytes 1572872 | tf_op jit(solution)/shard_map/ppermute | solution.py:610
  (137 other events, 1941.9 us)
Sparse Core Ops, SparseCore 0:
  11.2 121.9 all-gather.6
  135.7 54.3 all-gather.14
  192.0 176.2 all-gather.8
  370.0 92.5 all-gather.10
  464.4 72.1 all-gather.12
  540.7 138.0 reduce-scatter.3
  682.3 92.1 reduce-scatter.5
  778.1 168.3 reduce-scatter.7
  1055.1 51.8 all-reduce.2
  1119.1 49.3 all-reduce.4

commit v3 on v2

--- a/solution.py
+++ b/solution.py
@@ -14,6 +14,7 @@
 
 EPSILON = 1e-06
 NEGATIVE = -1e30
+LOG2_E = 1.4426950408889634
 CONTRACT_ROWS = (((0,), (0,)), ((), ()))
 CONTRACT_COLUMNS = (((1,), (1,)), ((), ()))
 BF16 = jnp.bfloat16
@@ -62,7 +63,7 @@
     head = pl.program_id(0)
     capacity = query_ref.shape[0] // sources
     tokens = key_ref.shape[0] // sources
-    scaling = HEAD_DIM ** (-0.5)
+    scaling = HEAD_DIM ** (-0.5) * LOG2_E
 
     @pl.when(head == 0)
     def _():
@@ -77,12 +78,12 @@
         places = lax.broadcasted_iota(jnp.int32, scores.shape, 1)
         scores = jnp.where((places >= first) & (places <= last), scores, NEGATIVE)
         peak = jnp.max(scores, axis=1, keepdims=True)
-        exponent = jnp.exp(scores - peak)
+        exponent = jnp.exp2(scores - peak)
         total = jnp.sum(exponent, axis=1, keepdims=True)
-        probs = (exponent * (1.0 / total)).astype(BF16)
-        out_ref[rows, :] = dot(probs, value_ref[:span, :]).astype(BF16)
+        mixed = dot(exponent.astype(BF16), value_ref[:span, :])
+        out_ref[rows, :] = (mixed * (1.0 / total)).astype(BF16)
         lanes = lax.broadcasted_iota(jnp.int32, (capacity, 128), 1)
-        logsum_ref[rows, :] = jnp.where(lanes == head, peak + jnp.log(total), logsum_ref[rows, :])
+        logsum_ref[rows, :] = jnp.where(lanes == head, peak + jnp.log2(total), logsum_ref[rows, :])
 
 
 def attend_forward(queries, keys_values, bounds, sources):
@@ -118,7 +119,6 @@
 
 def attend_backward_kernel(
     sources,
-    start,
     query_ref,
     key_ref,
     value_ref,
@@ -130,7 +130,7 @@
     key_total,
     value_total,
 ):
-    head = pl.program_id(0) + start
+    head = pl.program_id(0)
     capacity = query_ref.shape[0] // sources
     tokens = key_ref.shape[0] // sources
     scaling = HEAD_DIM ** (-0.5)
@@ -145,10 +145,10 @@
         logsum = jnp.sum(
             jnp.where(lanes == head, logsum_ref[rows, :], 0.0), axis=1, keepdims=True
         )
-        scores = dot(query, key_ref[:span, :], CONTRACT_COLUMNS) * scaling
+        scores = dot(query, key_ref[:span, :], CONTRACT_COLUMNS) * (scaling * LOG2_E)
         places = lax.broadcasted_iota(jnp.int32, scores.shape, 1)
         scores = jnp.where((places >= first) & (places <= last), scores, NEGATIVE)
-        probs = jnp.exp(scores - logsum)
+        probs = jnp.exp2(scores - logsum)
         grad_probs = dot(grad, value_ref[:span, :], CONTRACT_COLUMNS)
         weighted = probs * grad_probs
         correction = jnp.sum(weighted, axis=1, keepdims=True)
@@ -166,19 +166,19 @@
     grad_both_ref[:, HEAD_DIM:] = value_total[...].astype(BF16)
 
 
-def attend_backward(queries, keys_values, grads, bounds, logsums, sources, start, heads):
+def attend_backward(queries, keys_values, grads, bounds, logsums, sources):
     rows = queries.shape[0]
-    features = heads * HEAD_DIM
+    features = HEADS * HEAD_DIM
     seq = keys_values.shape[0]
     pairs = (sources + 1) / (2 * sources)
     return pl.pallas_call(
-        functools.partial(attend_backward_kernel, sources, start),
-        grid=(heads,),
+        functools.partial(attend_backward_kernel, sources),
+        grid=(HEADS,),
         in_specs=[
-            pl.BlockSpec((rows, HEAD_DIM), lambda h: (0, h + start)),
-            pl.BlockSpec((seq, HEAD_DIM), lambda h: (0, 2 * (h + start))),
-            pl.BlockSpec((seq, HEAD_DIM), lambda h: (0, 2 * (h + start) + 1)),
-            pl.BlockSpec((rows, HEAD_DIM), lambda h: (0, h + start)),
+            pl.BlockSpec((rows, HEAD_DIM), lambda h: (0, h)),
+            pl.BlockSpec((seq, HEAD_DIM), lambda h: (0, 2 * h)),
+            pl.BlockSpec((seq, HEAD_DIM), lambda h: (0, 2 * h + 1)),
+            pl.BlockSpec((rows, HEAD_DIM), lambda h: (0, h)),
             pl.BlockSpec((rows, 2), lambda h: (0, 0)),
             pl.BlockSpec((rows, 128), lambda h: (0, 0)),
         ],
@@ -195,31 +195,28 @@
         cost_estimate=pl.CostEstimate(
             flops=int(10 * rows * seq * features * pairs),
             bytes_accessed=8 * (rows + seq) * features,
-            transcendentals=int(heads * rows * seq * pairs),
+            transcendentals=int(HEADS * rows * seq * pairs),
         ),
         name="attend_backward",
     )(queries, keys_values, keys_values, grads, bounds, logsums)
 
 
 def feed_kernel(in_ref, grad_ref, gate_up_ref, down_ref, act_ref, grad_gate_up_ref):
-    rows = in_ref.shape[0]
-    step = rows // 3
     units = down_ref.shape[0]
-
-    @pl.loop(0, 3)
-    def _(part):
-        here = pl.ds(pl.multiple_of(part * step, step), step)
-        inputs = in_ref[here, :]
-        gate = dot(inputs, gate_up_ref[:, :units])
-        up = dot(inputs, gate_up_ref[:, units:])
-        grad_act = dot(grad_ref[here, :], down_ref[...], CONTRACT_COLUMNS)
+    step = units // 2
+    for start in range(0, units, step):
+        here = slice(start, start + step)
+        there = slice(units + start, units + start + step)
+        gate = dot(in_ref[...], gate_up_ref[:, here])
+        up = dot(in_ref[...], gate_up_ref[:, there])
+        grad_act = dot(grad_ref[...], down_ref[here, :], CONTRACT_COLUMNS)
         sigmoid = jax.nn.sigmoid(gate)
         silu = gate * sigmoid
-        act_ref[here, :] = (silu * up).astype(BF16)
-        grad_gate_up_ref[here, :units] = (
+        act_ref[:, here] = (silu * up).astype(BF16)
+        grad_gate_up_ref[:, here] = (
             grad_act * up * sigmoid * (1.0 + gate * (1.0 - sigmoid))
         ).astype(BF16)
-        grad_gate_up_ref[here, units:] = (grad_act * silu).astype(BF16)
+        grad_gate_up_ref[:, there] = (grad_act * silu).astype(BF16)
 
 
 def feed(inputs, grads, gate_up, down, offset):
@@ -254,71 +251,66 @@
     )(inputs, grads, gate_up, down)
 
 
-def assemble_kernel(starts, *refs):
-    out_ref = refs[-1]
-    tile = lax.rem(pl.program_id(0), starts[-1])
-    for index, ref in enumerate(refs[:-1]):
-
-        @pl.when((tile >= starts[index]) & (tile < starts[index + 1]))
-        def _():
-            out_ref[...] = ref[...].astype(F32)
+def assemble_kernel(counts, *refs):
+    *refs, out_ref = refs
+    hidden = out_ref.shape[1] // 2
+    start = 0
+    for count in counts:
+        terms, refs = refs[:count], refs[count:]
+        for tile in range(terms[0].shape[1] // (2 * TILE)):
+            for half in range(2):
+                there = half * hidden + start
+                here = (2 * tile + half) * TILE
+                out_ref[:, there : there + TILE] = sum(
+                    term[:, here : here + TILE].astype(F32) for term in terms
+                )
+            start += TILE
 
 
 def assemble(chunks):
-    rows = chunks[0].shape[0]
-    starts = [0]
-    for chunk in chunks:
-        starts.append(starts[-1] + chunk.shape[1] // (2 * TILE))
-    tiles = starts[-1]
-
-    def place(index):
-        last = starts[index + 1] - starts[index] - 1
-
-        def block(j):
-            return (0, jnp.clip(j % tiles - starts[index], 0, last) * 2 + j // tiles)
-
-        return block
-
+    arrays = [term for terms in chunks for term in terms]
+    rows = arrays[0].shape[0]
+    step = 32
+    columns = sum(terms[0].shape[1] for terms in chunks)
     return pl.pallas_call(
-        functools.partial(assemble_kernel, starts),
-        grid=(2 * tiles,),
-        in_specs=[pl.BlockSpec((rows, TILE), place(index)) for index in range(len(chunks))],
-        out_specs=pl.BlockSpec((rows, TILE), lambda j: (0, j)),
-        out_shape=jax.ShapeDtypeStruct((rows, 2 * tiles * TILE), F32),
+        functools.partial(assemble_kernel, [len(terms) for terms in chunks]),
+        grid=(rows // step,),
+        in_specs=[pl.BlockSpec((step, term.shape[1]), lambda i: (i, 0)) for term in arrays],
+        out_specs=pl.BlockSpec((step, columns), lambda i: (i, 0)),
+        out_shape=jax.ShapeDtypeStruct((rows, columns), F32),
+        compiler_params=pltpu.CompilerParams(vmem_limit_bytes=VMEM_BYTES),
         cost_estimate=pl.CostEstimate(
-            flops=0, bytes_accessed=12 * rows * tiles * TILE, transcendentals=0
+            flops=0, bytes_accessed=6 * rows * columns, transcendentals=0
         ),
         name="assemble",
-    )(*chunks)
-
-
-def transpose_kernel(each, first_ref, second_ref, out_ref):
-    head = lax.rem(pl.program_id(0), 2 * each)
-
-    @pl.when(head < each)
-    def _():
-        out_ref[...] = first_ref[...].astype(F32).T
-
-    @pl.when(head >= each)
-    def _():
-        out_ref[...] = second_ref[...].astype(F32).T
-
-
-def transpose(first, second):
-    rows, columns = first.shape
-    each = columns // (2 * HEAD_DIM)
-    spec = pl.BlockSpec((rows, HEAD_DIM), lambda j: (0, j % each * 2 + j // (2 * each)))
+    )(*arrays)
+
+
+def transpose_kernel(steps, in_ref, out_ref):
+    for value in range(2):
+
+        @pl.when(pl.program_id(0) // steps == value)
+        def _():
+            for head in range(TILE // HEAD_DIM):
+                columns = slice((2 * head + value) * HEAD_DIM, (2 * head + value + 1) * HEAD_DIM)
+                rows = slice(head * HEAD_DIM, (head + 1) * HEAD_DIM)
+                out_ref[rows, :] = in_ref[:, columns].astype(F32).T
+
+
+def transpose(values):
+    rows, columns = values.shape
+    steps = columns // (2 * TILE)
     return pl.pallas_call(
-        functools.partial(transpose_kernel, each),
-        grid=(4 * each,),
-        in_specs=[spec, spec],
-        out_specs=pl.BlockSpec((HEAD_DIM, rows), lambda j: (j, 0)),
-        out_shape=jax.ShapeDtypeStruct((2 * columns, rows), F32),
+        functools.partial(transpose_kernel, steps),
+        grid=(2 * steps,),
+        in_specs=[pl.BlockSpec((rows, 2 * TILE), lambda j: (0, j % steps))],
+        out_specs=pl.BlockSpec((TILE, rows), lambda j: (j, 0)),
+        out_shape=jax.ShapeDtypeStruct((columns, rows), F32),
         cost_estimate=pl.CostEstimate(
-            flops=0, bytes_accessed=12 * rows * columns, transcendentals=0
+            flops=0, bytes_accessed=6 * rows * columns, transcendentals=0
         ),
         name="transpose",
-    )(first, second)
+    )(values)
 
 
 MESH = pl.DeviceIdType.MESH
@@ -601,6 +593,296 @@
     return back.reshape(rows, width), full.reshape(-1, full.shape[2])
 
 
+def product_block(dims, left_ref, right_ref, out_ref):
+    out_ref[...] = dot(left_ref[...], right_ref[...], dims).astype(BF16)
+
+
+def multiply_rows(left_ref, right_ref, out_ref):
+    (rows, depth), columns = left_ref.shape, right_ref.shape[1]
+    tile = TILE // 2
+    pltpu.emit_pipeline(
+        functools.partial(product_block, (((1,), (0,)), ((), ()))),
+        grid=(columns // tile,),
+        in_specs=[
+            pl.BlockSpec((rows, depth), lambda j: (0, 0)),
+            pl.BlockSpec((depth, tile), lambda j: (0, j)),
+        ],
+        out_specs=[pl.BlockSpec((rows, tile), lambda j: (0, j))],
+    )(left_ref, right_ref, out_ref)
+
+
+def multiply_columns(left_ref, right_ref, out_ref):
+    (rows, columns), width = left_ref.shape, right_ref.shape[1]
+    tile = TILE // 2
+    pltpu.emit_pipeline(
+        functools.partial(product_block, CONTRACT_ROWS),
+        grid=(columns // tile,),
+        in_specs=[
+            pl.BlockSpec((rows, tile), lambda j: (0, j)),
+            pl.BlockSpec((rows, width), lambda j: (0, 0)),
+        ],
+        out_specs=[pl.BlockSpec((tile, width), lambda j: (j, 0))],
+    )(left_ref, right_ref, out_ref)
+
+
+def exchange_multiply_kernel(count, jobs, *refs):
+    values_ref, refs = refs[0], refs[1:]
+    given, refs = refs[: 2 * len(jobs)], refs[2 * len(jobs) :]
+    back_ref, *made, local, sent, got = refs
+    me = lax.axis_index("grp")
+    place = lax.axis_index("ep")
+    others = [lax.rem(place + shift, count) for shift in range(1, count)]
+    barrier = greet([(me, other) for other in others])
+    pl.semaphore_wait(barrier, count - 1)
+    copies = [
+        pltpu.make_async_remote_copy(
+            src_ref=values_ref.at[other],
+            dst_ref=back_ref.at[place],
+            send_sem=sent.at[index],
+            recv_sem=got.at[index],
+            device_id=(me, other),
+            device_id_type=MESH,
+        )
+        for index, other in enumerate(others)
+    ]
+    own = pltpu.make_async_copy(values_ref.at[place], back_ref.at[place], local)
+    for copy in copies:
+        copy.start()
+    own.start()
+    for index, job in enumerate(jobs):
+        job(given[2 * index], given[2 * index + 1], made[index])
+    for copy in copies:
+        copy.wait()
+    own.wait()
+
+
+def exchange_and_multiply(values, jobs, collective_id):
+    count = lax.axis_size("ep")
+    rows, width = values.shape
+    shape = (count, rows // count, width)
+    outs, flops = [], 0
+    for job, left, right in jobs:
+        by_rows = job is multiply_rows
+        outs.append(
+            jax.ShapeDtypeStruct((left.shape[0 if by_rows else 1], right.shape[1]), BF16)
+        )
+        flops += 2 * left.shape[0] * left.shape[1] * right.shape[1]
+    back, *made = pl.pallas_call(
+        functools.partial(exchange_multiply_kernel, count, [job for job, _, _ in jobs]),
+        in_specs=[pl.BlockSpec(memory_space=pl.ANY)] * (1 + 2 * len(jobs)),
+        out_specs=[pl.BlockSpec(memory_space=pl.ANY)] * (1 + len(jobs)),
+        out_shape=[jax.ShapeDtypeStruct(shape, BF16), *outs],
+        scratch_shapes=[
+            pltpu.SemaphoreType.DMA,
+            *[pltpu.SemaphoreType.DMA((count - 1,))] * 2,
+        ],
+        compiler_params=pltpu.CompilerParams(
+            collective_id=collective_id, has_side_effects=True, vmem_limit_bytes=VMEM_BYTES
+        ),
+        cost_estimate=pl.CostEstimate(
+            flops=flops, bytes_accessed=4 * rows * width, transcendentals=0
+        ),
+        name="exchange_and_multiply",
+    )(values.reshape(shape), *[array for _, left, right in jobs for array in (left, right)])
+    return back.reshape(rows, width), made
+
+
+def exchange_scatter_kernel(bits, count, lefts, sources, jobs, exchanged, *refs):
+    values_ref, refs = (refs[0], refs[1:]) if exchanged else (None, refs)
+    splits, refs = refs[: 2 * lefts], refs[2 * lefts :]
+    many = 1 + sources[-1][1]
+    rights, refs = refs[:many], refs[many:]
+    inputs = sum(job.inputs for job in jobs)
+    given, refs = refs[:inputs], refs[inputs:]
+    back_ref, refs = (refs[0], refs[1:]) if exchanged else (None, refs)
+    total_ref, *refs = refs
+    made, refs = refs[: len(jobs)], refs[len(jobs) :]
+    core_send, core_got, kept, *refs = refs
+    stages = bits - 1
+    sends, refs = refs[:stages], refs[stages:]
+    gots, refs = refs[:stages], refs[stages:]
+    local, out_sent, out_got, core_sent, core_came, stage_sent, stage_came = refs
+    me = lax.axis_index("grp")
+    place = lax.axis_index("ep")
+    others = [lax.rem(place + shift, count) for shift in range(1, count)] if exchanged else []
+    near = [(me ^ (1 << bit), place) for bit in range(bits)]
+    barrier = greet(near + [(me, other) for other in others])
+    pl.semaphore_wait(barrier, len(near) + len(others))
+    copies = [
+        pltpu.make_async_remote_copy(
+            src_ref=values_ref.at[other],
+            dst_ref=back_ref.at[place],
+            send_sem=out_sent.at[index],
+            recv_sem=out_got.at[index],
+            device_id=(me, other),
+            device_id_type=MESH,
+        )
+        for index, other in enumerate(others)
+    ]
+    for copy in copies:
+        copy.start()
+    if exchanged:
+        copies.append(pltpu.make_async_copy(values_ref.at[place], back_ref.at[place], local))
+        copies[-1].start()
+
+    chunks, blocks, rows, width = kept.shape
+    orders = list(range(1, bits)), list(range(1, bits))[::-1]
+
+    def flip(chunk):
+        return pltpu.make_async_remote_copy(
+            src_ref=core_send.at[chunk],
+            dst_ref=core_got.at[chunk],
+            send_sem=core_sent.at[chunk],
+            recv_sem=core_came.at[chunk],
+            device_id=near[0],
+            device_id_type=MESH,
+        )
+
+    def products(chunk):
+        left, source, at = sources[chunk]
+        columns = slice(at * width, (at + 1) * width)
+
+        def fill(left_ref, into):
+            @pl.loop(0, blocks)
+            def _(block):
+                offset = pl.multiple_of(((me ^ (2 * block)) // 2) * rows, rows)
+                into[chunk, block] = dot(
+                    left_ref[:, pl.ds(offset, rows)], rights[source][:, columns], CONTRACT_ROWS
+                ).astype(BF16)
+
+        fill(splits[2 * left + 1], core_send)
+        flip(chunk).start()
+        fill(splits[2 * left], kept)
+
+    def sent_blocks(chunk, stage):
+        order = orders[chunk % 2]
+        gone = sum(1 << (bit - 1) for bit in order[:stage])
+        return [i for i in range(blocks) if not i & gone and i >> (order[stage] - 1) & 1]
+
+    def total_of(chunk, block, stage):
+        value = kept[chunk, block].astype(F32) + core_got[chunk, block].astype(F32)
+        for before in range(stage):
+            bit = 1 << (orders[chunk % 2][before] - 1)
+            at = sent_blocks(chunk, before).index(block ^ bit)
+            value = value + gots[before][chunk, at].astype(F32)
+        return value
+
+    def transfer(chunk, stage):
+        return pltpu.make_async_remote_copy(
+            src_ref=sends[stage].at[chunk],
+            dst_ref=gots[stage].at[chunk],
+            send_sem=stage_sent.at[chunk, stage],
+            recv_sem=stage_came.at[chunk, stage],
+            device_id=near[orders[chunk % 2][stage]],
+            device_id_type=MESH,
+        )
+
+    def come(chunk, stage):
+        if stage == 0:
+            flip(chunk).wait_recv()
+        else:
+            transfer(chunk, stage - 1).wait_recv()
+
+    def advance(chunk, stage):
+        come(chunk, stage)
+        for at, block in enumerate(sent_blocks(chunk, stage)):
+            sends[stage][chunk, at] = total_of(chunk, block, stage).astype(BF16)
+        transfer(chunk, stage).start()
+
+    for chunk in range(chunks):
+        products(chunk)
+        if chunk:
+            advance(chunk - 1, 0)
+    advance(chunks - 1, 0)
+    for job, out_ref in zip(jobs, made):
+        job(*given[: job.inputs], out_ref)
+        given = given[job.inputs :]
+    for stage in range(1, stages):
+        for chunk in range(chunks):
+            advance(chunk, stage)
+    for chunk in range(chunks):
+        come(chunk, stages)
+        total_ref[:, chunk * width : (chunk + 1) * width] = total_of(chunk, 0, stages).astype(BF16)
+    for chunk in range(chunks):
+        flip(chunk).wait_send()
+        for stage in range(stages):
+            transfer(chunk, stage).wait_send()
+    for copy in copies:
+        copy.wait()
+
+
+def exchange_and_scatter(values, products, collective_id, jobs=(), costs=True):
+    groups, count = lax.axis_size("grp"), lax.axis_size("ep")
+    bits = groups.bit_length() - 1
+    exchanged = values is not None
+    columns = 1024
+    splits, rights, sources = [], [], []
+    for split, right in products:
+        if not splits or splits[-1] is not split:
+            splits.append(split)
+        for at in range(right.shape[1] // columns):
+            sources.append((len(splits) - 1, len(rights), at))
+        rights.append(right)
+    chunks, blocks = len(sources), groups // 2
+    own_rows = splits[0][0].shape[1] // blocks
+    block = (own_rows, columns)
+    buffer = pltpu.VMEM((chunks, blocks, *block), BF16)
+    stages = [pltpu.VMEM((chunks, blocks >> (at + 1), *block), BF16) for at in range(bits - 1)]
+    vmem = pl.BlockSpec(memory_space=pltpu.VMEM)
+    anywhere = pl.BlockSpec(memory_space=pl.ANY)
+    flops = 8 * splits[0][0].size * chunks * columns if costs else 0
+    arrays = [array for _, inputs, _ in jobs for array in inputs]
+    back_shape = []
+    if exchanged:
+        rows, width = values.shape
+        values = values.reshape(count, rows // count, width)
+        back_shape = [jax.ShapeDtypeStruct(values.shape, BF16)]
+    outs = pl.pallas_call(
+        functools.partial(
+            exchange_scatter_kernel,
+            bits,
+            count,
+            len(splits),
+            sources,
+            [job for job, _, _ in jobs],
+            exchanged,
+        ),
+        in_specs=[anywhere] * exchanged
+        + [vmem] * (2 * len(splits) + len(rights))
+        + [anywhere] * len(arrays),
+        out_specs=[anywhere] * exchanged + [vmem] + [anywhere] * len(jobs),
+        out_shape=[
+            *back_shape,
+            jax.ShapeDtypeStruct((own_rows, chunks * columns), BF16),
+            *[out for _, _, out in jobs],
+        ],
+        scratch_shapes=[
+            buffer,
+            buffer,
+            buffer,
+            *stages,
+            *stages,
+            pltpu.SemaphoreType.DMA,
+            *[pltpu.SemaphoreType.DMA((count - 1,))] * 2,
+            *[pltpu.SemaphoreType.DMA((chunks,))] * 2,
+            *[pltpu.SemaphoreType.DMA((chunks, bits - 1))] * 2,
+        ],
+        compiler_params=pltpu.CompilerParams(
+            collective_id=collective_id, has_side_effects=True, vmem_limit_bytes=60 * 2**20
+        ),
+        cost_estimate=pl.CostEstimate(flops=flops, bytes_accessed=0, transcendentals=0),
+        name="exchange_and_scatter" if exchanged else "scatter",
+    )(
+        *([values] if exchanged else []),
+        *[half for split in splits for half in split],
+        *rights,
+        *arrays,
+    )
+    if exchanged:
+        return outs[0].reshape(rows, width), outs[1], outs[2:]
+    return None, outs[0], outs[1:]
+
+
 def after(values, *tokens):
     return lax.optimization_barrier((values, *tokens))[0]
 
@@ -643,7 +925,8 @@
             return lax.dynamic_index_in_dim(term, which, axis, keepdims=False)
 
         self.sent = sum(part(term, 1 - mine).astype(F32) for term in terms).astype(BF16)
-        self.terms = [part(term, mine) for term in terms] + [flip(self.sent, bit)]
+        kept = sum(part(term, mine).astype(F32) for term in terms).astype(BF16)
+        self.terms = [kept, flip(self.sent, bit)]
 
     def finish(self):
         while self.order:
@@ -828,32 +1111,37 @@
         acts[index], grads[index] = feed(
             feed_in, grad_mlp_rows, gate_up, down_full, cuts[index][0]
         )
+        if index == 0:
+            steps(middle_scatter, acts[0])
+            grads[0] = after(grads[0], *[scatter.sent for scatter in middle_scatter])
         return total + dot(grads[index], gate_up, CONTRACT_COLUMNS)
 
-    grad_mlp_in = feed_chunk(1, mlp_in, 0.0)
+    normed_split = core_split(normed_all, groups)
+    att_split = core_split(att_in, groups)
+    heads_split = core_split(att_heads, groups)
+    grad_mlp_in = feed_chunk(
+        1, after(mlp_in, *mlp_split, *normed_split, *att_split, *heads_split), 0.0
+    )
     grad_mlp_in = feed_chunk(2, after(mlp_in, grad_mlp_in), grad_mlp_in)
     middle_scatter = scatter_product(mlp_split, [after(grads[1], grad_mlp_in), grads[2]], groups)
-    ready = [scatter.terms[0] for scatter in middle_scatter]
+    ready = [array for scatter in middle_scatter for array in (scatter.terms[0], scatter.sent)]
     grad_mlp_in = feed_chunk(0, after(mlp_in, *ready), grad_mlp_in)
-    steps(middle_scatter, grad_mlp_in)
     first_grad = dot(
         mlp_in,
-        after(grads[0], grad_mlp_in, *[scatter.sent for scatter in middle_scatter]),
+        after(grads[0], grad_mlp_in),
         CONTRACT_ROWS,
     ).astype(BF16)
     first_grad_sum = lax.psum_scatter(first_grad, "grp", scatter_dimension=0, tiled=True)
     grad_mlp_in = feed_chunk(3, after(mlp_in, first_grad), grad_mlp_in).astype(BF16)
-
-    activated = after(jnp.concatenate(acts, axis=1), grad_mlp_in)
-    mlp_rows = dot(activated, down_full).astype(BF16)
-    last_grad = dot(mlp_in, after(grads[3], mlp_rows), CONTRACT_ROWS).astype(BF16)
-    last_grad_sum = lax.psum_scatter(last_grad, "grp", scatter_dimension=0, tiled=True)
-    steps(middle_scatter, last_grad)
-    mlp_returned = after(
-        exchange(grad_mlp_in, experts),
-        mlp_rows,
-        last_grad,
-        *[scatter.sent for scatter in middle_scatter],
+    activated = jnp.concatenate(acts, axis=1)
+    mlp_returned, (down_grad, last_grad) = exchange_and_multiply(
+        grad_mlp_in,
+        [(multiply_columns, activated, grad_mlp_rows), (multiply_columns, mlp_in, grads[3])],
+        3,
+    )
+    down_grad_sum = lax.psum_scatter(down_grad, "grp", scatter_dimension=0, tiled=True)
+    last_grad_sum = lax.psum_scatter(
+        after(last_grad, down_grad), "grp", scatter_dimension=0, tiled=True
     )
 
     grad_final = cotangent.astype(F32)
@@ -865,37 +1153,19 @@
     sent_four = (
         dot(att_high, res_high) + dot(att_low, res_high) + dot(att_high, res_low)
     ).astype(BF16)
-    down_grad = dot(after(activated, sent_four), grad_mlp_rows, CONTRACT_ROWS).astype(BF16)
-    down_grad_sum = lax.psum_scatter(down_grad, "grp", scatter_dimension=0, tiled=True)
-    grad_att_rows = after(exchange(sent_four, experts), down_grad)
-    mlp_back = exchange(after(mlp_rows, grad_att_rows), experts)
-    grad_heads = dot(grad_att_rows, output_full, CONTRACT_COLUMNS).astype(BF16)
-    normed_split = core_split(normed_all, groups)
-    att_split = core_split(att_in, groups)
-    normed_split = core_split(normed_all, groups)
-    att_split = core_split(att_in, groups)
-    half = HEADS // 2
-    grad_one, both_one = attend_backward(
-        queries, keys_values, grad_heads, bounds, logsums, experts, 0, half
-    )
-    both_one = after(both_one, first_grad_sum)
-    grad_two, both_two = attend_backward(
-        after(queries, both_one),
-        keys_values,
-        grad_heads,
-        bounds,
-        logsums,
-        experts,
-        half,
-        HEADS - half,
-    )
-    both_two = after(both_two, mlp_back, last_grad_sum)
-    query_one, query_two = halves(query_full)
-    kv_full_one, kv_full_two = halves(kv_full)
-    grad_att_in = (
-        dot(after(grad_one, both_two), query_one, CONTRACT_COLUMNS)
-        + dot(grad_two, query_two, CONTRACT_COLUMNS)
+    grad_att_rows, (mlp_rows,) = exchange_and_multiply(
+        sent_four, [(multiply_rows, activated, down_full)], 4
+    )
+    steps(middle_scatter, grad_att_rows)
+    ready = [array for scatter in middle_scatter for array in (scatter.terms[0], scatter.sent)]
+    grad_heads = dot(
+        after(grad_att_rows, *ready), output_full, CONTRACT_COLUMNS
     ).astype(BF16)
+    mlp_back = exchange(after(mlp_rows, grad_heads), experts)
+    grad_queries, grad_kv = attend_backward(
+        queries, keys_values, grad_heads, bounds, logsums, experts
+    )
+    grad_att_in = dot(grad_queries, query_full, CONTRACT_COLUMNS).astype(BF16)
     grad_all = (
         jnp.einsum(
             "sct,scd->std",
@@ -903,56 +1173,37 @@
             grad_att_in.reshape(experts, capacity, model_width),
             preferred_element_type=F32,
         ).reshape(experts * tok_dev, model_width)
-        + dot(both_one, kv_full_one, CONTRACT_COLUMNS)
-        + dot(both_two, kv_full_two, CONTRACT_COLUMNS)
+        + dot(grad_kv, kv_full, CONTRACT_COLUMNS)
     ).astype(BF16)
-    grad_back = exchange(grad_all, experts)
-    kv_one = scatter_product(normed_split, halves(after(both_one, grad_all)), groups)
-    ready = [scatter.terms[0] for scatter in kv_one]
-    steps(kv_one, *ready)
-    ready = [scatter.sent for scatter in kv_one]
-    kv_two = scatter_product(normed_split, halves(after(both_two, *ready)), groups)
-    ready = [scatter.terms[0] for scatter in kv_two]
-    steps(kv_one, *ready)
-    steps(kv_two, *[scatter.sent for scatter in kv_one])
-    ready = [scatter.sent for scatter in kv_two]
-    query_scatter = scatter_product(att_split, [after(grad_one, *ready)], groups)
-    query_scatter += scatter_product(att_split, [after(grad_two, *ready)], groups, 1)
-    ready = [scatter.terms[0] for scatter in query_scatter]
-    part_one = after(finish(kv_one), *ready, down_grad_sum).astype(BF16)
-    kv_grad_one = lax.psum(part_one, "ep")
-    steps(kv_two, part_one)
-    ready = [scatter.sent for scatter in kv_two]
-    steps(query_scatter, *ready)
-    ready = [scatter.sent for scatter in query_scatter]
-    output_scatter = scatter_product(
-        core_split(att_heads, groups), halves(after(grad_att_rows, *ready)), groups
-    )
-    ready = [scatter.terms[0] for scatter in output_scatter]
-    part_two = after(finish(kv_two), *ready, grad_back).astype(BF16)
-    kv_grad_two = lax.psum(after(part_two, kv_grad_one), "ep")
-    steps(output_scatter, part_two)
-    ready = [scatter.sent for scatter in output_scatter]
-    mlp_back = after(mlp_back, *ready)
+    grad_back, kv_part, _ = exchange_and_scatter(
+        after(grad_all, mlp_back, first_grad_sum, down_grad_sum), [(normed_split, grad_kv)], 5
+    )
+    kv_grad = lax.psum(kv_part, "ep")
+    while middle_scatter[0].order:
+        steps(middle_scatter)
+    middle_terms = [[after(term, kv_part) for term in scatter.terms] for scatter in middle_scatter]
+    _, both_maps, _ = exchange_and_scatter(
+        None,
+        [
+            (att_split, after(grad_queries, kv_part, last_grad_sum)),
+            (heads_split, grad_att_rows),
+        ],
+        6,
+        costs=False,
+    )
+    kv_grad = after(kv_grad, both_maps)
+    chunks = [[first_grad_sum], *middle_terms, [last_grad_sum]]
+    gate_up_grad = assemble([[after(term, kv_grad) for term in terms] for terms in chunks])[None]
+    down_grad = after(down_grad_sum, kv_grad).astype(F32)[None]
+    query_grad, output_grad = [part.astype(F32)[None] for part in halves(both_maps)]
+    mlp_back = after(mlp_back, kv_grad)
     output = (
         residual_one + dot(mlp_high, mlp_back, CONTRACT_ROWS) + dot(mlp_low, mlp_back, CONTRACT_ROWS)
     ).astype(BF16)
-    steps(query_scatter, output)
-    weight_grads = [
-        after(part, output)
-        for part in (first_grad_sum, *[scatter.finish() for scatter in middle_scatter], last_grad_sum)
-    ]
-    down_grad = after(down_grad_sum, output).astype(F32)[None]
-    ready = [scatter.sent for scatter in query_scatter]
-    steps(output_scatter, *ready)
-    ready = [scatter.sent for scatter in output_scatter]
     grad_normed_one = jnp.sum(
-        after(grad_back, *ready).reshape(experts, tok_dev, model_width).astype(F32), axis=0
-    )
-    query_grad = finish(query_scatter)[None]
-    output_grad = finish(output_scatter)[None]
-    kv_grad = transpose(kv_grad_one, kv_grad_two)
-    gate_up_grad = assemble(weight_grads)[None]
+        grad_back.reshape(experts, tok_dev, model_width).astype(F32), axis=0
+    )
+    kv_grad = transpose(kv_grad)
     grad_inner_one, grad_gain_one = norm_backward(grad_normed_one, unit_one, inverse_one, gain_one)
     grad_input = grad_residual + grad_inner_one
 

time: 1220 us -> 1150 us (0.943)
  Pallas kernels: 435 us -> 759 us
  matrix products: 363 us -> 223 us
  waiting for transfers between devices: 123 us -> 17.3 us
  blocking collectives: 74.9 us -> 0 us
  other arithmetic: 94.8 us -> 56.2 us
  local copies, waits for them, and re-layouts: 50.4 us -> 28.1 us
  starting transfers between devices: 53.8 us -> 41.3 us
    pallas_call x4 -> x7, Pallas kernels: 87 us -> 417 us  [the longest x2 226 us: exchange_and_scatter(): pl.pallas_call(functools.partial(exchange_scatter_kernel, bits, count, le...]
    dot_general x47 -> x26, matrix products: 358 us -> 218 us  [dot(): return lax.dot_general(left, right, dims, preferred_element_type=F32)]
    ppermute x33 -> x9, waiting for transfers between devices: 95.5 us -> 2.87 us  [flip(): return lax.ppermute(values, 'grp', [(i, i ^ 1 << bit) for i in range(size)])]
    all_to_all x1 -> x0, blocking collectives: 74.9 us -> none  [exchange(): lax.all_to_all(values.reshape(experts, rows // experts, width), 'ep', spl...]
    convert_element_type x20 -> x2, other arithmetic: 42.3 us -> 7.73 us  [step(): sum((part(term, 1 - mine).astype(F32) for term in terms)).astype(BF16)]
    squeeze x20 -> x0, local copies, waits for them, and re-layouts: 28.6 us -> none  [part(): return lax.dynamic_index_in_dim(term, which, axis, keepdims=False)]
    ppermute x33 -> x9, starting transfers between devices: 28.7 us -> 9.48 us  [flip(): return lax.ppermute(values, 'grp', [(i, i ^ 1 << bit) for i in range(size)])]
    add x10 -> x0, other arithmetic: 16.9 us -> none  [finish(): return sum((term.astype(F32) for term in self.terms))]
  transfers between devices with their start and end apart: 52 -> 25, of which waited for: 15 -> 6; matrix products, arithmetic and copies ran while one was open for 41% -> 25% of each run, Pallas kernels for 36% -> 65%
where the time goes in v3:
time: 1150 us; the launch traced here: 1140 us
  Pallas kernels  759 us (66%)
  matrix products  223 us (19%)
  other arithmetic  56.2 us (5%)
  starting transfers between devices  41.3 us (4%)
  local copies, waits for them, and re-layouts  28.1 us (2%)
  waiting for transfers between devices  17.3 us (2%)
  between operations  15.2 us (1%)
    pallas_call x2, Pallas kernels, exchange_and_scatter(): pl.pallas_call(functools.partial(exchange_scatter_kernel, bits, count, le...  226 us
    dot_general x26, matrix products, dot(): return lax.dot_general(left, right, dims, preferred_element_type=F32)  218 us
    pallas_call x2, Pallas kernels, exchange_and_gather(): pl.pallas_call(functools.partial(exchange_kernel, bits, count), in_specs=...  151 us
    pallas_call x2, Pallas kernels, exchange_and_multiply(): pl.pallas_call(functools.partial(exchange_multiply_kernel, count, [job fo...  127 us
    pallas_call x4, Pallas kernels, feed(): pl.pallas_call(feed_kernel, grid=(tiles,), in_specs=[pl.BlockSpec((rows,...  84.7 us
    pallas_call x1, Pallas kernels, opening(): pl.pallas_call(functools.partial(opening_kernel, bits, count, len(cuts)),...  73.4 us
    pallas_call x1, Pallas kernels, attend_backward(): pl.pallas_call(functools.partial(attend_backward_kernel, sources), grid=(...  48.3 us
    pallas_call x1, Pallas kernels, attend_forward(): pl.pallas_call(functools.partial(attend_forward_kernel, sources), grid=(H...  32 us
  transfers between devices with their start and end apart: 25, of which 6 were waited for; matrix products, arithmetic and copies ran while one was open for 25% of the time, Pallas kernels for 65%

profile of v3, /device:TPU:0, one launch (start us, length us, event | category | flops | bytes accessed | tf_op | source)
XLA Modules:
  0.0 1139.7 jit_solution(10703681283893668000)
XLA Ops:
  25.6 73.4 %opening.1 = (bf16[4,256,2048]{2,1,0:T(8,128)(2,1)}, bf16[8,256,2048]{2,1,0:T(8,128)(2,1)}, bf16[256,4096]{1,0:T(8,128)(2,1)}, bf16[256,2048]{1,0:T(8,128)(2,1)}...) custom-call(bf16[256,2048]{1,0:T(8,128)(2,1)} %fusion.17.refs_0_, ...), custom_call_target="tpu_custom_call" | custom-call | tf_op jit(solution)/shard_map/opening/pallas_call | solution.py:511
  116.4 11.4 %convolution_convert_fusion.7.query_ref = bf16[768,2048]{1,0:T(8,128)(2,1)} fusion(bf16[768,2048]{1,0:T(8,128)(2,1)S(1)} %bitcast.243, bf16[2048,2048]{1,0:T(8,128)(2,1)} %bitcast.284), kind=kOutput, calls=%fused_computation.23 | convolution fusion | flops 6444023808 | bytes 14680064 | tf_op jit(solution)/shard_map/dot_general | solution.py:38
  137.3 23.0 %convolution_convert_fusion.1.key_ref.value_ref = bf16[1024,4096]{1,0:T(8,128)(2,1)} fusion(bf16[1024,2048]{1,0:T(8,128)(2,1)} %bitcast.241, bf16[2048,4096]{0,1:T(8,128)(2,1)} %all-gather.7.cloned.1.call-done), kind=kOutput, calls=%fused_computation.8 | convolution fusion | flops 17184063488 | bytes 29360128 | tf_op jit(solution)/shard_map/dot_general | solution.py:38
  160.3 32.0 %attend_forward.1 = (bf16[768,2048]{1,0:T(8,128)(2,1)}, f32[768,128]{1,0:T(8,128)}) custom-call(bf16[768,2048]{1,0:T(8,128)(2,1)} %convolution_convert_fusion.7.query_ref, bf16[1024,4096]{1,0:T(8,128)(2,1)} %convolution_convert_fusion.1.key_ref.value_ref, bf16[1024,4096]{1,0:T(8,128)(2,1)} %convolution_convert_fusion.1.key_ref.value_ref, ...), custom_call_target="tpu_custom_call" | custom-call | flops 4026531840 | bytes 14680064 | tf_op jit(solution)/shard_map/attend_forward/pallas_call | solution.py:93
  192.3 13.1 %fusion.5 = bf16[768,2048]{1,0:T(8,128)(2,1)} fusion(bf16[768,2048]{1,0:T(8,128)(2,1)} %get-tuple-element.83, bf16[1,2048,2048]{2,1,0:T(8,128)(2,1)} %all-gather.15.cloned.1.call-done), kind=kOutput, calls=%fused_computation.26 | convolution fusion | flops 6444023808 | bytes 14680064 | tf_op jit(solution)/shard_map/dot_general | solution.py:38
  205.5 69.2 %exchange_and_gather.2 = (bf16[4,192,2048]{2,1,0:T(8,128)(2,1)}, bf16[8,256,2048]{2,1,0:T(8,128)(2,1)}) custom-call(bf16[4,192,2048]{2,1,0:T(8,128)(2,1)} %bitcast.262, bf16[256,2048]{1,0:T(8,128)(2,1)} %get-tuple-element.84.shard_ref), custom_call_target="tpu_custom_call" | custom-call | tf_op jit(solution)/shard_map/exchange_and_gather/pallas_call | solution.py:577
  283.1 81.9 %exchange_and_gather.3 = (bf16[4,192,2048]{2,1,0:T(8,128)(2,1)}, bf16[8,256,2048]{2,1,0:T(8,128)(2,1)}) custom-call(bf16[4,192,2048]{2,1,0:T(8,128)(2,1)} %bitcast.245, bf16[256,2048]{1,0:T(8,128)(2,1)} %get-tuple-element.86.shard_ref), custom_call_target="tpu_custom_call" | custom-call | tf_op jit(solution)/shard_map/exchange_and_gather/pallas_call | solution.py:577
  370.2 16.5 %feed.4 = (bf16[768,1024]{1,0:T(8,128)(2,1)}, bf16[768,2048]{1,0:T(8,128)(2,1)}) custom-call(bf16[768,2048]{1,0:T(8,128)(2,1)} %bitcast.232, bf16[768,2048]{1,0:T(8,128)(2,1)} %bitcast.227, bf16[2048,2048]{1,0:T(8,128)(2,1)} %bitcast.251, bf16[5632,2048]{1,0:T(8,128)(2,1)} %all-gather.9.cloned.1.call-done.down_ref.refs_2_), custom_call_target="tpu_custom_call" | custom-call | flops 9663676416 | bytes 18874368 | tf_op jit(solution)/shard_map/feed/pallas_call | solution.py:227
  386.7 11.7 %fusion.101 = f32[768,2048]{1,0:T(8,128)} fusion(bf16[768,2048]{1,0:T(8,128)(2,1)} %get-tuple-element.95, bf16[2048,2048]{1,0:T(8,128)(2,1)} %bitcast.252), kind=kOutput, calls=%fused_computation.202 | convolution fusion | flops 6442450944 | bytes 17825792 | tf_op jit(solution)/shard_map/dot_general | solution.py:38
  398.5 16.7 %feed.5 = (bf16[768,1024]{1,0:T(8,128)(2,1)}, bf16[768,2048]{1,0:T(8,128)(2,1)}) custom-call(bf16[768,2048]{1,0:T(8,128)(2,1)} %bitcast.233, bf16[768,2048]{1,0:T(8,128)(2,1)} %bitcast.228, bf16[2048,2048]{1,0:T(8,128)(2,1)} %bitcast.253, bf16[5632,2048]{1,0:T(8,128)(2,1)} %all-gather.9.cloned.1.call-done.down_ref.refs_2_), custom_call_target="tpu_custom_call" | custom-call | flops 9663676416 | bytes 18874368 | tf_op jit(solution)/shard_map/feed/pallas_call | solution.py:227
  415.2 13.6 %convolution_add_fusion.1 = f32[768,2048]{1,0:T(8,128)} fusion(f32[768,2048]{1,0:T(8,128)} %fusion.101, bf16[768,2048]{1,0:T(8,128)(2,1)} %get-tuple-element.94, bf16[2048,2048]{1,0:T(8,128)(2,1)} %bitcast.254), kind=kOutput, calls=%fused_computation.21 | convolution fusion | flops 6444023808 | bytes 24117248 | tf_op jit(solution)/shard_map/dot_general | solution.py:38
  428.8 5.1 convolution_convert_fusion.2
  439.4 7.5 convolution_convert_fusion.5
  451.9 8.0 all-gather.11.cloned.1.call-done.gate_up_ref
  459.9 27.1 %feed.6 = (bf16[768,2048]{1,0:T(8,128)(2,1)}, bf16[768,4096]{1,0:T(8,128)(2,1)}) custom-call(bf16[768,2048]{1,0:T(8,128)(2,1)} %bitcast.234, bf16[768,2048]{1,0:T(8,128)(2,1)} %bitcast.229, bf16[2048,4096]{1,0:T(8,128)(2,1)} %all-gather.11.cloned.1.call-done.gate_up_ref, bf16[5632,2048]{1,0:T(8,128)(2,1)} %all-gather.9.cloned.1.call-done.down_ref.refs_2_), custom_call_target="tpu_custom_call" | custom-call | flops 19327352832 | bytes 31457280 | tf_op jit(solution)/shard_map/feed/pallas_call | solution.py:227
  487.1 6.7 fusion.27
  493.8 6.6 fusion.26
  500.4 21.6 %convolution_add_fusion = f32[768,2048]{1,0:T(8,128)} fusion(f32[768,2048]{1,0:T(8,128)} %convolution_add_fusion.1, bf16[768,4096]{1,0:T(8,128)(2,1)} %get-tuple-element.105, bf16[2048,4096]{1,0:T(8,128)(2,1)} %all-gather.11.cloned.1.call-done.gate_up_ref), kind=kOutput, calls=%fused_computation.16 | convolution fusion | flops 12886474752 | bytes 35651584 | tf_op jit(solution)/shard_map/dot_general | solution.py:38
  522.0 18.8 %convolution_convert_fusion = bf16[2048,4096]{1,0:T(8,128)(2,1)} fusion(bf16[768,2048]{1,0:T(8,128)(2,1)S(1)} %bitcast.238, bf16[768,4096]{1,0:T(8,128)(2,1)} %get-tuple-element.105), kind=kOutput, calls=%fused_computation | convolution fusion | flops 12893290496 | bytes 26214400 | tf_op jit(solution)/shard_map/dot_general | solution.py:38
  547.9 24.4 %feed.7 = (bf16[768,1536]{1,0:T(8,128)(2,1)}, bf16[768,3072]{1,0:T(8,128)(2,1)}) custom-call(bf16[768,2048]{1,0:T(8,128)(2,1)} %bitcast.235, bf16[768,2048]{1,0:T(8,128)(2,1)} %bitcast.230, bf16[2048,3072]{1,0:T(8,128)(2,1)} %all-gather.13.cloned.1.call-done.gate_up_ref, bf16[5632,2048]{1,0:T(8,128)(2,1)} %all-gather.9.cloned.1.call-done.down_ref.refs_2_), custom_call_target="tpu_custom_call" | custom-call | flops 14495514624 | bytes 25165824 | tf_op jit(solution)/shard_map/feed/pallas_call | solution.py:227
  575.7 15.7 %add_convert_fusion.1 = bf16[768,2048]{1,0:T(8,128)(2,1)} fusion(f32[768,2048]{1,0:T(8,128)} %convolution_add_fusion, bf16[768,3072]{1,0:T(8,128)(2,1)S(1)} %copy-done.63, bf16[2048,3072]{1,0:T(8,128)(2,1)} %all-gather.13.cloned.1.call-done.gate_up_ref), kind=kOutput, calls=%fused_computation.10 | convolution fusion | flops 9666822144 | bytes 26738688 | tf_op jit(solution)/shard_map/dot_general | solution.py:38
  591.4 55.6 %exchange_and_multiply.2 = (bf16[4,192,2048]{2,1,0:T(8,128)(2,1)}, bf16[5632,2048]{1,0:T(8,128)(2,1)}, bf16[2048,3072]{1,0:T(8,128)(2,1)}) custom-call(bf16[4,192,2048]{2,1,0:T(8,128)(2,1)} %bitcast.287, bf16[768,5632]{1,0:T(8,128)(2,1)} %constant_dynamic-update-slice_fusion.refs_1_, bf16[768,2048]{1,0:T(8,128)(2,1)} %bitcast.231, ...), custom_call_target="tpu_custom_call" | custom-call | flops 27380416512 | bytes 6291456 | tf_op jit(solution)/shard_map/exchange_and_multiply/pallas_call | solution.py:670
  660.6 71.4 %exchange_and_multiply.3 = (bf16[4,192,2048]{2,1,0:T(8,128)(2,1)}, bf16[768,2048]{1,0:T(8,128)(2,1)}) custom-call(bf16[4,192,2048]{2,1,0:T(8,128)(2,1)} %bitcast.263, bf16[768,5632]{1,0:T(8,128)(2,1)} %constant_dynamic-update-slice_fusion.refs_1_, bf16[5632,2048]{1,0:T(8,128)(2,1)} %all-gather.9.cloned.1.call-done.down_ref.refs_2_), custom_call_target="tpu_custom_call" | custom-call | flops 17716740096 | bytes 6291456 | tf_op jit(solution)/shard_map/exchange_and_multiply/pallas_call | solution.py:670
  742.0 10.2 fusion.8.grad_ref
  752.3 20.0 %all-to-all-start.1 = ((bf16[4,192,2048]{2,1,0:T(8,128)(2,1)}), bf16[4,192,2048]{2,1,0:T(8,128)(2,1)S(1)}, u32[]{:S(2)}, u32[]{:S(2)}) async-start(bf16[4,192,2048]{2,1,0:T(8,128)(2,1)} %bitcast.261), calls=%async_computation.1 | async-start | bytes 6291456 | tf_op jit(solution)/shard_map/all_to_all | solution.py:978
  772.4 48.3 %attend_backward.1 = (bf16[768,2048]{1,0:T(8,128)(2,1)}, bf16[1024,4096]{1,0:T(8,128)(2,1)}) custom-call(bf16[768,2048]{1,0:T(8,128)(2,1)} %convolution_convert_fusion.7.query_ref, bf16[1024,4096]{1,0:T(8,128)(2,1)} %convolution_convert_fusion.1.key_ref.value_ref, bf16[1024,4096]{1,0:T(8,128)(2,1)} %convolution_convert_fusion.1.key_ref.value_ref, ...), custom_call_target="tpu_custom_call" | custom-call | flops 10066329600 | bytes 29360128 | tf_op jit(solution)/shard_map/attend_backward/pallas_call | solution.py:174
  820.7 10.2 convolution_convert_fusion.6
  834.3 21.6 %fusion = bf16[1024,2048]{1,0:T(8,128)(2,1)} fusion(f32[4,256,2048]{2,1,0:T(8,128)S(1)} %fusion.43, bf16[1024,4096]{1,0:T(8,128)(2,1)S(1)} %copy-done.62, bf16[2048,4096]{0,1:T(8,128)(2,1)} %all-gather.7.cloned.1.call-done), kind=kOutput, calls=%fused_computation.2 | convolution fusion | flops 17184063488 | bytes 37748736 | tf_op jit(solution)/shard_map/dot_general | solution.py:38
  856.0 133.4 %exchange_and_scatter.1 = (bf16[4,256,2048]{2,1,0:T(8,128)(2,1)}, bf16[256,4096]{1,0:T(8,128)(2,1)}) custom-call(bf16[4,256,2048]{2,1,0:T(8,128)(2,1)} %bitcast.286, bf16[1024,1024]{1,0:T(8,128)(2,1)} %get-tuple-element.159.refs_1_, bf16[1024,1024]{1,0:T(8,128)(2,1)} %get-tuple-element.158.refs_2_, bf16[1024,4096]{1,0:T(8,128)(2,1)} %get-tuple-element.123.refs_3_), custom_call_target="tpu_custom_call" | custom-call | flops 34359738368 | tf_op jit(solution)/shard_map/exchange_and_scatter/pallas_call | solution.py:840
  1008.4 92.4 %scatter.1 = bf16[256,4096]{1,0:T(8,128)(2,1)} custom-call(bf16[768,1024]{1,0:T(8,128)(2,1)} %get-tuple-element.179.refs_0_, bf16[768,1024]{1,0:T(8,128)(2,1)} %get-tuple-element.178.refs_1_, bf16[768,1024]{1,0:T(8,128)(2,1)} %get-tuple-element.169.refs_2_, bf16[768,1024]{1,0:T(8,128)(2,1)} %get-tuple-element.168.refs_3_, ...), custom_call_target="tpu_custom_call" | custom-call | tf_op jit(solution)/shard_map/scatter/pallas_call | solution.py:840
  1107.9 7.1 transpose.38
  1123.5 9.2 assemble.1
  (271 shorter events, 140.7 us)
Async XLA Ops:
  7.2 130.1 %all-gather.7.cloned.1.call-start = ((), (), s32[]{:S(2)}) async-start(), calls=%async_computation.5 | async-start | bytes 18874368 | tf_op jit(solution)/shard_map/all_gather | solution.py:1029
  11.1 181.2 %all-gather.15.cloned.1.call-start = ((), (), s32[]{:S(2)}) async-start(), calls=%async_computation.13 | async-start | bytes 9437184 | tf_op jit(solution)/shard_map/all_gather | solution.py:1029
  13.1 357.1 %all-gather.9.cloned.1.call-start = ((), (), s32[]{:S(2)}) async-start(), calls=%async_computation.6 | async-start | bytes 25952256 | tf_op jit(solution)/shard_map/all_gather | solution.py:1029
  13.2 3.2 collective-permute-start
  16.4 4.1 collective-permute-start.1
  20.6 3.7 collective-permute-start.2
  22.7 76.4 %copy-start.51 = (f32[256]{0:T(256)}, f32[256]{0:T(256)S(1)}, u32[]{:S(2)}) copy-start(f32[256]{0:T(256)S(1)} %add_rsqrt_fusion.1) | copy-start | bytes 3076
  24.3 74.7 %copy-start.40 = (f32[1,2048]{1,0:T(1,128)}, f32[1,2048]{1,0:T(1,128)S(1)}, u32[]{:S(2)}) copy-start(f32[1,2048]{1,0:T(1,128)S(1)} %get-tuple-element.201) | copy-start | bytes 24580
  24.3 254.7 %copy-start.38 = (f32[1,2048]{1,0:T(1,128)}, f32[1,2048]{1,0:T(1,128)S(1)}, u32[]{:S(2)}) copy-start(f32[1,2048]{1,0:T(1,128)S(1)} %get-tuple-element.200) | copy-start | bytes 24580
  99.2 360.8 %all-gather.11.cloned.1.call-start = ((), (), s32[]{:S(2)}) async-start(), calls=%async_computation.7 | async-start | bytes 18874368 | tf_op jit(solution)/shard_map/all_gather | solution.py:1029
  109.4 82.9 %all-to-all-start = ((bf16[4,192,2048]{2,1,0:T(8,128)(2,1)}), bf16[4,192,2048]{2,1,0:T(8,128)(2,1)S(1)}, u32[]{:S(2)}, u32[]{:S(2)}) async-start(bf16[4,192,2048]{2,1,0:T(8,128)(2,1)} %bitcast.246), calls=%async_computation | async-start | bytes 6291456 | tf_op jit(solution)/shard_map/all_to_all | solution.py:978
  113.1 434.8 %all-gather.13.cloned.1.call-start = ((), (), s32[]{:S(2)}) async-start(), calls=%async_computation.8 | async-start | bytes 14155776 | tf_op jit(solution)/shard_map/all_gather | solution.py:1029
  127.9 728.1 %reduce-scatter.4.cloned.1.call-start = ((), (), s32[]{:S(2)}) async-start(), calls=%async_computation.9 | async-start | bytes 18874368 | tf_op jit(solution)/shard_map/reduce_scatter | solution.py:1134
  279.0 86.0 %copy-start.47 = (f32[256]{0:T(256)}, f32[256]{0:T(256)S(1)}, u32[]{:S(2)}) copy-start(f32[256]{0:T(256)S(1)} %add_rsqrt_fusion) | copy-start | bytes 3076
  283.1 81.9 %copy-start.29 = (bf16[768,2048]{1,0:T(8,128)(2,1)S(1)}, bf16[768,2048]{1,0:T(8,128)(2,1)}, u32[]{:S(2)}) copy-start(bf16[768,2048]{1,0:T(8,128)(2,1)} %get-tuple-element.83) | copy-start | bytes 9437188
  433.9 53.2 %collective-permute-start.4 = (bf16[1024,2048]{1,0:T(8,128)(2,1)}, bf16[1024,2048]{1,0:T(8,128)(2,1)}, u32[]{:S(2)}, u32[]{:S(2)}) collective-permute-start(bf16[1024,2048]{1,0:T(8,128)(2,1)} %convolution_convert_fusion.2), channel_id=1, source_target_pairs={{0,4},{4,0},{8,12},{12,8},{16,20},{20,16},{24,28},{28,24},{1,5},{5... | collective-permute-start | bytes 12582920 | tf_op jit(solution)/shard_map/ppermute | solution.py:892
  439.4 47.6 %collective-permute-start.3 = (bf16[1024,2048]{1,0:T(8,128)(2,1)}, bf16[1024,2048]{1,0:T(8,128)(2,1)}, u32[]{:S(2)}, u32[]{:S(2)}) collective-permute-start(bf16[1024,2048]{1,0:T(8,128)(2,1)} %convolution_convert_fusion.4), channel_id=1, source_target_pairs={{0,4},{4,0},{8,12},{12,8},{16,20},{20,16},{24,28},{28,24},{1,5},{5... | collective-permute-start | bytes 12582920 | tf_op jit(solution)/shard_map/ppermute | solution.py:892
  540.9 315.1 %reduce-scatter.6.cloned.1.call-start = ((), (), s32[]{:S(2)}) async-start(), calls=%async_computation.10 | async-start | bytes 25952256 | tf_op jit(solution)/shard_map/reduce_scatter | solution.py:1142
  647.0 349.0 %reduce-scatter.8.cloned.1.call-start = ((), (), s32[]{:S(2)}) async-start(), calls=%async_computation.12 | async-start | bytes 14155776 | tf_op jit(solution)/shard_map/reduce_scatter | solution.py:1143
  647.5 84.6 %collective-permute-start.5 = (bf16[2,256,2048]{2,1,0:T(8,128)(2,1)}, bf16[2,256,2048]{2,1,0:T(8,128)(2,1)}, u32[]{:S(2)}, u32[]{:S(2)}) collective-permute-start(bf16[2,256,2048]{2,1,0:T(8,128)(2,1)} %get-tuple-element.153), channel_id=1, source_target_pairs={{0,8},{4,12},{8,0},{12,4},{16,24},{20,28},{24,16},{28,20},{1,9},{5... | collective-permute-start | bytes 6291464 | tf_op jit(solution)/shard_map/ppermute | solution.py:892
  649.0 83.0 %collective-permute-start.6 = (bf16[2,256,2048]{2,1,0:T(8,128)(2,1)}, bf16[2,256,2048]{2,1,0:T(8,128)(2,1)}, u32[]{:S(2)}, u32[]{:S(2)}) collective-permute-start(bf16[2,256,2048]{2,1,0:T(8,128)(2,1)} %get-tuple-element.151), channel_id=1, source_target_pairs={{0,16},{4,20},{8,24},{12,28},{16,0},{20,4},{24,8},{28,12},{1,17},{... | collective-permute-start | bytes 6291464 | tf_op jit(solution)/shard_map/ppermute | solution.py:892
  660.6 71.5 %copy-start.20 = (bf16[2,256,2048]{2,1,0:T(8,128)(2,1)S(1)}, bf16[2,256,2048]{2,1,0:T(8,128)(2,1)}, u32[]{:S(2)}) copy-start(bf16[2,256,2048]{2,1,0:T(8,128)(2,1)} %get-tuple-element.115) | copy-start | bytes 6291460
  736.0 260.1 %collective-permute-start.12 = (bf16[256,2048]{1,0:T(8,128)(2,1)}, bf16[256,2048]{1,0:T(8,128)(2,1)}, u32[]{:S(2)}, u32[]{:S(2)}) collective-permute-start(bf16[256,2048]{1,0:T(8,128)(2,1)} %get-tuple-element.156), channel_id=1, source_target_pairs={{0,16},{4,20},{8,24},{12,28},{16,0},{20,4},{24,8},{28,12},{1,17},{... | collective-permute-start | bytes 3145736 | tf_op jit(solution)/shard_map/ppermute | solution.py:892
  741.6 254.5 %collective-permute-start.13 = (bf16[256,2048]{1,0:T(8,128)(2,1)}, bf16[256,2048]{1,0:T(8,128)(2,1)}, u32[]{:S(2)}, u32[]{:S(2)}) collective-permute-start(bf16[256,2048]{1,0:T(8,128)(2,1)} %get-tuple-element.154), channel_id=1, source_target_pairs={{0,8},{4,12},{8,0},{12,4},{16,24},{20,28},{24,16},{28,20},{1,9},{5... | collective-permute-start | bytes 3145736 | tf_op jit(solution)/shard_map/ppermute | solution.py:892
  752.3 103.6 %all-to-all-start.1 = ((bf16[4,192,2048]{2,1,0:T(8,128)(2,1)}), bf16[4,192,2048]{2,1,0:T(8,128)(2,1)S(1)}, u32[]{:S(2)}, u32[]{:S(2)}) async-start(bf16[4,192,2048]{2,1,0:T(8,128)(2,1)} %bitcast.261), calls=%async_computation.1 | async-start | bytes 6291456 | tf_op jit(solution)/shard_map/all_to_all | solution.py:978
  772.3 335.7 %all-reduce.2.cloned.1.call-start = ((), (), s32[]{:S(2)}) async-start(), calls=%async_computation.11 | async-start | bytes 4194304 | tf_op jit(solution)/shard_map/psum | solution.py:1181
  855.9 133.4 %copy-start.8 = (bf16[4,192,2048]{2,1,0:T(8,128)(2,1)}, bf16[4,192,2048]{2,1,0:T(8,128)(2,1)S(1)}, u32[]{:S(2)}) copy-start(bf16[4,192,2048]{2,1,0:T(8,128)(2,1)S(1)} %all-to-all-done.1) | copy-start | bytes 9437188
  994.8 3.7 collective-permute-start.7
  998.6 3.7 collective-permute-start.8
  1002.2 1.2 collective-permute-start.9
  1003.4 97.4 %collective-permute-start.10 = (f32[2,256]{1,0:T(2,128)S(1)}, f32[2,256]{1,0:T(2,128)S(1)}, u32[]{:S(2)}, u32[]{:S(2)}) collective-permute-start(f32[2,256]{1,0:T(2,128)S(1)} %fusion.87), channel_id=1, source_target_pairs={{0,1},{1,0},{2,3},{3,2},{4,5},{5,4},{6,7},{7,6},{8,9},{9,8},{10,11... | collective-permute-start | bytes 6152 | tf_op jit(solution)/shard_map/ppermute | solution.py:1220
  1100.8 6.5 collective-permute-start.11
  (57 other events, 363.3 us)
Sparse Core Ops, SparseCore 0:
  11.2 121.9 all-gather.6
  135.7 54.3 all-gather.14
  192.0 176.2 all-gather.8
  370.0 89.8 all-gather.10
  461.7 72.1 all-gather.12
  541.0 120.7 reduce-scatter.3
  665.4 169.5 reduce-scatter.5
  838.4 134.7 reduce-scatter.7
  996.2 86.7 all-reduce.1

commit v4 on v3

--- a/solution.py
+++ b/solution.py
@@ -21,6 +21,7 @@
 F32 = jnp.float32
 VMEM_BYTES = 56 * 2**20
 TILE = 512
+NO_COST = pl.CostEstimate(flops=0, bytes_accessed=0, transcendentals=0)
 
 
 def normalize(values):
@@ -89,7 +90,6 @@
 def attend_forward(queries, keys_values, bounds, sources):
     rows, features = queries.shape
     seq = keys_values.shape[0]
-    pairs = (sources + 1) / (2 * sources)
     return pl.pallas_call(
         functools.partial(attend_forward_kernel, sources),
         grid=(HEADS,),
@@ -108,11 +108,7 @@
             jax.ShapeDtypeStruct((rows, 128), F32),
         ],
         compiler_params=pltpu.CompilerParams(vmem_limit_bytes=VMEM_BYTES),
-        cost_estimate=pl.CostEstimate(
-            flops=int(4 * rows * seq * features * pairs),
-            bytes_accessed=4 * (rows + seq) * features,
-            transcendentals=int(HEADS * rows * seq * pairs),
-        ),
+        cost_estimate=NO_COST,
         name="attend_forward",
     )(queries, keys_values, keys_values, bounds)
 
@@ -125,12 +121,42 @@
     grad_ref,
     bounds_ref,
     logsum_ref,
+    values_ref,
     grad_query_ref,
     grad_both_ref,
+    back_ref,
     key_total,
     value_total,
+    local,
+    sent,
+    got,
 ):
     head = pl.program_id(0)
+    me = lax.axis_index("grp")
+    place = lax.axis_index("ep")
+    others = [lax.rem(place + shift, sources) for shift in range(1, sources)]
+    columns = pl.ds(0, back_ref.shape[2])
+    copies = [
+        pltpu.make_async_remote_copy(
+            src_ref=values_ref.at[other, :, columns],
+            dst_ref=back_ref.at[place],
+            send_sem=sent.at[index],
+            recv_sem=got.at[index],
+            device_id=(me, other),
+            device_id_type=MESH,
+        )
+        for index, other in enumerate(others)
+    ]
+    copies.append(
+        pltpu.make_async_copy(values_ref.at[place, :, columns], back_ref.at[place], local)
+    )
+
+    @pl.when(head == 0)
+    def _():
+        pl.semaphore_wait(greet([(me, other) for other in others]), len(others))
+        for copy in copies:
+            copy.start()
+
     capacity = query_ref.shape[0] // sources
     tokens = key_ref.shape[0] // sources
     scaling = HEAD_DIM ** (-0.5)
@@ -165,13 +191,20 @@
     grad_both_ref[:, :HEAD_DIM] = (key_total[...] * scaling).astype(BF16)
     grad_both_ref[:, HEAD_DIM:] = value_total[...].astype(BF16)
 
-
-def attend_backward(queries, keys_values, grads, bounds, logsums, sources):
+    @pl.when(head == HEADS - 1)
+    def _():
+        for copy in copies:
+            copy.wait()
+
+
+def attend_backward(
+    queries, keys_values, grads, bounds, logsums, values, sources, collective_id
+):
     rows = queries.shape[0]
     features = HEADS * HEAD_DIM
     seq = keys_values.shape[0]
-    pairs = (sources + 1) / (2 * sources)
-    return pl.pallas_call(
+    shape = (sources, values.shape[0] // sources, values.shape[1])
+    grad_queries, grad_both, back = pl.pallas_call(
         functools.partial(attend_backward_kernel, sources),
         grid=(HEADS,),
         in_specs=[
@@ -181,27 +214,35 @@
             pl.BlockSpec((rows, HEAD_DIM), lambda h: (0, h)),
             pl.BlockSpec((rows, 2), lambda h: (0, 0)),
             pl.BlockSpec((rows, 128), lambda h: (0, 0)),
+            pl.BlockSpec(memory_space=pl.ANY),
         ],
         out_specs=[
             pl.BlockSpec((rows, HEAD_DIM), lambda h: (0, h)),
             pl.BlockSpec((seq, 2 * HEAD_DIM), lambda h: (0, h)),
+            pl.BlockSpec(memory_space=pl.ANY),
         ],
         out_shape=[
             jax.ShapeDtypeStruct((rows, features), BF16),
             jax.ShapeDtypeStruct((seq, 2 * features), BF16),
-        ],
-        scratch_shapes=[pltpu.VMEM((seq, HEAD_DIM), F32), pltpu.VMEM((seq, HEAD_DIM), F32)],
-        compiler_params=pltpu.CompilerParams(vmem_limit_bytes=VMEM_BYTES),
-        cost_estimate=pl.CostEstimate(
-            flops=int(10 * rows * seq * features * pairs),
-            bytes_accessed=8 * (rows + seq) * features,
-            transcendentals=int(HEADS * rows * seq * pairs),
+            jax.ShapeDtypeStruct((*shape[:2], shape[2] // 2), BF16),
+        ],
+        scratch_shapes=[
+            pltpu.VMEM((seq, HEAD_DIM), F32),
+            pltpu.VMEM((seq, HEAD_DIM), F32),
+            pltpu.SemaphoreType.DMA,
+            *[pltpu.SemaphoreType.DMA((sources - 1,))] * 2,
+        ],
+        compiler_params=pltpu.CompilerParams(
+            collective_id=collective_id, has_side_effects=True, vmem_limit_bytes=VMEM_BYTES
         ),
+        cost_estimate=NO_COST,
         name="attend_backward",
-    )(queries, keys_values, keys_values, grads, bounds, logsums)
-
-
-def feed_kernel(in_ref, grad_ref, gate_up_ref, down_ref, act_ref, grad_gate_up_ref):
+    )(queries, keys_values, keys_values, grads, bounds, logsums, values.reshape(shape))
+    return grad_queries, grad_both, back.reshape(values.shape[0], -1)
+
+
+def feed_kernel(in_ref, grad_ref, gate_up_ref, down_ref, *refs):
+    act_ref, grad_gate_up_ref = refs[-2:]
     units = down_ref.shape[0]
     step = units // 2
     for start in range(0, units, step):
@@ -219,11 +260,12 @@
         grad_gate_up_ref[:, there] = (grad_act * silu).astype(BF16)
 
 
-def feed(inputs, grads, gate_up, down, offset):
+def feed(inputs, grads, gate_up, down, offset, acts=None):
     rows, width = inputs.shape
     units = gate_up.shape[1] // 2
     tiles = units // TILE
     start = offset // TILE
+    before = [] if acts is None else [acts]
     return pl.pallas_call(
         feed_kernel,
         grid=(tiles,),
@@ -232,23 +274,70 @@
             pl.BlockSpec((rows, width), lambda j: (0, 0)),
             pl.BlockSpec((width, 2 * TILE), lambda j: (0, j)),
             pl.BlockSpec((TILE, width), lambda j: (j + start, 0)),
-        ],
+        ]
+        + [pl.BlockSpec(memory_space=pl.ANY)] * len(before),
         out_specs=[
-            pl.BlockSpec((rows, TILE), lambda j: (0, j)),
+            pl.BlockSpec((rows, TILE), lambda j: (0, j + start)),
             pl.BlockSpec((rows, 2 * TILE), lambda j: (0, j)),
         ],
         out_shape=[
-            jax.ShapeDtypeStruct((rows, units), BF16),
+            jax.ShapeDtypeStruct((rows, down.shape[0]), BF16),
             jax.ShapeDtypeStruct((rows, 2 * units), BF16),
         ],
+        input_output_aliases={4: 0} if before else {},
         compiler_params=pltpu.CompilerParams(vmem_limit_bytes=VMEM_BYTES),
-        cost_estimate=pl.CostEstimate(
-            flops=6 * rows * width * units,
-            bytes_accessed=6 * width * units + 4 * rows * width,
-            transcendentals=rows * units,
-        ),
+        cost_estimate=NO_COST,
         name="feed",
-    )(inputs, grads, gate_up, down)
+    )(inputs, grads, gate_up, down, *before)
+
+
+def back_kernel(grad_ref, weight_ref, *refs):
+    *before, out_ref = refs
+    value = dot(grad_ref[...], weight_ref[...], CONTRACT_COLUMNS)
+    for ref in before:
+        value = value + ref[...]
+    out_ref[...] = value.astype(out_ref.dtype)
+
+
+def back(grads, weights, total, dtype):
+    (rows, depth), columns = grads.shape, weights.shape[0]
+    before = [] if total is None else [total]
+    return pl.pallas_call(
+        back_kernel,
+        grid=(columns // TILE,),
+        in_specs=[
+            pl.BlockSpec((rows, depth), lambda j: (0, 0)),
+            pl.BlockSpec((TILE, depth), lambda j: (j, 0)),
+        ]
+        + [pl.BlockSpec((rows, TILE), lambda j: (0, j))] * len(before),
+        out_specs=pl.BlockSpec((rows, TILE), lambda j: (0, j)),
+        out_shape=jax.ShapeDtypeStruct((rows, columns), dtype),
+        compiler_params=pltpu.CompilerParams(vmem_limit_bytes=VMEM_BYTES),
+        cost_estimate=NO_COST,
+        name="back",
+    )(grads, weights, *before)
+
+
+def weight_kernel(left_ref, right_ref, out_ref):
+    out_ref[...] = dot(left_ref[...], right_ref[...], CONTRACT_ROWS).astype(BF16)
+
+
+def weight_product(left, right):
+    (rows, columns), width = left.shape, right.shape[1]
+    tile = TILE // 2
+    return pl.pallas_call(
+        weight_kernel,
+        grid=(columns // tile,),
+        in_specs=[
+            pl.BlockSpec((rows, tile), lambda j: (0, j)),
+            pl.BlockSpec((rows, width), lambda j: (0, 0)),
+        ],
+        out_specs=pl.BlockSpec((tile, width), lambda j: (j, 0)),
+        out_shape=jax.ShapeDtypeStruct((columns, width), BF16),
+        compiler_params=pltpu.CompilerParams(vmem_limit_bytes=VMEM_BYTES),
+        cost_estimate=NO_COST,
+        name="weight_product",
+    )(left, right)
 
 
 def assemble_kernel(counts, *refs):
@@ -279,9 +368,7 @@
         out_specs=pl.BlockSpec((step, columns), lambda i: (i, 0)),
         out_shape=jax.ShapeDtypeStruct((rows, columns), F32),
         compiler_params=pltpu.CompilerParams(vmem_limit_bytes=VMEM_BYTES),
-        cost_estimate=pl.CostEstimate(
-            flops=0, bytes_accessed=6 * rows * columns, transcendentals=0
-        ),
+        cost_estimate=NO_COST,
         name="assemble",
     )(*arrays)
 
@@ -306,9 +393,7 @@
         in_specs=[pl.BlockSpec((rows, 2 * TILE), lambda j: (0, j % steps))],
         out_specs=pl.BlockSpec((TILE, rows), lambda j: (j, 0)),
         out_shape=jax.ShapeDtypeStruct((columns, rows), F32),
-        cost_estimate=pl.CostEstimate(
-            flops=0, bytes_accessed=6 * rows * columns, transcendentals=0
-        ),
+        cost_estimate=NO_COST,
         name="transpose",
     )(values)
 
@@ -526,6 +611,7 @@
         compiler_params=pltpu.CompilerParams(
             collective_id=0, has_side_effects=True, vmem_limit_bytes=VMEM_BYTES
         ),
+        cost_estimate=NO_COST,
         name="opening",
     )(tokens, shard, gate_up, down)
     return whole, full.reshape(-1, full.shape[2]), lows[:-1], lows[-1]
@@ -588,6 +674,7 @@
             *weight_gather_semaphores(groups),
         ],
         compiler_params=pltpu.CompilerParams(collective_id=collective_id, has_side_effects=True),
+        cost_estimate=NO_COST,
         name="exchange_and_gather",
     )(values.reshape(shape), shard)
     return back.reshape(rows, width), full.reshape(-1, full.shape[2])
@@ -625,15 +712,20 @@
     )(left_ref, right_ref, out_ref)
 
 
-def exchange_multiply_kernel(count, jobs, *refs):
+def exchange_multiply_kernel(count, jobs, bits, *refs):
     values_ref, refs = refs[0], refs[1:]
     given, refs = refs[: 2 * len(jobs)], refs[2 * len(jobs) :]
-    back_ref, *made, local, sent, got = refs
+    passed, refs = refs[: len(bits)], refs[len(bits) :]
+    back_ref, refs = refs[0], refs[1:]
+    made, refs = refs[: len(jobs)], refs[len(jobs) :]
+    taken, refs = refs[: len(bits)], refs[len(bits) :]
+    local, sent, got, pass_sent, pass_got = refs
     me = lax.axis_index("grp")
     place = lax.axis_index("ep")
     others = [lax.rem(place + shift, count) for shift in range(1, count)]
-    barrier = greet([(me, other) for other in others])
-    pl.semaphore_wait(barrier, count - 1)
+    across = [(me ^ (1 << bit), place) for bit in sorted(set(bits))]
+    barrier = greet([(me, other) for other in others] + across)
+    pl.semaphore_wait(barrier, len(others) + len(across))
     copies = [
         pltpu.make_async_remote_copy(
             src_ref=values_ref.at[other],
@@ -645,56 +737,76 @@
         )
         for index, other in enumerate(others)
     ]
-    own = pltpu.make_async_copy(values_ref.at[place], back_ref.at[place], local)
+    copies += [
+        pltpu.make_async_remote_copy(
+            src_ref=passed[index],
+            dst_ref=taken[index],
+            send_sem=pass_sent.at[index],
+            recv_sem=pass_got.at[index],
+            device_id=(me ^ (1 << bit), place),
+            device_id_type=MESH,
+        )
+        for index, bit in enumerate(bits)
+    ]
+    copies.append(pltpu.make_async_copy(values_ref.at[place], back_ref.at[place], local))
     for copy in copies:
         copy.start()
-    own.start()
     for index, job in enumerate(jobs):
         job(given[2 * index], given[2 * index + 1], made[index])
     for copy in copies:
         copy.wait()
-    own.wait()
-
-
-def exchange_and_multiply(values, jobs, collective_id):
+
+
+def exchange_and_multiply(values, jobs, scatters, collective_id):
     count = lax.axis_size("ep")
     rows, width = values.shape
     shape = (count, rows // count, width)
-    outs, flops = [], 0
+    outs = []
     for job, left, right in jobs:
         by_rows = job is multiply_rows
         outs.append(
             jax.ShapeDtypeStruct((left.shape[0 if by_rows else 1], right.shape[1]), BF16)
         )
-        flops += 2 * left.shape[0] * left.shape[1] * right.shape[1]
+    passed = [scatter.sent for scatter in scatters]
+    outs += [jax.ShapeDtypeStruct(array.shape, BF16) for array in passed]
     back, *made = pl.pallas_call(
-        functools.partial(exchange_multiply_kernel, count, [job for job, _, _ in jobs]),
-        in_specs=[pl.BlockSpec(memory_space=pl.ANY)] * (1 + 2 * len(jobs)),
-        out_specs=[pl.BlockSpec(memory_space=pl.ANY)] * (1 + len(jobs)),
+        functools.partial(
+            exchange_multiply_kernel,
+            count,
+            [job for job, _, _ in jobs],
+            [scatter.bit for scatter in scatters],
+        ),
+        in_specs=[pl.BlockSpec(memory_space=pl.ANY)] * (1 + 2 * len(jobs) + len(passed)),
+        out_specs=[pl.BlockSpec(memory_space=pl.ANY)] * (1 + len(outs)),
         out_shape=[jax.ShapeDtypeStruct(shape, BF16), *outs],
         scratch_shapes=[
             pltpu.SemaphoreType.DMA,
             *[pltpu.SemaphoreType.DMA((count - 1,))] * 2,
+            *[pltpu.SemaphoreType.DMA((max(len(passed), 1),))] * 2,
         ],
         compiler_params=pltpu.CompilerParams(
             collective_id=collective_id, has_side_effects=True, vmem_limit_bytes=VMEM_BYTES
         ),
-        cost_estimate=pl.CostEstimate(
-            flops=flops, bytes_accessed=4 * rows * width, transcendentals=0
-        ),
+        cost_estimate=NO_COST,
         name="exchange_and_multiply",
-    )(values.reshape(shape), *[array for _, left, right in jobs for array in (left, right)])
-    return back.reshape(rows, width), made
+    )(
+        values.reshape(shape),
+        *[array for _, left, right in jobs for array in (left, right)],
+        *passed,
+    )
+    for scatter, got in zip(scatters, made[len(jobs) :]):
+        scatter.receive(got)
+    return back.reshape(rows, width), made[: len(jobs)]
 
 
 def exchange_scatter_kernel(bits, count, lefts, sources, jobs, exchanged, *refs):
-    values_ref, refs = (refs[0], refs[1:]) if exchanged else (None, refs)
+    values_refs, refs = refs[:exchanged], refs[exchanged:]
     splits, refs = refs[: 2 * lefts], refs[2 * lefts :]
     many = 1 + sources[-1][1]
     rights, refs = refs[:many], refs[many:]
     inputs = sum(job.inputs for job in jobs)
     given, refs = refs[:inputs], refs[inputs:]
-    back_ref, refs = (refs[0], refs[1:]) if exchanged else (None, refs)
+    back_refs, refs = refs[:exchanged], refs[exchanged:]
     total_ref, *refs = refs
     made, refs = refs[: len(jobs)], refs[len(jobs) :]
     core_send, core_got, kept, *refs = refs
@@ -708,22 +820,28 @@
     near = [(me ^ (1 << bit), place) for bit in range(bits)]
     barrier = greet(near + [(me, other) for other in others])
     pl.semaphore_wait(barrier, len(near) + len(others))
-    copies = [
-        pltpu.make_async_remote_copy(
-            src_ref=values_ref.at[other],
-            dst_ref=back_ref.at[place],
-            send_sem=out_sent.at[index],
-            recv_sem=out_got.at[index],
-            device_id=(me, other),
-            device_id_type=MESH,
-        )
-        for index, other in enumerate(others)
-    ]
+    copies = []
+    for which, (values_ref, back_ref) in enumerate(zip(values_refs, back_refs)):
+        width = back_ref.shape[2]
+        columns = pl.ds(values_ref.shape[2] - width, width)
+        copies += [
+            pltpu.make_async_remote_copy(
+                src_ref=values_ref.at[other, :, columns],
+                dst_ref=back_ref.at[place],
+                send_sem=out_sent.at[which, index],
+                recv_sem=out_got.at[which, index],
+                device_id=(me, other),
+                device_id_type=MESH,
+            )
+            for index, other in enumerate(others)
+        ]
+        copies.append(
+            pltpu.make_async_copy(
+                values_ref.at[place, :, columns], back_ref.at[place], local.at[which]
+            )
+        )
     for copy in copies:
         copy.start()
-    if exchanged:
-        copies.append(pltpu.make_async_copy(values_ref.at[place], back_ref.at[place], local))
-        copies[-1].start()
 
     chunks, blocks, rows, width = kept.shape
     orders = list(range(1, bits)), list(range(1, bits))[::-1]
@@ -811,10 +929,10 @@
         copy.wait()
 
 
-def exchange_and_scatter(values, products, collective_id, jobs=(), costs=True):
+def exchange_and_scatter(values, products, collective_id, jobs=()):
     groups, count = lax.axis_size("grp"), lax.axis_size("ep")
     bits = groups.bit_length() - 1
-    exchanged = values is not None
+    exchanged = len(values)
     columns = 1024
     splits, rights, sources = [], [], []
     for split, right in products:
@@ -830,13 +948,12 @@
     stages = [pltpu.VMEM((chunks, blocks >> (at + 1), *block), BF16) for at in range(bits - 1)]
     vmem = pl.BlockSpec(memory_space=pltpu.VMEM)
     anywhere = pl.BlockSpec(memory_space=pl.ANY)
-    flops = 8 * splits[0][0].size * chunks * columns if costs else 0
     arrays = [array for _, inputs, _ in jobs for array in inputs]
-    back_shape = []
-    if exchanged:
-        rows, width = values.shape
-        values = values.reshape(count, rows // count, width)
-        back_shape = [jax.ShapeDtypeStruct(values.shape, BF16)]
+    given = [array.reshape(count, -1, array.shape[1]) for array, _ in values]
+    back_shape = [
+        jax.ShapeDtypeStruct((*array.shape[:2], width), BF16)
+        for array, (_, width) in zip(given, values)
+    ]
     outs = pl.pallas_call(
         functools.partial(
             exchange_scatter_kernel,
@@ -862,25 +979,24 @@
             buffer,
             *stages,
             *stages,
-            pltpu.SemaphoreType.DMA,
-            *[pltpu.SemaphoreType.DMA((count - 1,))] * 2,
+            pltpu.SemaphoreType.DMA((max(exchanged, 1),)),
+            *[pltpu.SemaphoreType.DMA((max(exchanged, 1), count - 1))] * 2,
             *[pltpu.SemaphoreType.DMA((chunks,))] * 2,
             *[pltpu.SemaphoreType.DMA((chunks, bits - 1))] * 2,
         ],
         compiler_params=pltpu.CompilerParams(
             collective_id=collective_id, has_side_effects=True, vmem_limit_bytes=60 * 2**20
         ),
-        cost_estimate=pl.CostEstimate(flops=flops, bytes_accessed=0, transcendentals=0),
+        cost_estimate=NO_COST,
         name="exchange_and_scatter" if exchanged else "scatter",
     )(
-        *([values] if exchanged else []),
+        *given,
         *[half for split in splits for half in split],
         *rights,
         *arrays,
     )
-    if exchanged:
-        return outs[0].reshape(rows, width), outs[1], outs[2:]
-    return None, outs[0], outs[1:]
+    backs = [out.reshape(-1, out.shape[2]) for out in outs[:exchanged]]
+    return backs, outs[exchanged], outs[exchanged + 1 :]
 
 
 def after(values, *tokens):
@@ -912,9 +1028,12 @@
         self.order = list(order)
 
     def step(self, *tokens):
-        if not self.order:
-            return
-        bit = self.order.pop(0)
+        if self.order:
+            self.prepare(*tokens)
+            self.receive(flip(self.sent, self.bit))
+
+    def prepare(self, *tokens):
+        self.bit = bit = self.order.pop(0)
         axis = sum(other > bit for other in self.order)
         mine = (lax.axis_index("grp") >> bit) & 1
         terms = self.terms
@@ -925,8 +1044,10 @@
             return lax.dynamic_index_in_dim(term, which, axis, keepdims=False)
 
         self.sent = sum(part(term, 1 - mine).astype(F32) for term in terms).astype(BF16)
-        kept = sum(part(term, mine).astype(F32) for term in terms).astype(BF16)
-        self.terms = [kept, flip(self.sent, bit)]
+        self.kept = sum(part(term, mine).astype(F32) for term in terms).astype(BF16)
+
+    def receive(self, got):
+        self.terms = [self.kept, got]
 
     def finish(self):
         while self.order:
@@ -1103,40 +1224,40 @@
     mlp_given = dot(mlp_send, normed_two).astype(BF16)
     mlp_in, gate_up_full[2] = exchange_and_gather(mlp_given, gate_up_low[2], 2)
     mlp_split = core_split(mlp_in, groups)
-    acts = [None] * len(cuts)
+    acts = [None]
     grads = [None] * len(cuts)
 
     def feed_chunk(index, feed_in, total):
         gate_up = gate_up_full[index]
-        acts[index], grads[index] = feed(
-            feed_in, grad_mlp_rows, gate_up, down_full, cuts[index][0]
+        acts[0], grads[index] = feed(
+            feed_in, grad_mlp_rows, gate_up, down_full, cuts[index][0], acts[0]
         )
         if index == 0:
-            steps(middle_scatter, acts[0])
-            grads[0] = after(grads[0], *[scatter.sent for scatter in middle_scatter])
-        return total + dot(grads[index], gate_up, CONTRACT_COLUMNS)
+            steps(middle_scatter, grads[0])
+            ready = [array for scatter in middle_scatter for array in (scatter.sent, scatter.kept)]
+            grads[0] = after(grads[0], *ready)
+        return back(grads[index], gate_up, total, BF16 if index == 3 else F32)
 
     normed_split = core_split(normed_all, groups)
     att_split = core_split(att_in, groups)
     heads_split = core_split(att_heads, groups)
     grad_mlp_in = feed_chunk(
-        1, after(mlp_in, *mlp_split, *normed_split, *att_split, *heads_split), 0.0
+        1, after(mlp_in, *mlp_split, *normed_split, *att_split, *heads_split), None
     )
     grad_mlp_in = feed_chunk(2, after(mlp_in, grad_mlp_in), grad_mlp_in)
     middle_scatter = scatter_product(mlp_split, [after(grads[1], grad_mlp_in), grads[2]], groups)
     ready = [array for scatter in middle_scatter for array in (scatter.terms[0], scatter.sent)]
     grad_mlp_in = feed_chunk(0, after(mlp_in, *ready), grad_mlp_in)
-    first_grad = dot(
-        mlp_in,
-        after(grads[0], grad_mlp_in),
-        CONTRACT_ROWS,
-    ).astype(BF16)
+    first_grad = weight_product(mlp_in, after(grads[0], grad_mlp_in))
     first_grad_sum = lax.psum_scatter(first_grad, "grp", scatter_dimension=0, tiled=True)
-    grad_mlp_in = feed_chunk(3, after(mlp_in, first_grad), grad_mlp_in).astype(BF16)
-    activated = jnp.concatenate(acts, axis=1)
+    grad_mlp_in = feed_chunk(3, after(mlp_in, first_grad), grad_mlp_in)
+    activated = acts[0]
+    for scatter in middle_scatter:
+        scatter.prepare(grad_mlp_in)
     mlp_returned, (down_grad, last_grad) = exchange_and_multiply(
         grad_mlp_in,
         [(multiply_columns, activated, grad_mlp_rows), (multiply_columns, mlp_in, grads[3])],
+        middle_scatter,
         3,
     )
     down_grad_sum = lax.psum_scatter(down_grad, "grp", scatter_dimension=0, tiled=True)
@@ -1154,16 +1275,11 @@
         dot(att_high, res_high) + dot(att_low, res_high) + dot(att_high, res_low)
     ).astype(BF16)
     grad_att_rows, (mlp_rows,) = exchange_and_multiply(
-        sent_four, [(multiply_rows, activated, down_full)], 4
-    )
-    steps(middle_scatter, grad_att_rows)
-    ready = [array for scatter in middle_scatter for array in (scatter.terms[0], scatter.sent)]
-    grad_heads = dot(
-        after(grad_att_rows, *ready), output_full, CONTRACT_COLUMNS
-    ).astype(BF16)
-    mlp_back = exchange(after(mlp_rows, grad_heads), experts)
-    grad_queries, grad_kv = attend_backward(
-        queries, keys_values, grad_heads, bounds, logsums, experts
+        sent_four, [(multiply_rows, activated, down_full)], [], 4
+    )
+    grad_heads = dot(grad_att_rows, output_full, CONTRACT_COLUMNS).astype(BF16)
+    grad_queries, grad_kv, mlp_first = attend_backward(
+        queries, keys_values, grad_heads, bounds, logsums, mlp_rows, experts, 7
     )
     grad_att_in = dot(grad_queries, query_full, CONTRACT_COLUMNS).astype(BF16)
     grad_all = (
@@ -1175,33 +1291,33 @@
         ).reshape(experts * tok_dev, model_width)
         + dot(grad_kv, kv_full, CONTRACT_COLUMNS)
     ).astype(BF16)
-    grad_back, kv_part, _ = exchange_and_scatter(
-        after(grad_all, mlp_back, first_grad_sum, down_grad_sum), [(normed_split, grad_kv)], 5
+    grad_all = after(grad_all, first_grad_sum, down_grad_sum)
+    (grad_back, mlp_second), kv_part, _ = exchange_and_scatter(
+        [(grad_all, model_width), (mlp_rows, model_width // 2)], [(normed_split, grad_kv)], 5
     )
     kv_grad = lax.psum(kv_part, "ep")
     while middle_scatter[0].order:
         steps(middle_scatter)
     middle_terms = [[after(term, kv_part) for term in scatter.terms] for scatter in middle_scatter]
     _, both_maps, _ = exchange_and_scatter(
-        None,
+        [],
         [
             (att_split, after(grad_queries, kv_part, last_grad_sum)),
             (heads_split, grad_att_rows),
         ],
         6,
-        costs=False,
     )
     kv_grad = after(kv_grad, both_maps)
     chunks = [[first_grad_sum], *middle_terms, [last_grad_sum]]
     gate_up_grad = assemble([[after(term, kv_grad) for term in terms] for terms in chunks])[None]
     down_grad = after(down_grad_sum, kv_grad).astype(F32)[None]
     query_grad, output_grad = [part.astype(F32)[None] for part in halves(both_maps)]
-    mlp_back = after(mlp_back, kv_grad)
+    mlp_back = jnp.concatenate([after(mlp_first, kv_grad), mlp_second], axis=1)
     output = (
         residual_one + dot(mlp_high, mlp_back, CONTRACT_ROWS) + dot(mlp_low, mlp_back, CONTRACT_ROWS)
     ).astype(BF16)
     grad_normed_one = jnp.sum(
-        grad_back.reshape(experts, tok_dev, model_width).astype(F32), axis=0
+        after(grad_back, kv_grad).reshape(experts, tok_dev, model_width).astype(F32), axis=0
     )
     kv_grad = transpose(kv_grad)
     grad_inner_one, grad_gain_one = norm_backward(grad_normed_one, unit_one, inverse_one, gain_one)
@@ -1209,6 +1325,7 @@
 
     gains_grad = jnp.stack([grad_gain_one, grad_gain_two])
     gains_grad = gains_grad.reshape((2,) + (2,) * bits + (-1,))
+    beside = [kv_grad, gate_up_grad, down_grad]
     for bit in reversed(range(bits)):
         mine_bit = (lax.axis_index("grp") >> bit) & 1
         kept = lax.dynamic_index_in_dim(gains_grad, mine_bit, 1, keepdims=False)
@@ -1216,6 +1333,8 @@
         gains_grad = kept + lax.ppermute(
             sent, "grp", [(i, i ^ (1 << bit)) for i in range(groups)]
         )
+        if beside:
+            gains_grad = after(gains_grad, beside.pop(0))
     for bit in range(experts.bit_length() - 1):
         gains_grad = gains_grad + lax.ppermute(
             gains_grad, "ep", [(i, i ^ (1 << bit)) for i in range(experts)]

time: 1150 us -> 1150 us (level)
  Pallas kernels: 759 us -> 858 us
  matrix products: 223 us -> 140 us
  starting transfers between devices: 41.3 us -> 18.7 us
  waiting for transfers between devices: 17.3 us -> 36 us
  local copies, waits for them, and re-layouts: 28.1 us -> 15.4 us
    dot_general x26 -> x21, matrix products: 218 us -> 135 us  [dot(): return lax.dot_general(left, right, dims, preferred_element_type=F32)]
    pallas_call x0 -> x5, Pallas kernels: none -> 82.6 us  [the longest x4 63.6 us: back(): pl.pallas_call(back_kernel, grid=(columns // TILE,), in_specs=[pl.BlockSp...]
    all_to_all x2 -> x1, starting transfers between devices: 23.7 us -> 3.76 us  [exchange(): lax.all_to_all(values.reshape(experts, rows // experts, width), 'ep', spl...]
    pallas_call x1, Pallas kernels: 48.3 us -> 66.1 us  [attend_backward(): pl.pallas_call(functools.partial(attend_backward_kernel, sources), grid=(...]
    ppermute x9 -> x7, waiting for transfers between devices: 2.87 us -> 20.5 us  [flip(): return lax.ppermute(values, 'grp', [(i, i ^ 1 << bit) for i in range(size)])]
  transfers between devices with their start and end apart: 25 -> 22, of which waited for: 6 -> 8; matrix products, arithmetic and copies ran while one was open for 25% -> 17% of each run, Pallas kernels for 65% -> 75%
where the time goes in v4:
time: 1150 us; the launch traced here: 1140 us
  Pallas kernels  858 us (75%)
  matrix products  140 us (12%)
  other arithmetic  54.5 us (5%)
  waiting for transfers between devices  36 us (3%)
  starting transfers between devices  18.7 us (2%)
  local copies, waits for them, and re-layouts  15.4 us (1%)
  between operations  14.9 us (1%)
    pallas_call x2, Pallas kernels, exchange_and_scatter(): pl.pallas_call(functools.partial(exchange_scatter_kernel, bits, count, le...  230 us
    pallas_call x2, Pallas kernels, exchange_and_gather(): pl.pallas_call(functools.partial(exchange_kernel, bits, count), in_specs=...  151 us
    dot_general x21, matrix products, dot(): return lax.dot_general(left, right, dims, preferred_element_type=F32)  135 us
    pallas_call x2, Pallas kernels, exchange_and_multiply(): pl.pallas_call(functools.partial(exchange_multiply_kernel, count, [job fo...  124 us
    pallas_call x4, Pallas kernels, feed(): pl.pallas_call(feed_kernel, grid=(tiles,), in_specs=[pl.BlockSpec((rows,...  82.9 us
    pallas_call x1, Pallas kernels, opening(): pl.pallas_call(functools.partial(opening_kernel, bits, count, len(cuts)),...  73.4 us
    pallas_call x1, Pallas kernels, attend_backward(): pl.pallas_call(functools.partial(attend_backward_kernel, sources), grid=(...  66.1 us
    pallas_call x4, Pallas kernels, back(): pl.pallas_call(back_kernel, grid=(columns // TILE,), in_specs=[pl.BlockSp...  63.6 us
  transfers between devices with their start and end apart: 22, of which 8 were waited for; matrix products, arithmetic and copies ran while one was open for 17% of the time, Pallas kernels for 75%

profile of v4, /device:TPU:0, one launch (start us, length us, event | category | flops | bytes accessed | tf_op | source)
XLA Modules:
  0.0 1136.9 jit_solution(10720249411040114213)
XLA Ops:
  25.6 73.4 %opening.1 = (bf16[4,256,2048]{2,1,0:T(8,128)(2,1)}, bf16[8,256,2048]{2,1,0:T(8,128)(2,1)}, bf16[256,4096]{1,0:T(8,128)(2,1)}, bf16[256,2048]{1,0:T(8,128)(2,1)}...) custom-call(bf16[256,2048]{1,0:T(8,128)(2,1)} %fusion.17.refs_0_, ...), custom_call_target="tpu_custom_call" | custom-call | tf_op jit(solution)/shard_map/opening/pallas_call | solution.py:596
  116.9 10.5 convolution_convert_fusion.6.query_ref
  135.1 23.0 %convolution_convert_fusion.key_ref.value_ref = bf16[1024,4096]{1,0:T(8,128)(2,1)} fusion(bf16[1024,2048]{1,0:T(8,128)(2,1)} %bitcast.235, bf16[2048,4096]{0,1:T(8,128)(2,1)} %all-gather.7.cloned.1.call-done), kind=kOutput, calls=%fused_computation.7 | convolution fusion | flops 17184063488 | bytes 29360128 | tf_op jit(solution)/shard_map/dot_general | solution.py:39
  158.1 32.0 %attend_forward.1 = (bf16[768,2048]{1,0:T(8,128)(2,1)}, f32[768,128]{1,0:T(8,128)}) custom-call(bf16[768,2048]{1,0:T(8,128)(2,1)} %convolution_convert_fusion.6.query_ref, bf16[1024,4096]{1,0:T(8,128)(2,1)} %convolution_convert_fusion.key_ref.value_ref, bf16[1024,4096]{1,0:T(8,128)(2,1)} %convolution_convert_fusion.key_ref.value_ref, s32[768,2]{1,0:T(8,128)} %copy.80.bounds_ref), custom_call_target="tpu_custom_call" | custom-call | tf_op jit(solution)/shard_map/attend_forward/pallas_call | solution.py:93
  190.2 13.1 %fusion.5 = bf16[768,2048]{1,0:T(8,128)(2,1)} fusion(bf16[768,2048]{1,0:T(8,128)(2,1)} %get-tuple-element.89, bf16[1,2048,2048]{2,1,0:T(8,128)(2,1)} %all-gather.15.cloned.1.call-done), kind=kOutput, calls=%fused_computation.22 | convolution fusion | flops 6444023808 | bytes 14680064 | tf_op jit(solution)/shard_map/dot_general | solution.py:39
  203.3 71.4 %exchange_and_gather.2 = (bf16[4,192,2048]{2,1,0:T(8,128)(2,1)}, bf16[8,256,2048]{2,1,0:T(8,128)(2,1)}) custom-call(bf16[4,192,2048]{2,1,0:T(8,128)(2,1)} %bitcast.256, bf16[256,2048]{1,0:T(8,128)(2,1)} %get-tuple-element.90.shard_ref), custom_call_target="tpu_custom_call" | custom-call | tf_op jit(solution)/shard_map/exchange_and_gather/pallas_call | solution.py:663
  283.1 79.5 %exchange_and_gather.3 = (bf16[4,192,2048]{2,1,0:T(8,128)(2,1)}, bf16[8,256,2048]{2,1,0:T(8,128)(2,1)}) custom-call(bf16[4,192,2048]{2,1,0:T(8,128)(2,1)} %bitcast.242, bf16[256,2048]{1,0:T(8,128)(2,1)} %get-tuple-element.92.shard_ref), custom_call_target="tpu_custom_call" | custom-call | tf_op jit(solution)/shard_map/exchange_and_gather/pallas_call | solution.py:663
  370.3 16.5 %feed.4 = (bf16[768,5632]{1,0:T(8,128)(2,1)}, bf16[768,2048]{1,0:T(8,128)(2,1)}) custom-call(bf16[768,2048]{1,0:T(8,128)(2,1)} %bitcast.219, bf16[768,2048]{1,0:T(8,128)(2,1)} %bitcast.226, bf16[2048,2048]{1,0:T(8,128)(2,1)} %bitcast.233, bf16[5632,2048]{1,0:T(8,128)(2,1)} %all-gather.9.cloned.1.call-done.down_ref.refs_2_), custom_call_target="tpu_custom_call" | custom-call | tf_op jit(solution)/shard_map/feed/pallas_call | solution.py:269
  386.7 11.5 %back.4.refs_0_ = f32[768,2048]{1,0:T(8,128)} custom-call(bf16[768,2048]{1,0:T(8,128)(2,1)} %get-tuple-element.102.grad_ref, bf16[2048,2048]{1,0:T(8,128)(2,1)} %bitcast.234), custom_call_target="tpu_custom_call" | custom-call | tf_op jit(solution)/shard_map/back/pallas_call | solution.py:305
  398.2 16.9 %feed.5 = (bf16[768,5632]{1,0:T(8,128)(2,1)}, bf16[768,2048]{1,0:T(8,128)(2,1)}) custom-call(bf16[768,2048]{1,0:T(8,128)(2,1)} %bitcast.220, bf16[768,2048]{1,0:T(8,128)(2,1)} %bitcast.227, bf16[2048,2048]{1,0:T(8,128)(2,1)} %bitcast.231, bf16[5632,2048]{1,0:T(8,128)(2,1)} %all-gather.9.cloned.1.call-done.down_ref.refs_2_, ...), custom_call_target="tpu_custom_call", output_to_operand_aliasing={{0}: (4, {})} | custom-call | tf_op jit(solution)/shard_map/feed/pallas_call | solution.py:269
  415.2 13.4 %back.5.refs_0_ = f32[768,2048]{1,0:T(8,128)} custom-call(bf16[768,2048]{1,0:T(8,128)(2,1)} %get-tuple-element.101.grad_ref, bf16[2048,2048]{1,0:T(8,128)(2,1)} %bitcast.232, f32[768,2048]{1,0:T(8,128)} %back.4.refs_0_), custom_call_target="tpu_custom_call" | custom-call | tf_op jit(solution)/shard_map/back/pallas_call | solution.py:305
  439.1 6.6 convolution_convert_fusion.4
  445.7 5.2 convolution_convert_fusion.2
  450.9 11.0 all-gather.11.cloned.1.call-done.gate_up_ref.weight_ref
  461.9 27.1 %feed.6 = (bf16[768,5632]{1,0:T(8,128)(2,1)}, bf16[768,4096]{1,0:T(8,128)(2,1)}) custom-call(bf16[768,2048]{1,0:T(8,128)(2,1)} %bitcast.221, bf16[768,2048]{1,0:T(8,128)(2,1)} %bitcast.228, bf16[2048,4096]{1,0:T(8,128)(2,1)} %all-gather.11.cloned.1.call-done.gate_up_ref.weight_ref, ...), custom_call_target="tpu_custom_call", output_to_operand_aliasing={{0}: (4, {})} | custom-call | tf_op jit(solution)/shard_map/feed/pallas_call | solution.py:269
  489.1 5.8 fusion.27
  494.9 6.5 fusion.25
  501.4 21.3 %back.6.refs_0_ = f32[768,2048]{1,0:T(8,128)} custom-call(bf16[768,4096]{1,0:T(8,128)(2,1)} %get-tuple-element.112.grad_ref.right_ref, bf16[2048,4096]{1,0:T(8,128)(2,1)} %all-gather.11.cloned.1.call-done.gate_up_ref.weight_ref, f32[768,2048]{1,0:T(8,128)} %back.5.refs_0_), custom_call_target="tpu_custom_call" | custom-call | tf_op jit(solution)/shard_map/back/pallas_call | solution.py:305
  522.7 18.9 %weight_product.1 = bf16[2048,4096]{1,0:T(8,128)(2,1)} custom-call(bf16[768,2048]{1,0:T(8,128)(2,1)} %bitcast.222, bf16[768,4096]{1,0:T(8,128)(2,1)} %get-tuple-element.112.grad_ref.right_ref), custom_call_target="tpu_custom_call" | custom-call | tf_op jit(solution)/shard_map/weight_product/pallas_call | solution.py:328
  544.1 22.4 %feed.7 = (bf16[768,5632]{1,0:T(8,128)(2,1)}, bf16[768,3072]{1,0:T(8,128)(2,1)}) custom-call(bf16[768,2048]{1,0:T(8,128)(2,1)} %bitcast.223, bf16[768,2048]{1,0:T(8,128)(2,1)} %bitcast.229, bf16[2048,3072]{1,0:T(8,128)(2,1)} %all-gather.13.cloned.1.call-done.gate_up_ref.weight_ref, ...), custom_call_target="tpu_custom_call", output_to_operand_aliasing={{0}: (4, {})} | custom-call | tf_op jit(solution)/shard_map/feed/pallas_call | solution.py:269
  566.5 17.4 %back.7 = bf16[768,2048]{1,0:T(8,128)(2,1)} custom-call(bf16[768,3072]{1,0:T(8,128)(2,1)} %get-tuple-element.116.grad_ref.refs_4_, bf16[2048,3072]{1,0:T(8,128)(2,1)} %all-gather.13.cloned.1.call-done.gate_up_ref.weight_ref, f32[768,2048]{1,0:T(8,128)} %back.6.refs_0_), custom_call_target="tpu_custom_call" | custom-call | tf_op jit(solution)/shard_map/back/pallas_call | solution.py:305
  584.0 16.1 %collective-permute-done.6 = bf16[2,256,2048]{2,1,0:T(8,128)(2,1)} collective-permute-done((bf16[2,256,2048]{2,1,0:T(8,128)(2,1)}, bf16[2,256,2048]{2,1,0:T(8,128)(2,1)}, u32[]{:S(2)}, u32[]{:S(2)}) %collective-permute-start.6) | collective-permute-done | bytes 2097184 | tf_op jit(solution)/shard_map/ppermute | solution.py:1008
  609.0 54.1 %exchange_and_multiply.2 = (bf16[4,192,2048]{2,1,0:T(8,128)(2,1)}, bf16[5632,2048]{1,0:T(8,128)(2,1)}, bf16[2048,3072]{1,0:T(8,128)(2,1)}, bf16[256,2048]{1,0:T(8,128)(2,1)}, bf16[256,2048]{1,0:T(8,128)(2,1)}) custom-call(bf16[4,192,2048]{2,1,0:T(8,128)(2,1)} %bitcast.241, bf16[768,5632]{1,0:T(8,128)(2,1)} %get-tuple-element.117.refs_1_, ...), custom_call_target="tpu_custom_call" | custom-call | tf_op jit(solution)/shard_map/exchange_and_multiply/pallas_call | solution.py:772
  674.2 69.5 %exchange_and_multiply.3 = (bf16[4,192,2048]{2,1,0:T(8,128)(2,1)}, bf16[768,2048]{1,0:T(8,128)(2,1)}) custom-call(bf16[4,192,2048]{2,1,0:T(8,128)(2,1)} %bitcast.244, bf16[768,5632]{1,0:T(8,128)(2,1)} %get-tuple-element.117.refs_1_, bf16[5632,2048]{1,0:T(8,128)(2,1)} %all-gather.9.cloned.1.call-done.down_ref.refs_2_), custom_call_target="tpu_custom_call" | custom-call | tf_op jit(solution)/shard_map/exchange_and_multiply/pallas_call | solution.py:772
  743.7 12.3 %fusion.8.grad_ref = bf16[768,2048]{1,0:T(8,128)(2,1)} fusion(bf16[768,2048]{1,0:T(8,128)(2,1)} %bitcast.254, bf16[1,2048,2048]{2,1,0:T(8,128)(2,1)} %all-gather.15.cloned.1.call-done), kind=kOutput, calls=%fused_computation.23 | convolution fusion | flops 6444023808 | bytes 14680064 | tf_op jit(solution)/shard_map/dot_general | solution.py:39
  755.9 66.1 %attend_backward.1 = (bf16[768,2048]{1,0:T(8,128)(2,1)}, bf16[1024,4096]{1,0:T(8,128)(2,1)}, bf16[4,192,1024]{2,1,0:T(8,128)(2,1)}) custom-call(bf16[768,2048]{1,0:T(8,128)(2,1)} %convolution_convert_fusion.6.query_ref, bf16[1024,4096]{1,0:T(8,128)(2,1)} %convolution_convert_fusion.key_ref.value_ref, ...), custom_call_target="tpu_custom_call" | custom-call | tf_op jit(solution)/shard_map/attend_backward/pallas_call | solution.py:207
  822.1 10.1 convolution_convert_fusion.5
  835.7 22.1 %fusion = bf16[1024,2048]{1,0:T(8,128)(2,1)} fusion(f32[4,256,2048]{2,1,0:T(8,128)S(1)} %fusion.43, bf16[1024,4096]{1,0:T(8,128)(2,1)S(1)} %copy-done.16, bf16[2048,4096]{0,1:T(8,128)(2,1)} %all-gather.7.cloned.1.call-done), kind=kOutput, calls=%fused_computation.2 | convolution fusion | flops 17184063488 | bytes 37748736 | tf_op jit(solution)/shard_map/dot_general | solution.py:39
  857.8 137.4 %exchange_and_scatter.1 = (bf16[4,256,2048]{2,1,0:T(8,128)(2,1)}, bf16[4,192,1024]{2,1,0:T(8,128)(2,1)}, bf16[256,4096]{1,0:T(8,128)(2,1)}) custom-call(bf16[4,256,2048]{2,1,0:T(8,128)(2,1)} %bitcast.253, bf16[4,192,2048]{2,1,0:T(8,128)(2,1)} %bitcast.240, bf16[1024,1024]{1,0:T(8,128)(2,1)} %get-tuple-element.171.refs_2_, ...), custom_call_target="tpu_custom_call" | custom-call | tf_op jit(solution)/shard_map/exchange_and_scatter/pallas_call | solution.py:957
  995.3 92.5 %scatter.1 = bf16[256,4096]{1,0:T(8,128)(2,1)} custom-call(bf16[768,1024]{1,0:T(8,128)(2,1)} %get-tuple-element.191.refs_0_, bf16[768,1024]{1,0:T(8,128)(2,1)} %get-tuple-element.190.refs_1_, bf16[768,1024]{1,0:T(8,128)(2,1)} %get-tuple-element.181.refs_2_, bf16[768,1024]{1,0:T(8,128)(2,1)} %get-tuple-element.180.refs_3_, ...), custom_call_target="tpu_custom_call" | custom-call | tf_op jit(solution)/shard_map/scatter/pallas_call | solution.py:957
  1101.7 7.0 transpose.38
  1110.1 9.4 assemble.1
  (247 shorter events, 122.0 us)
Async XLA Ops:
  7.2 127.9 %all-gather.7.cloned.1.call-start = ((), (), s32[]{:S(2)}) async-start(), calls=%async_computation.4 | async-start | bytes 18874368 | tf_op jit(solution)/shard_map/all_gather | solution.py:1150
  11.1 179.1 %all-gather.15.cloned.1.call-start = ((), (), s32[]{:S(2)}) async-start(), calls=%async_computation.12 | async-start | bytes 9437184 | tf_op jit(solution)/shard_map/all_gather | solution.py:1150
  13.1 357.2 %all-gather.9.cloned.1.call-start = ((), (), s32[]{:S(2)}) async-start(), calls=%async_computation.5 | async-start | bytes 25952256 | tf_op jit(solution)/shard_map/all_gather | solution.py:1150
  13.2 3.2 collective-permute-start
  16.4 4.1 collective-permute-start.1
  20.6 3.7 collective-permute-start.2
  22.7 76.4 %copy-start.47 = (f32[256]{0:T(256)}, f32[256]{0:T(256)S(1)}, u32[]{:S(2)}) copy-start(f32[256]{0:T(256)S(1)} %add_rsqrt_fusion.1) | copy-start | bytes 3076
  24.3 74.7 %copy-start.37 = (f32[1,2048]{1,0:T(1,128)}, f32[1,2048]{1,0:T(1,128)S(1)}, u32[]{:S(2)}) copy-start(f32[1,2048]{1,0:T(1,128)S(1)} %get-tuple-element.213) | copy-start | bytes 24580
  24.3 254.7 %copy-start.35 = (f32[1,2048]{1,0:T(1,128)}, f32[1,2048]{1,0:T(1,128)S(1)}, u32[]{:S(2)}) copy-start(f32[1,2048]{1,0:T(1,128)S(1)} %get-tuple-element.212) | copy-start | bytes 24580
  99.2 362.8 %all-gather.11.cloned.1.call-start = ((), (), s32[]{:S(2)}) async-start(), calls=%async_computation.6 | async-start | bytes 18874368 | tf_op jit(solution)/shard_map/all_gather | solution.py:1150
  99.7 444.4 %all-gather.13.cloned.1.call-start = ((), (), s32[]{:S(2)}) async-start(), calls=%async_computation.7 | async-start | bytes 14155776 | tf_op jit(solution)/shard_map/all_gather | solution.py:1150
  109.9 80.2 %all-to-all-start = ((bf16[4,192,2048]{2,1,0:T(8,128)(2,1)}), bf16[4,192,2048]{2,1,0:T(8,128)(2,1)S(1)}, u32[]{:S(2)}, u32[]{:S(2)}) async-start(bf16[4,192,2048]{2,1,0:T(8,128)(2,1)} %bitcast.243), calls=%async_computation | async-start | bytes 6291456 | tf_op jit(solution)/shard_map/all_to_all | solution.py:1099
  113.7 744.1 %reduce-scatter.4.cloned.1.call-start = ((), (), s32[]{:S(2)}) async-start(), calls=%async_computation.8 | async-start | bytes 18874368 | tf_op jit(solution)/shard_map/reduce_scatter | solution.py:1252
  203.3 71.4 %copy-start.8 = (bf16[256,2048]{1,0:T(8,128)(2,1)S(1)}, bf16[256,2048]{1,0:T(8,128)(2,1)}, u32[]{:S(2)}) copy-start(bf16[256,2048]{1,0:T(8,128)(2,1)} %param.13) | copy-start | bytes 3145732
  279.0 83.5 %copy-start.43 = (f32[256]{0:T(256)}, f32[256]{0:T(256)S(1)}, u32[]{:S(2)}) copy-start(f32[256]{0:T(256)S(1)} %add_rsqrt_fusion) | copy-start | bytes 3076
  283.1 79.5 %copy-start.20 = (bf16[768,2048]{1,0:T(8,128)(2,1)S(1)}, bf16[768,2048]{1,0:T(8,128)(2,1)}, u32[]{:S(2)}) copy-start(bf16[768,2048]{1,0:T(8,128)(2,1)} %get-tuple-element.89) | copy-start | bytes 9437188
  415.2 13.4 %copy-start.22 = (bf16[768,2048]{1,0:T(8,128)(2,1)S(1)}, bf16[768,2048]{1,0:T(8,128)(2,1)}, u32[]{:S(2)}) copy-start(bf16[768,2048]{1,0:T(8,128)(2,1)} %get-tuple-element.101.grad_ref) | copy-start | bytes 9437188
  415.2 13.4 %copy-start.30 = (bf16[768,1024]{1,0:T(8,128)(2,1)S(1)}, bf16[768,1024]{1,0:T(8,128)(2,1)}, u32[]{:S(2)}) copy-start(bf16[768,1024]{1,0:T(8,128)(2,1)} %get-tuple-element.200) | copy-start | bytes 4718596
  433.6 55.4 %collective-permute-start.4 = (bf16[1024,2048]{1,0:T(8,128)(2,1)}, bf16[1024,2048]{1,0:T(8,128)(2,1)}, u32[]{:S(2)}, u32[]{:S(2)}) collective-permute-start(bf16[1024,2048]{1,0:T(8,128)(2,1)} %convolution_convert_fusion.1), channel_id=1, source_target_pairs={{0,4},{4,0},{8,12},{12,8},{16,20},{20,16},{24,28},{28,24},{1,5},{5... | collective-permute-start | bytes 12582920 | tf_op jit(solution)/shard_map/ppermute | solution.py:1008
  438.9 50.2 %collective-permute-start.3 = (bf16[1024,2048]{1,0:T(8,128)(2,1)}, bf16[1024,2048]{1,0:T(8,128)(2,1)}, u32[]{:S(2)}, u32[]{:S(2)}) collective-permute-start(bf16[1024,2048]{1,0:T(8,128)(2,1)} %convolution_convert_fusion.3), channel_id=1, source_target_pairs={{0,4},{4,0},{8,12},{12,8},{16,20},{20,16},{24,28},{28,24},{1,5},{5... | collective-permute-start | bytes 12582920 | tf_op jit(solution)/shard_map/ppermute | solution.py:1008
  461.9 27.2 %copy-start.19 = (bf16[1024,2048]{1,0:T(8,128)(2,1)S(1)}, bf16[1024,2048]{1,0:T(8,128)(2,1)}, u32[]{:S(2)}) copy-start(bf16[1024,2048]{1,0:T(8,128)(2,1)} %convolution_convert_fusion.2) | copy-start | bytes 12582916
  541.7 316.1 %reduce-scatter.6.cloned.1.call-start = ((), (), s32[]{:S(2)}) async-start(), calls=%async_computation.9 | async-start | bytes 25952256 | tf_op jit(solution)/shard_map/reduce_scatter | solution.py:1263
  541.8 58.3 %collective-permute-start.6 = (bf16[2,256,2048]{2,1,0:T(8,128)(2,1)}, bf16[2,256,2048]{2,1,0:T(8,128)(2,1)}, u32[]{:S(2)}, u32[]{:S(2)}) collective-permute-start(bf16[2,256,2048]{2,1,0:T(8,128)(2,1)} %get-tuple-element.163), channel_id=1, source_target_pairs={{0,16},{4,20},{8,24},{12,28},{16,0},{20,4},{24,8},{28,12},{1,17},{... | collective-permute-start | bytes 6291464 | tf_op jit(solution)/shard_map/ppermute | solution.py:1008
  542.7 58.9 %collective-permute-start.5 = (bf16[2,256,2048]{2,1,0:T(8,128)(2,1)}, bf16[2,256,2048]{2,1,0:T(8,128)(2,1)}, u32[]{:S(2)}, u32[]{:S(2)}) collective-permute-start(bf16[2,256,2048]{2,1,0:T(8,128)(2,1)} %get-tuple-element.165), channel_id=1, source_target_pairs={{0,8},{4,12},{8,0},{12,4},{16,24},{20,28},{24,16},{28,20},{1,9},{5... | collective-permute-start | bytes 6291464 | tf_op jit(solution)/shard_map/ppermute | solution.py:1008
  584.0 21.3 %copy-start.15 = (bf16[2,256,2048]{2,1,0:T(8,128)(2,1)S(1)}, bf16[2,256,2048]{2,1,0:T(8,128)(2,1)}, u32[]{:S(2)}) copy-start(bf16[2,256,2048]{2,1,0:T(8,128)(2,1)} %get-tuple-element.118) | copy-start | bytes 6291460
  663.1 332.1 %reduce-scatter.8.cloned.1.call-start = ((), (), s32[]{:S(2)}) async-start(), calls=%async_computation.11 | async-start | bytes 14155776 | tf_op jit(solution)/shard_map/reduce_scatter | solution.py:1264
  663.9 428.0 %all-reduce.2.cloned.1.call-start = ((), (), s32[]{:S(2)}) async-start(), calls=%async_computation.10 | async-start | bytes 4194304 | tf_op jit(solution)/shard_map/psum | solution.py:1298
  1097.3 11.4 %collective-permute-start.7 = (f32[2,2,2,256]{3,0,2,1:T(2,128)S(1)}, f32[2,2,2,256]{3,0,2,1:T(2,128)S(1)}, u32[]{:S(2)}, u32[]{:S(2)}) collective-permute-start(f32[2,2,2,256]{3,0,2,1:T(2,128)S(1)} %fusion.72), channel_id=1, source_target_pairs={{0,16},{4,20},{8,24},{12,28},{16,0},{20,4},{24,8},{28,12},{1,17},{... | collective-permute-start | bytes 24584 | tf_op jit(solution)/shard_map/ppermute | solution.py:1333
  1108.7 10.7 collective-permute-start.8
  1119.5 2.0 collective-permute-start.9
  1121.5 3.6 collective-permute-start.10
  1125.1 4.5 collective-permute-start.11
  (47 other events, 201.5 us)
Sparse Core Ops, SparseCore 0:
  11.2 121.9 all-gather.6
  135.7 54.3 all-gather.14
  192.0 178.2 all-gather.8
  372.0 89.8 all-gather.10
  463.6 72.1 all-gather.12
  541.8 149.3 reduce-scatter.3
  694.8 145.9 reduce-scatter.5
  844.3 138.7 reduce-scatter.7
  995.4 86.5 all-reduce.1

commit v5 on v4

--- a/solution.py
+++ b/solution.py
@@ -1225,6 +1225,7 @@
     mlp_in, gate_up_full[2] = exchange_and_gather(mlp_given, gate_up_low[2], 2)
     mlp_split = core_split(mlp_in, groups)
     acts = [None]
+    weight_grads = []
     grads = [None] * len(cuts)
 
     def feed_chunk(index, feed_in, total):
@@ -1233,7 +1234,8 @@
             feed_in, grad_mlp_rows, gate_up, down_full, cuts[index][0], acts[0]
         )
         if index == 0:
-            steps(middle_scatter, grads[0])
+            weight_grads.append(weight_product(mlp_in, grads[0]))
+            steps(middle_scatter, weight_grads[0])
             ready = [array for scatter in middle_scatter for array in (scatter.sent, scatter.kept)]
             grads[0] = after(grads[0], *ready)
         return back(grads[index], gate_up, total, BF16 if index == 3 else F32)
@@ -1248,9 +1250,8 @@
     middle_scatter = scatter_product(mlp_split, [after(grads[1], grad_mlp_in), grads[2]], groups)
     ready = [array for scatter in middle_scatter for array in (scatter.terms[0], scatter.sent)]
     grad_mlp_in = feed_chunk(0, after(mlp_in, *ready), grad_mlp_in)
-    first_grad = weight_product(mlp_in, after(grads[0], grad_mlp_in))
-    first_grad_sum = lax.psum_scatter(first_grad, "grp", scatter_dimension=0, tiled=True)
-    grad_mlp_in = feed_chunk(3, after(mlp_in, first_grad), grad_mlp_in)
+    first_grad_sum = lax.psum_scatter(weight_grads[0], "grp", scatter_dimension=0, tiled=True)
+    grad_mlp_in = feed_chunk(3, after(mlp_in, grad_mlp_in), grad_mlp_in)
     activated = acts[0]
     for scatter in middle_scatter:
         scatter.prepare(grad_mlp_in)

time: 1150 us -> 1140 us (level)
    pallas_call x2, Pallas kernels: 230 us -> 217 us  [exchange_and_scatter(): pl.pallas_call(functools.partial(exchange_scatter_kernel, bits, count, le...]
where the time goes in v5:
time: 1140 us; the launch traced here: 1130 us
  Pallas kernels  850 us (75%)
  matrix products  139 us (12%)
  other arithmetic  53.1 us (5%)
  waiting for transfers between devices  34.9 us (3%)
  starting transfers between devices  24.2 us (2%)
  local copies, waits for them, and re-layouts  15.6 us (1%)
  between operations  14.9 us (1%)
    pallas_call x2, Pallas kernels, exchange_and_scatter(): pl.pallas_call(functools.partial(exchange_scatter_kernel, bits, count, le...  217 us
    pallas_call x2, Pallas kernels, exchange_and_gather(): pl.pallas_call(functools.partial(exchange_kernel, bits, count), in_specs=...  151 us
    dot_general x21, matrix products, dot(): return lax.dot_general(left, right, dims, preferred_element_type=F32)  134 us
    pallas_call x2, Pallas kernels, exchange_and_multiply(): pl.pallas_call(functools.partial(exchange_multiply_kernel, count, [job fo...  126 us
    pallas_call x4, Pallas kernels, feed(): pl.pallas_call(feed_kernel, grid=(tiles,), in_specs=[pl.BlockSpec((rows,...  84.6 us
    pallas_call x1, Pallas kernels, opening(): pl.pallas_call(functools.partial(opening_kernel, bits, count, len(cuts)),...  73.4 us
    pallas_call x1, Pallas kernels, attend_backward(): pl.pallas_call(functools.partial(attend_backward_kernel, sources), grid=(...  67.6 us
    pallas_call x4, Pallas kernels, back(): pl.pallas_call(back_kernel, grid=(columns // TILE,), in_specs=[pl.BlockSp...  63.1 us
  transfers between devices with their start and end apart: 22, of which 8 were waited for; matrix products, arithmetic and copies ran while one was open for 17% of the time, Pallas kernels for 75%

profile of v5, /device:TPU:0, one launch (start us, length us, event | category | flops | bytes accessed | tf_op | source)
XLA Modules:
  0.0 1131.4 jit_solution(10354754241355028884)
XLA Ops:
  25.6 73.4 %opening.1 = (bf16[4,256,2048]{2,1,0:T(8,128)(2,1)}, bf16[8,256,2048]{2,1,0:T(8,128)(2,1)}, bf16[256,4096]{1,0:T(8,128)(2,1)}, bf16[256,2048]{1,0:T(8,128)(2,1)}...) custom-call(bf16[256,2048]{1,0:T(8,128)(2,1)} %fusion.17.refs_0_, ...), custom_call_target="tpu_custom_call" | custom-call | tf_op jit(solution)/shard_map/opening/pallas_call | solution.py:596
  116.9 10.6 convolution_convert_fusion.6.query_ref
  135.3 23.0 %convolution_convert_fusion.key_ref.value_ref = bf16[1024,4096]{1,0:T(8,128)(2,1)} fusion(bf16[1024,2048]{1,0:T(8,128)(2,1)} %bitcast.235, bf16[2048,4096]{0,1:T(8,128)(2,1)} %all-gather.7.cloned.1.call-done), kind=kOutput, calls=%fused_computation.7 | convolution fusion | flops 17184063488 | bytes 29360128 | tf_op jit(solution)/shard_map/dot_general | solution.py:39
  158.3 32.0 %attend_forward.1 = (bf16[768,2048]{1,0:T(8,128)(2,1)}, f32[768,128]{1,0:T(8,128)}) custom-call(bf16[768,2048]{1,0:T(8,128)(2,1)} %convolution_convert_fusion.6.query_ref, bf16[1024,4096]{1,0:T(8,128)(2,1)} %convolution_convert_fusion.key_ref.value_ref, bf16[1024,4096]{1,0:T(8,128)(2,1)} %convolution_convert_fusion.key_ref.value_ref, s32[768,2]{1,0:T(8,128)} %copy.80.bounds_ref), custom_call_target="tpu_custom_call" | custom-call | tf_op jit(solution)/shard_map/attend_forward/pallas_call | solution.py:93
  190.4 13.3 %fusion.5 = bf16[768,2048]{1,0:T(8,128)(2,1)} fusion(bf16[768,2048]{1,0:T(8,128)(2,1)} %get-tuple-element.88, bf16[1,2048,2048]{2,1,0:T(8,128)(2,1)} %all-gather.15.cloned.1.call-done), kind=kOutput, calls=%fused_computation.22 | convolution fusion | flops 6444023808 | bytes 14680064 | tf_op jit(solution)/shard_map/dot_general | solution.py:39
  203.7 70.9 %exchange_and_gather.2 = (bf16[4,192,2048]{2,1,0:T(8,128)(2,1)}, bf16[8,256,2048]{2,1,0:T(8,128)(2,1)}) custom-call(bf16[4,192,2048]{2,1,0:T(8,128)(2,1)} %bitcast.256, bf16[256,2048]{1,0:T(8,128)(2,1)} %get-tuple-element.89.shard_ref), custom_call_target="tpu_custom_call" | custom-call | tf_op jit(solution)/shard_map/exchange_and_gather/pallas_call | solution.py:663
  283.1 79.8 %exchange_and_gather.3 = (bf16[4,192,2048]{2,1,0:T(8,128)(2,1)}, bf16[8,256,2048]{2,1,0:T(8,128)(2,1)}) custom-call(bf16[4,192,2048]{2,1,0:T(8,128)(2,1)} %bitcast.242, bf16[256,2048]{1,0:T(8,128)(2,1)} %get-tuple-element.91.shard_ref), custom_call_target="tpu_custom_call" | custom-call | tf_op jit(solution)/shard_map/exchange_and_gather/pallas_call | solution.py:663
  369.8 16.5 %feed.4 = (bf16[768,5632]{1,0:T(8,128)(2,1)}, bf16[768,2048]{1,0:T(8,128)(2,1)}) custom-call(bf16[768,2048]{1,0:T(8,128)(2,1)} %bitcast.219, bf16[768,2048]{1,0:T(8,128)(2,1)} %bitcast.226, bf16[2048,2048]{1,0:T(8,128)(2,1)} %bitcast.233, bf16[5632,2048]{1,0:T(8,128)(2,1)} %all-gather.9.cloned.1.call-done.down_ref.refs_2_), custom_call_target="tpu_custom_call" | custom-call | tf_op jit(solution)/shard_map/feed/pallas_call | solution.py:269
  386.3 11.4 %back.4.refs_0_ = f32[768,2048]{1,0:T(8,128)} custom-call(bf16[768,2048]{1,0:T(8,128)(2,1)} %get-tuple-element.101.grad_ref, bf16[2048,2048]{1,0:T(8,128)(2,1)} %bitcast.234), custom_call_target="tpu_custom_call" | custom-call | tf_op jit(solution)/shard_map/back/pallas_call | solution.py:305
  397.7 16.8 %feed.5 = (bf16[768,5632]{1,0:T(8,128)(2,1)}, bf16[768,2048]{1,0:T(8,128)(2,1)}) custom-call(bf16[768,2048]{1,0:T(8,128)(2,1)} %bitcast.220, bf16[768,2048]{1,0:T(8,128)(2,1)} %bitcast.227, bf16[2048,2048]{1,0:T(8,128)(2,1)} %bitcast.231, bf16[5632,2048]{1,0:T(8,128)(2,1)} %all-gather.9.cloned.1.call-done.down_ref.refs_2_, ...), custom_call_target="tpu_custom_call", output_to_operand_aliasing={{0}: (4, {})} | custom-call | tf_op jit(solution)/shard_map/feed/pallas_call | solution.py:269
  414.5 13.3 %back.5.refs_0_ = f32[768,2048]{1,0:T(8,128)} custom-call(bf16[768,2048]{1,0:T(8,128)(2,1)} %get-tuple-element.100.grad_ref, bf16[2048,2048]{1,0:T(8,128)(2,1)} %bitcast.232, f32[768,2048]{1,0:T(8,128)} %back.4.refs_0_), custom_call_target="tpu_custom_call" | custom-call | tf_op jit(solution)/shard_map/back/pallas_call | solution.py:305
  447.9 13.5 %all-gather.11.cloned.1.call-done.gate_up_ref.weight_ref = bf16[2048,4096]{1,0:T(8,128)(2,1)} async-done(((bf16[256,4096]{1,0:T(8,128)(2,1)}), bf16[2048,4096]{1,0:T(8,128)(2,1)}) %all-gather.11.cloned.1.call-update) | async-done | bytes 16777232 | tf_op jit(solution)/shard_map/all_gather | solution.py:1150
  461.5 27.3 %feed.6 = (bf16[768,5632]{1,0:T(8,128)(2,1)}, bf16[768,4096]{1,0:T(8,128)(2,1)}) custom-call(bf16[768,2048]{1,0:T(8,128)(2,1)} %bitcast.221, bf16[768,2048]{1,0:T(8,128)(2,1)} %bitcast.228, bf16[2048,4096]{1,0:T(8,128)(2,1)} %all-gather.11.cloned.1.call-done.gate_up_ref.weight_ref, ...), custom_call_target="tpu_custom_call", output_to_operand_aliasing={{0}: (4, {})} | custom-call | tf_op jit(solution)/shard_map/feed/pallas_call | solution.py:269
  488.8 19.2 %weight_product.1 = bf16[2048,4096]{1,0:T(8,128)(2,1)} custom-call(bf16[768,2048]{1,0:T(8,128)(2,1)} %bitcast.222, bf16[768,4096]{1,0:T(8,128)(2,1)} %get-tuple-element.110.right_ref.grad_ref), custom_call_target="tpu_custom_call" | custom-call | tf_op jit(solution)/shard_map/weight_product/pallas_call | solution.py:328
  508.6 7.7 collective-permute-done.3
  516.3 6.3 collective-permute-done.4
  522.6 5.4 fusion.25
  529.5 6.6 fusion.27
  536.5 21.6 %back.6.refs_0_ = f32[768,2048]{1,0:T(8,128)} custom-call(bf16[768,4096]{1,0:T(8,128)(2,1)} %get-tuple-element.110.right_ref.grad_ref, bf16[2048,4096]{1,0:T(8,128)(2,1)} %all-gather.11.cloned.1.call-done.gate_up_ref.weight_ref, f32[768,2048]{1,0:T(8,128)} %back.5.refs_0_), custom_call_target="tpu_custom_call" | custom-call | tf_op jit(solution)/shard_map/back/pallas_call | solution.py:305
  558.1 24.0 %feed.7 = (bf16[768,5632]{1,0:T(8,128)(2,1)}, bf16[768,3072]{1,0:T(8,128)(2,1)}) custom-call(bf16[768,2048]{1,0:T(8,128)(2,1)} %bitcast.223, bf16[768,2048]{1,0:T(8,128)(2,1)} %bitcast.229, bf16[2048,3072]{1,0:T(8,128)(2,1)} %all-gather.13.cloned.1.call-done.gate_up_ref.weight_ref, ...), custom_call_target="tpu_custom_call", output_to_operand_aliasing={{0}: (4, {})} | custom-call | tf_op jit(solution)/shard_map/feed/pallas_call | solution.py:269
  582.2 16.8 %back.7 = bf16[768,2048]{1,0:T(8,128)(2,1)} custom-call(bf16[768,3072]{1,0:T(8,128)(2,1)} %get-tuple-element.114.grad_ref.refs_4_, bf16[2048,3072]{1,0:T(8,128)(2,1)} %all-gather.13.cloned.1.call-done.gate_up_ref.weight_ref, f32[768,2048]{1,0:T(8,128)} %back.6.refs_0_), custom_call_target="tpu_custom_call" | custom-call | tf_op jit(solution)/shard_map/back/pallas_call | solution.py:305
  606.5 56.3 %exchange_and_multiply.2 = (bf16[4,192,2048]{2,1,0:T(8,128)(2,1)}, bf16[5632,2048]{1,0:T(8,128)(2,1)}, bf16[2048,3072]{1,0:T(8,128)(2,1)}, bf16[256,2048]{1,0:T(8,128)(2,1)}, bf16[256,2048]{1,0:T(8,128)(2,1)}) custom-call(bf16[4,192,2048]{2,1,0:T(8,128)(2,1)} %bitcast.241, bf16[768,5632]{1,0:T(8,128)(2,1)} %get-tuple-element.115.refs_1_, ...), custom_call_target="tpu_custom_call" | custom-call | tf_op jit(solution)/shard_map/exchange_and_multiply/pallas_call | solution.py:772
  674.0 69.7 %exchange_and_multiply.3 = (bf16[4,192,2048]{2,1,0:T(8,128)(2,1)}, bf16[768,2048]{1,0:T(8,128)(2,1)}) custom-call(bf16[4,192,2048]{2,1,0:T(8,128)(2,1)} %bitcast.244, bf16[768,5632]{1,0:T(8,128)(2,1)} %get-tuple-element.115.refs_1_, bf16[5632,2048]{1,0:T(8,128)(2,1)} %all-gather.9.cloned.1.call-done.down_ref.refs_2_), custom_call_target="tpu_custom_call" | custom-call | tf_op jit(solution)/shard_map/exchange_and_multiply/pallas_call | solution.py:772
  743.8 12.0 %fusion.8.grad_ref = bf16[768,2048]{1,0:T(8,128)(2,1)} fusion(bf16[768,2048]{1,0:T(8,128)(2,1)} %bitcast.254, bf16[1,2048,2048]{2,1,0:T(8,128)(2,1)} %all-gather.15.cloned.1.call-done), kind=kOutput, calls=%fused_computation.23 | convolution fusion | flops 6444023808 | bytes 14680064 | tf_op jit(solution)/shard_map/dot_general | solution.py:39
  755.8 67.6 %attend_backward.1 = (bf16[768,2048]{1,0:T(8,128)(2,1)}, bf16[1024,4096]{1,0:T(8,128)(2,1)}, bf16[4,192,1024]{2,1,0:T(8,128)(2,1)}) custom-call(bf16[768,2048]{1,0:T(8,128)(2,1)} %convolution_convert_fusion.6.query_ref, bf16[1024,4096]{1,0:T(8,128)(2,1)} %convolution_convert_fusion.key_ref.value_ref, ...), custom_call_target="tpu_custom_call" | custom-call | tf_op jit(solution)/shard_map/attend_backward/pallas_call | solution.py:207
  823.4 10.2 convolution_convert_fusion.5
  837.1 23.0 %fusion = bf16[1024,2048]{1,0:T(8,128)(2,1)} fusion(f32[4,256,2048]{2,1,0:T(8,128)S(1)} %fusion.43, bf16[1024,4096]{1,0:T(8,128)(2,1)S(1)} %copy-done.16, bf16[2048,4096]{0,1:T(8,128)(2,1)} %all-gather.7.cloned.1.call-done), kind=kOutput, calls=%fused_computation.2 | convolution fusion | flops 17184063488 | bytes 37748736 | tf_op jit(solution)/shard_map/dot_general | solution.py:39
  860.1 124.1 %exchange_and_scatter.1 = (bf16[4,256,2048]{2,1,0:T(8,128)(2,1)}, bf16[4,192,1024]{2,1,0:T(8,128)(2,1)}, bf16[256,4096]{1,0:T(8,128)(2,1)}) custom-call(bf16[4,256,2048]{2,1,0:T(8,128)(2,1)} %bitcast.253, bf16[4,192,2048]{2,1,0:T(8,128)(2,1)} %bitcast.240, bf16[1024,1024]{1,0:T(8,128)(2,1)} %get-tuple-element.169.refs_2_, ...), custom_call_target="tpu_custom_call" | custom-call | tf_op jit(solution)/shard_map/exchange_and_scatter/pallas_call | solution.py:957
  984.2 92.5 %scatter.1 = bf16[256,4096]{1,0:T(8,128)(2,1)} custom-call(bf16[768,1024]{1,0:T(8,128)(2,1)} %get-tuple-element.189.refs_0_, bf16[768,1024]{1,0:T(8,128)(2,1)} %get-tuple-element.188.refs_1_, bf16[768,1024]{1,0:T(8,128)(2,1)} %get-tuple-element.179.refs_2_, bf16[768,1024]{1,0:T(8,128)(2,1)} %get-tuple-element.178.refs_3_, ...), custom_call_target="tpu_custom_call" | custom-call | tf_op jit(solution)/shard_map/scatter/pallas_call | solution.py:957
  1091.0 7.0 transpose.38
  1099.1 9.4 assemble.1
  1110.6 7.5 collective-permute-start.10
  (239 shorter events, 127.6 us)
Async XLA Ops:
  7.2 128.1 %all-gather.7.cloned.1.call-start = ((), (), s32[]{:S(2)}) async-start(), calls=%async_computation.4 | async-start | bytes 18874368 | tf_op jit(solution)/shard_map/all_gather | solution.py:1150
  11.1 179.3 %all-gather.15.cloned.1.call-start = ((), (), s32[]{:S(2)}) async-start(), calls=%async_computation.12 | async-start | bytes 9437184 | tf_op jit(solution)/shard_map/all_gather | solution.py:1150
  13.1 356.7 %all-gather.9.cloned.1.call-start = ((), (), s32[]{:S(2)}) async-start(), calls=%async_computation.5 | async-start | bytes 25952256 | tf_op jit(solution)/shard_map/all_gather | solution.py:1150
  13.2 3.2 collective-permute-start
  16.4 4.1 collective-permute-start.1
  20.6 3.7 collective-permute-start.2
  22.7 76.4 %copy-start.43 = (f32[256]{0:T(256)}, f32[256]{0:T(256)S(1)}, u32[]{:S(2)}) copy-start(f32[256]{0:T(256)S(1)} %add_rsqrt_fusion.1) | copy-start | bytes 3076
  24.3 74.7 %copy-start.33 = (f32[1,2048]{1,0:T(1,128)}, f32[1,2048]{1,0:T(1,128)S(1)}, u32[]{:S(2)}) copy-start(f32[1,2048]{1,0:T(1,128)S(1)} %get-tuple-element.211) | copy-start | bytes 24580
  24.3 254.7 %copy-start.31 = (f32[1,2048]{1,0:T(1,128)}, f32[1,2048]{1,0:T(1,128)S(1)}, u32[]{:S(2)}) copy-start(f32[1,2048]{1,0:T(1,128)S(1)} %get-tuple-element.210) | copy-start | bytes 24580
  99.2 362.3 %all-gather.11.cloned.1.call-start = ((), (), s32[]{:S(2)}) async-start(), calls=%async_computation.6 | async-start | bytes 18874368 | tf_op jit(solution)/shard_map/all_gather | solution.py:1150
  99.7 458.4 %all-gather.13.cloned.1.call-start = ((), (), s32[]{:S(2)}) async-start(), calls=%async_computation.7 | async-start | bytes 14155776 | tf_op jit(solution)/shard_map/all_gather | solution.py:1150
  103.4 10.3 copy-start.29
  109.9 80.4 %all-to-all-start = ((bf16[4,192,2048]{2,1,0:T(8,128)(2,1)}), bf16[4,192,2048]{2,1,0:T(8,128)(2,1)S(1)}, u32[]{:S(2)}, u32[]{:S(2)}) async-start(bf16[4,192,2048]{2,1,0:T(8,128)(2,1)} %bitcast.243), calls=%async_computation | async-start | bytes 6291456 | tf_op jit(solution)/shard_map/all_to_all | solution.py:1099
  113.7 746.4 %reduce-scatter.4.cloned.1.call-start = ((), (), s32[]{:S(2)}) async-start(), calls=%async_computation.8 | async-start | bytes 18874368 | tf_op jit(solution)/shard_map/reduce_scatter | solution.py:1253
  190.3 13.4 %copy-start.1 = (bf16[4,192,2048]{2,1,0:T(8,128)(2,1)}, bf16[4,192,2048]{2,1,0:T(8,128)(2,1)S(1)}, u32[]{:S(2)}) copy-start(bf16[4,192,2048]{2,1,0:T(8,128)(2,1)S(1)} %all-to-all-done) | copy-start | bytes 9437188
  203.7 71.0 %copy-start.8 = (bf16[256,2048]{1,0:T(8,128)(2,1)S(1)}, bf16[256,2048]{1,0:T(8,128)(2,1)}, u32[]{:S(2)}) copy-start(bf16[256,2048]{1,0:T(8,128)(2,1)} %param.13) | copy-start | bytes 3145732
  279.0 83.9 %copy-start.39 = (f32[256]{0:T(256)}, f32[256]{0:T(256)S(1)}, u32[]{:S(2)}) copy-start(f32[256]{0:T(256)S(1)} %add_rsqrt_fusion) | copy-start | bytes 3076
  283.1 79.8 %copy-start.19 = (bf16[768,2048]{1,0:T(8,128)(2,1)S(1)}, bf16[768,2048]{1,0:T(8,128)(2,1)}, u32[]{:S(2)}) copy-start(bf16[768,2048]{1,0:T(8,128)(2,1)} %get-tuple-element.88) | copy-start | bytes 9437188
  414.5 13.3 %copy-start.20 = (bf16[768,2048]{1,0:T(8,128)(2,1)S(1)}, bf16[768,2048]{1,0:T(8,128)(2,1)}, u32[]{:S(2)}) copy-start(bf16[768,2048]{1,0:T(8,128)(2,1)} %get-tuple-element.101.grad_ref) | copy-start | bytes 9437188
  508.0 352.1 %reduce-scatter.6.cloned.1.call-start = ((), (), s32[]{:S(2)}) async-start(), calls=%async_computation.9 | async-start | bytes 25952256 | tf_op jit(solution)/shard_map/reduce_scatter | solution.py:1264
  508.0 8.3 collective-permute-start.3
  508.4 14.3 %collective-permute-start.4 = (bf16[1024,2048]{1,0:T(8,128)(2,1)}, bf16[1024,2048]{1,0:T(8,128)(2,1)}, u32[]{:S(2)}, u32[]{:S(2)}) collective-permute-start(bf16[1024,2048]{1,0:T(8,128)(2,1)} %convolution_convert_fusion.1), channel_id=1, source_target_pairs={{0,4},{4,0},{8,12},{12,8},{16,20},{20,16},{24,28},{28,24},{1,5},{5... | collective-permute-start | bytes 12582920 | tf_op jit(solution)/shard_map/ppermute | solution.py:1008
  528.0 71.0 %collective-permute-start.5 = (bf16[2,256,2048]{2,1,0:T(8,128)(2,1)}, bf16[2,256,2048]{2,1,0:T(8,128)(2,1)}, u32[]{:S(2)}, u32[]{:S(2)}) collective-permute-start(bf16[2,256,2048]{2,1,0:T(8,128)(2,1)} %get-tuple-element.163), channel_id=1, source_target_pairs={{0,8},{4,12},{8,0},{12,4},{16,24},{20,28},{24,16},{28,20},{1,9},{5... | collective-permute-start | bytes 6291464 | tf_op jit(solution)/shard_map/ppermute | solution.py:1008
  536.0 62.9 %collective-permute-start.6 = (bf16[2,256,2048]{2,1,0:T(8,128)(2,1)}, bf16[2,256,2048]{2,1,0:T(8,128)(2,1)}, u32[]{:S(2)}, u32[]{:S(2)}) collective-permute-start(bf16[2,256,2048]{2,1,0:T(8,128)(2,1)} %get-tuple-element.161), channel_id=1, source_target_pairs={{0,16},{4,20},{8,24},{12,28},{16,0},{20,4},{24,8},{28,12},{1,17},{... | collective-permute-start | bytes 6291464 | tf_op jit(solution)/shard_map/ppermute | solution.py:1008
  662.8 321.4 %reduce-scatter.8.cloned.1.call-start = ((), (), s32[]{:S(2)}) async-start(), calls=%async_computation.11 | async-start | bytes 14155776 | tf_op jit(solution)/shard_map/reduce_scatter | solution.py:1265
  663.6 417.3 %all-reduce.2.cloned.1.call-start = ((), (), s32[]{:S(2)}) async-start(), calls=%async_computation.10 | async-start | bytes 4194304 | tf_op jit(solution)/shard_map/psum | solution.py:1299
  823.4 10.2 copy-start.30
  1086.2 11.7 %collective-permute-start.7 = (f32[2,2,2,256]{3,0,2,1:T(2,128)S(1)}, f32[2,2,2,256]{3,0,2,1:T(2,128)S(1)}, u32[]{:S(2)}, u32[]{:S(2)}) collective-permute-start(f32[2,2,2,256]{3,0,2,1:T(2,128)S(1)} %fusion.72), channel_id=1, source_target_pairs={{0,16},{4,20},{8,24},{12,28},{16,0},{20,4},{24,8},{28,12},{1,17},{... | collective-permute-start | bytes 24584 | tf_op jit(solution)/shard_map/ppermute | solution.py:1334
  1098.0 10.5 collective-permute-start.8
  1108.6 2.0 collective-permute-start.9
  1110.6 9.0 collective-permute-start.10
  1119.6 4.5 collective-permute-start.11
  (43 other events, 184.9 us)
Sparse Core Ops, SparseCore 0:
  11.2 121.9 all-gather.6
  135.7 54.3 all-gather.14
  192.0 177.7 all-gather.8
  371.6 89.8 all-gather.10
  463.2 73.4 all-gather.12
  540.1 140.0 reduce-scatter.3
  683.8 145.8 reduce-scatter.5
  833.2 129.4 reduce-scatter.7
  984.4 92.8 all-reduce.1
